TPU v7x, 32 devices: a whole 2x2x4 slice. The times are simulated.
32 devices in a mesh: section: 4 (over y, x), dp: 8 (over z, core).
Axes of the slice: x: 2, y: 2, z: 4, core: 2. Of those that a mesh axis runs over, the one named last changes fastest.
Arguments:
- voxel_feats: bfloat16 [8, 16384, 64], P(None, 'dp'), may hold values from -6 to 6
- down_map: int32 [8, 8, 4096], P(None, None, 'dp'), may hold values from 0 to 2048, as said below
- neighbours: int32 [8, 27, 4096], P(None, None, 'dp'), may hold values from 0 to 512, as said below
- w_down: bfloat16 [8, 64, 128], replicated, may hold values from -0.25 to 0.25
- w_first: bfloat16 [27, 128, 128], replicated, may hold values from -0.109375 to 0.109375
- w_second: bfloat16 [27, 128, 128], replicated, may hold values from -0.109375 to 0.109375
- bn_scale: float32 [3, 128], replicated, may hold values from 0.25 to 1.75
- bn_shift: float32 [3, 128], replicated, may hold values from -3 to 3
- out_grad: bfloat16 [8, 4096, 128], P(None, 'dp'), may hold values from -6 to 6
Outputs:
- features: bfloat16 [8, 4096, 128], P('section', 'dp')
- input_grad: bfloat16 [8, 16384, 64], P('section', 'dp')
- grad_down: float32 [8, 64, 128], replicated
- grad_first: float32 [27, 128, 128], replicated
- grad_second: float32 [27, 128, 128], replicated
- grad_scale: float32 [3, 128], replicated
- grad_shift: float32 [3, 128], replicated
Inputs may be any that keep to these rules, and one draw needn't show every extreme that they name: Offset k stands for the step (k // 9 - 1, (k // 3) % 3 - 1, k % 3 - 1) on the coarse grid. Entries index rows of the same bucket. The live rows of a bucket are its first ones; a live row r has neighbours[m, 13, r] = r, and every entry of a row that is not live is 512. The map is symmetric: where neighbours[m, k, p] = q, neighbours[m, 26 - k, q] = p. A bucket has 32 live rows or more, and in each micro-batch one bucket has all 512 live. `down_map`: entries index fine rows of the same bucket; 2048 marks an absent child. Each fine row is named at most once in a micro-batch. A live coarse row has 1 to 7 children and a row that is not live has none; the children of a bucket's live rows are its first 4 times as many fine rows, grouped by coarse row in order. In each micro-batch one bucket uses all 2048 fine rows.
All inputs are finite; a program needn't handle non-finite values.
Results may differ from a plain program's by a relative error of at most 0.012.
Values may be sent and summed in bfloat16 or wider, within the bound.
No kernel may reach another device: no remote copies, remote signals or barrier semaphores. Data moves between devices by JAX's collectives and lax.ppermute only.
A program may use at most 64 MiB of HBM per device.

v0:
```python
import jax
import jax.numpy as jnp
from jax import lax
from jax.sharding import PartitionSpec as P

EPSILON = 1e-05


def from_behind(value, axis, steps):
    count = lax.axis_size(axis)
    first, last = (max(0, -steps), min(count, count - steps))
    return lax.ppermute(value, axis, [(source, source + steps) for source in range(first, last)])


def shortened(value):

    def short(part):
        return part.astype(jnp.bfloat16) if part.dtype == jnp.float32 else part

    return jax.tree.map(short, value)


def with_zero(source):
    return jnp.concatenate([source, jnp.zeros((1, source.shape[1]), source.dtype)], axis=0)


def offset_conv(inputs, offset_map, weight):
    gathered = with_zero(inputs)[offset_map]
    return lax.dot_general(
        gathered, weight, (((0, 2), (0, 1)), ((), ())), preferred_element_type=jnp.float32
    )


def offset_grad(inputs, offset_map, grad_rows):
    gathered = with_zero(inputs)[offset_map]
    return lax.dot_general(
        gathered, grad_rows, (((1,), (0,)), ((), ())), preferred_element_type=jnp.float32
    )


def offset_back(grad_rows, offset_map, weight):
    flipped = with_zero(grad_rows)[offset_map[::-1]]
    return lax.dot_general(
        flipped, weight, (((0, 2), (0, 2)), ((), ())), preferred_element_type=jnp.float32
    )


def down_back(grad_rows, offset_map, weight, fine_rows):
    pieces = lax.dot_general(
        grad_rows, weight, (((1,), (2,)), ((), ())), preferred_element_type=jnp.float32
    )
    places = offset_map.T.reshape(-1)
    blank = jnp.zeros((fine_rows, weight.shape[1]), jnp.float32)
    return blank.at[places].set(pieces.reshape(-1, weight.shape[1]), mode="drop")


def norm_stats(hidden, live_rows):
    return lax.psum(
        (
            jnp.sum(live_rows * hidden, axis=0),
            jnp.sum(live_rows * hidden * hidden, axis=0),
            jnp.sum(live_rows),
        ),
        "dp",
    )


def normalize(hidden, totals):
    mean_row = totals[0] / totals[2]
    inv_std = lax.rsqrt(totals[1] / totals[2] - mean_row * mean_row + EPSILON)
    return ((hidden - mean_row) * inv_std, mean_row, inv_std)


def silu_slope(values):
    sigmoid = jax.nn.sigmoid(values)
    return sigmoid * (1.0 + values * (1.0 - sigmoid))


def norm_back(upstream, centred, live_rows, inv_std, gain_row, count):
    sums = lax.psum((jnp.sum(upstream, axis=0), jnp.sum(upstream * centred, axis=0)), "dp")
    return (
        live_rows * (inv_std * gain_row) * (upstream - sums[0] / count - centred * sums[1] / count)
    )


def total_grads(down_sum, first_sum, second_sum, gain_grid, shift_grid):
    return lax.psum((down_sum, first_sum, second_sum, gain_grid, shift_grid), ("section", "dp"))


def store_at(buffer, where_at, update, keep_it):
    return lax.dynamic_update_index_in_dim(
        buffer, jnp.where(keep_it, update, buffer[where_at]), where_at, 0
    )


def local(
    voxel_feats, down_map, neighbours, w_down, w_first, w_second, bn_scale, bn_shift, out_grad
):
    sections = lax.axis_size("section")
    section_at = lax.axis_index("section")
    micro_count = voxel_feats.shape[0]
    fine_rows = voxel_feats.shape[1]
    coarse_rows = neighbours.shape[2]
    channels = w_first.shape[2]
    live_all = (neighbours[:, 13, :] < coarse_rows).astype(jnp.float32)[:, :, None]
    norm_row = jnp.where(section_at == 3, 2, jnp.minimum(section_at, 1))
    gain_row = bn_scale[norm_row]
    shift_row = bn_shift[norm_row]
    ticks = micro_count + sections - 1
    blank_rows = jnp.zeros((coarse_rows, channels), jnp.bfloat16)
    blank_fine = jnp.zeros((fine_rows, w_down.shape[1]), jnp.bfloat16)
    kept_shape = (micro_count, coarse_rows, channels)

    def front_down(incoming, micro_at):
        return offset_conv(voxel_feats[micro_at], down_map[micro_at], w_down)

    def front_first(incoming, micro_at):
        return offset_conv(incoming, neighbours[micro_at], w_first)

    def front_second(incoming, micro_at):
        return offset_conv(incoming, neighbours[micro_at], w_second)

    def front_last(incoming, micro_at):
        return incoming.astype(jnp.float32)

    def front_none(incoming, micro_at):
        return jnp.zeros((coarse_rows, channels), jnp.float32)

    def forward_tick(moment, state):
        arriving, inputs_kept, skip_kept, means_kept, stds_kept, counts_kept, shown_kept = state
        position = moment - section_at
        in_range = (position >= 0) & (position < micro_count)
        micro_at = jnp.clip(position, 0, micro_count - 1)
        hidden = lax.switch(
            section_at, [front_down, front_first, front_second, front_last], arriving, micro_at
        )
        live_rows = live_all[micro_at]
        totals = norm_stats(hidden, live_rows)
        centred, mean_row, inv_std = normalize(hidden, totals)
        normed = (
            centred * gain_row
            + shift_row
            + jnp.where(section_at == 3, skip_kept[micro_at].astype(jnp.float32), 0.0)
        )
        outgoing = jnp.where(section_at == 2, hidden, live_rows * jax.nn.silu(normed)).astype(
            jnp.bfloat16
        )
        passed = from_behind(outgoing, "section", 1)
        skipped = from_behind(outgoing, "section", 3)
        due = jnp.clip(moment, 0, micro_count - 1)
        shown_next = store_at(shown_kept, micro_at, outgoing, in_range)
        return (
            passed,
            store_at(inputs_kept, micro_at, arriving, in_range),
            store_at(skip_kept, due, skipped, moment < micro_count),
            store_at(means_kept, micro_at, mean_row, in_range),
            store_at(stds_kept, micro_at, inv_std, in_range),
            store_at(counts_kept, micro_at, totals[2], in_range),
            shown_next,
        )

    start_state = (
        blank_rows,
        jnp.zeros(kept_shape, jnp.bfloat16),
        jnp.zeros(kept_shape, jnp.bfloat16),
        jnp.zeros((micro_count, channels), jnp.float32),
        jnp.zeros((micro_count, channels), jnp.float32),
        jnp.zeros((micro_count,), jnp.float32),
        jnp.zeros((micro_count, coarse_rows, channels), jnp.bfloat16),
    )
    ended = lax.fori_loop(0, ticks, forward_tick, start_state)
    inputs_kept, skip_kept, means_kept, stds_kept, counts_kept, shown_kept = (
        ended[1],
        ended[2],
        ended[3],
        ended[4],
        ended[5],
        ended[6],
    )

    def back_down(grad_rows, micro_at):
        return (
            jnp.zeros(w_first.shape, jnp.float32),
            offset_grad(voxel_feats[micro_at], down_map[micro_at], grad_rows),
            blank_rows,
            down_back(grad_rows, down_map[micro_at], w_down, fine_rows).astype(jnp.bfloat16),
        )

    def back_first(grad_rows, micro_at):
        return (
            offset_grad(inputs_kept[micro_at], neighbours[micro_at], grad_rows),
            jnp.zeros(w_down.shape, jnp.float32),
            offset_back(grad_rows, neighbours[micro_at], w_first).astype(jnp.bfloat16),
            blank_fine,
        )

    def back_second(grad_rows, micro_at):
        return (
            offset_grad(inputs_kept[micro_at], neighbours[micro_at], grad_rows),
            jnp.zeros(w_down.shape, jnp.float32),
            offset_back(grad_rows, neighbours[micro_at], w_second).astype(jnp.bfloat16),
            blank_fine,
        )

    def back_last(grad_rows, micro_at):
        return (
            jnp.zeros(w_first.shape, jnp.float32),
            jnp.zeros(w_down.shape, jnp.float32),
            grad_rows,
            blank_fine,
        )

    def backward_tick(moment, state):
        arriving, skip_grads, conv_sum, down_sum, gain_sum, shift_sum, fine_kept = state
        position = moment - (sections - 1 - section_at)
        in_range = (position >= 0) & (position < micro_count)
        micro_at = jnp.clip(position, 0, micro_count - 1)
        weight_now = in_range.astype(jnp.float32)
        hidden = lax.switch(
            section_at,
            [front_down, front_first, front_none, front_last],
            inputs_kept[micro_at],
            micro_at,
        )
        live_rows = live_all[micro_at]
        centred = (hidden - means_kept[micro_at]) * stds_kept[micro_at]
        normed = (
            centred * gain_row
            + shift_row
            + jnp.where(section_at == 3, skip_kept[micro_at].astype(jnp.float32), 0.0)
        )
        incoming = jnp.where(section_at == 3, out_grad[micro_at], arriving).astype(jnp.float32)
        incoming = incoming + jnp.where(
            section_at == 0, skip_grads[micro_at].astype(jnp.float32), 0.0
        )
        upstream = incoming * live_rows * silu_slope(normed)
        returned = from_behind(upstream.astype(jnp.bfloat16), "section", -3)
        due = jnp.clip(moment, 0, micro_count - 1)
        rows_back = norm_back(
            upstream, centred, live_rows, stds_kept[micro_at], gain_row, counts_kept[micro_at]
        )
        grad_rows = jnp.where(section_at == 2, arriving, rows_back.astype(jnp.bfloat16))
        counted = weight_now * (section_at != 2).astype(jnp.float32)
        gain_sum = gain_sum + counted * jnp.sum(upstream * centred, axis=0)
        shift_sum = shift_sum + counted * jnp.sum(upstream, axis=0)
        conv_grad, down_grad, sent, fine_grad = lax.switch(
            section_at, [back_down, back_first, back_second, back_last], grad_rows, micro_at
        )
        sent_back = jax.tree.map(
            lambda part, own: part.astype(own.dtype),
            from_behind(shortened(sent), "section", -1),
            sent,
        )
        fine_next = store_at(fine_kept, micro_at, fine_grad, in_range)
        return (
            sent_back,
            store_at(skip_grads, due, returned, moment < micro_count),
            conv_sum + weight_now * conv_grad,
            down_sum + weight_now * down_grad,
            gain_sum,
            shift_sum,
            fine_next,
        )

    back_state = (
        blank_rows,
        jnp.zeros(kept_shape, jnp.bfloat16),
        jnp.zeros(w_first.shape, jnp.float32),
        jnp.zeros(w_down.shape, jnp.float32),
        jnp.zeros((channels,), jnp.float32),
        jnp.zeros((channels,), jnp.float32),
        jnp.zeros((micro_count, fine_rows, w_down.shape[1]), jnp.bfloat16),
    )
    finished_state = lax.fori_loop(0, ticks, backward_tick, back_state)
    conv_sum, down_sum, gain_sum, shift_sum, fine_kept = (
        finished_state[2],
        finished_state[3],
        finished_state[4],
        finished_state[5],
        finished_state[6],
    )
    first_flag = (section_at == 1).astype(jnp.float32)
    second_flag = (section_at == 2).astype(jnp.float32)
    row_pick = ((jnp.arange(3) == norm_row) & (section_at != 2))[:, None]
    gain_grid = jnp.where(row_pick, gain_sum[None, :], 0.0)
    shift_grid = jnp.where(row_pick, shift_sum[None, :], 0.0)
    grad_down, grad_first, grad_second, grad_scale, grad_shift = total_grads(
        down_sum, conv_sum * first_flag, conv_sum * second_flag, gain_grid, shift_grid
    )
    shown = jnp.where(section_at == 3, shown_kept, jnp.zeros_like(shown_kept))
    delivered = (
        lax.psum_scatter(shown, "section", scatter_dimension=0, tiled=True).astype(jnp.float32),
        lax.psum_scatter(fine_kept, "section", scatter_dimension=0, tiled=True).astype(jnp.float32),
    )
    features = delivered[0].astype(jnp.bfloat16)
    input_grad = delivered[1].astype(jnp.bfloat16)
    return (features, input_grad, grad_down, grad_first, grad_second, grad_scale, grad_shift)


def solution(mesh):
    in_specs = (
        P(None, "dp", None),
        P(None, None, "dp"),
        P(None, None, "dp"),
        P(),
        P(),
        P(),
        P(),
        P(),
        P(None, "dp", None),
    )
    out_specs = (P("section", "dp", None), P("section", "dp", None), P(), P(), P(), P(), P())
    return jax.shard_map(local, mesh=mesh, in_specs=in_specs, out_specs=out_specs, check_vma=False)
```

profile of v0, /device:TPU:1, one launch (start us, length us, event | category | flops | bytes accessed | tf_op | source)
XLA Modules:
  0.0 2254.8 jit_solution(12731946655601193952)
XLA Ops:
  18.1 646.0 %while.57 = (s32[]{:T(128)}, bf16[512,128]{1,0:T(8,128)(2,1)S(1)}, bf16[8,512,128]{2,1,0:T(8,128)(2,1)}, bf16[8,512,128]{2,1,0:T(8,128)(2,1)}, f32[8,128]{1,0:T(...) while((s32[]{:T(128)}, bf16[512,128]{1,0:T(8,128)(2,1)S(1)}, ...), condition=%wide.region_11.12_spmd, body=%wide.region_0.11_spmd.sunk | while | flops 454418304 | bytes 16106359 | solution.py:171
  50.4 21.3 collective-permute-start
  111.9 20.6 collective-permute-start
  170.4 20.6 collective-permute-start
  228.8 20.6 collective-permute-start
  287.2 20.6 collective-permute-start
  345.6 20.5 collective-permute-start
  404.0 20.6 collective-permute-start
  462.4 20.6 collective-permute-start
  520.8 20.6 collective-permute-start
  579.2 20.6 collective-permute-start
  637.6 20.6 collective-permute-start
  666.9 1428.5 %while.58 = (s32[]{:T(128)}, bf16[512,128]{1,0:T(8,128)(2,1)S(1)}, bf16[8,512,128]{2,1,0:T(8,128)(2,1)}, f32[27,128,128]{2,1,0:T(8,128)}, f32[8,64,128]{2,1,0:T(...) while((s32[]{:T(128)}, bf16[512,128]{1,0:T(8,128)(2,1)S(1)}, ...), condition=%wide.region_27.28_spmd.clone, body=%wide.region_13.0_spmd.clone.sunk | while | flops 1363333632 | bytes 55689484 | solution.py:274
  700.8 30.0 %conditional.10 = (f32[27,128,128]{2,1,0:T(8,128)S(1)}, f32[8,64,128]{2,1,0:T(8,128)}, bf16[512,128]{1,0:T(8,128)(2,1)}, bf16[2048,64]{1,0:T(8,128)(2,1)}) conditional(s32[]{:T(128)} %get-tuple-element.2146, (s32[]{:T(128)}, bf16[8,2048,64]{2,1,0:T(8,128)(2,1)}, s32[8,8,512]{2,1,0:T(8,128)}, ...), branch_computations={%region_22.23_spmd, %region_24.24_spmd, %region_25.25_spmd, %regio... | conditional | flops 906146816 | bytes 26460760 | solution.py:246
  738.5 24.4 %collective-permute-done.3 = bf16[512,128]{1,0:T(8,128)(2,1)S(1)} collective-permute-done((bf16[512,128]{1,0:T(8,128)(2,1)}, bf16[512,128]{1,0:T(8,128)(2,1)S(1)}, u32[]{:S(2)}, u32[]{:S(2)}) %collective-permute-start.3) | collective-permute-done | bytes 131104 | tf_op jit(solution)/shard_map/while/body/eval_jaxpr/ppermute | solution.py:12
  763.6 29.6 %collective-permute-done.2 = bf16[512,128]{1,0:T(8,128)(2,1)S(1)} collective-permute-done((bf16[512,128]{1,0:T(8,128)(2,1)}, bf16[512,128]{1,0:T(8,128)(2,1)S(1)}, u32[]{:S(2)}, u32[]{:S(2)}) %collective-permute-start.2) | collective-permute-done | bytes 131104 | tf_op jit(solution)/shard_map/while/body/eval_jaxpr/ppermute | solution.py:12
  826.9 30.0 %conditional.10 = (f32[27,128,128]{2,1,0:T(8,128)S(1)}, f32[8,64,128]{2,1,0:T(8,128)}, bf16[512,128]{1,0:T(8,128)(2,1)}, bf16[2048,64]{1,0:T(8,128)(2,1)}) conditional(s32[]{:T(128)} %get-tuple-element.2146, (s32[]{:T(128)}, bf16[8,2048,64]{2,1,0:T(8,128)(2,1)}, s32[8,8,512]{2,1,0:T(8,128)}, ...), branch_computations={%region_22.23_spmd, %region_24.24_spmd, %region_25.25_spmd, %regio... | conditional | flops 906146816 | bytes 26460760 | solution.py:246
  866.1 27.7 %collective-permute-done.3 = bf16[512,128]{1,0:T(8,128)(2,1)S(1)} collective-permute-done((bf16[512,128]{1,0:T(8,128)(2,1)}, bf16[512,128]{1,0:T(8,128)(2,1)S(1)}, u32[]{:S(2)}, u32[]{:S(2)}) %collective-permute-start.3) | collective-permute-done | bytes 131104 | tf_op jit(solution)/shard_map/while/body/eval_jaxpr/ppermute | solution.py:12
  894.5 26.8 %collective-permute-done.2 = bf16[512,128]{1,0:T(8,128)(2,1)S(1)} collective-permute-done((bf16[512,128]{1,0:T(8,128)(2,1)}, bf16[512,128]{1,0:T(8,128)(2,1)S(1)}, u32[]{:S(2)}, u32[]{:S(2)}) %collective-permute-start.2) | collective-permute-done | bytes 131104 | tf_op jit(solution)/shard_map/while/body/eval_jaxpr/ppermute | solution.py:12
  955.0 30.0 %conditional.10 = (f32[27,128,128]{2,1,0:T(8,128)S(1)}, f32[8,64,128]{2,1,0:T(8,128)}, bf16[512,128]{1,0:T(8,128)(2,1)}, bf16[2048,64]{1,0:T(8,128)(2,1)}) conditional(s32[]{:T(128)} %get-tuple-element.2146, (s32[]{:T(128)}, bf16[8,2048,64]{2,1,0:T(8,128)(2,1)}, s32[8,8,512]{2,1,0:T(8,128)}, ...), branch_computations={%region_22.23_spmd, %region_24.24_spmd, %region_25.25_spmd, %regio... | conditional | flops 906146816 | bytes 26460760 | solution.py:246
  994.2 30.2 %collective-permute-done.3 = bf16[512,128]{1,0:T(8,128)(2,1)S(1)} collective-permute-done((bf16[512,128]{1,0:T(8,128)(2,1)}, bf16[512,128]{1,0:T(8,128)(2,1)S(1)}, u32[]{:S(2)}, u32[]{:S(2)}) %collective-permute-start.3) | collective-permute-done | bytes 131104 | tf_op jit(solution)/shard_map/while/body/eval_jaxpr/ppermute | solution.py:12
  1025.1 25.7 %collective-permute-done.2 = bf16[512,128]{1,0:T(8,128)(2,1)S(1)} collective-permute-done((bf16[512,128]{1,0:T(8,128)(2,1)}, bf16[512,128]{1,0:T(8,128)(2,1)S(1)}, u32[]{:S(2)}, u32[]{:S(2)}) %collective-permute-start.2) | collective-permute-done | bytes 131104 | tf_op jit(solution)/shard_map/while/body/eval_jaxpr/ppermute | solution.py:12
  1084.6 30.0 %conditional.10 = (f32[27,128,128]{2,1,0:T(8,128)S(1)}, f32[8,64,128]{2,1,0:T(8,128)}, bf16[512,128]{1,0:T(8,128)(2,1)}, bf16[2048,64]{1,0:T(8,128)(2,1)}) conditional(s32[]{:T(128)} %get-tuple-element.2146, (s32[]{:T(128)}, bf16[8,2048,64]{2,1,0:T(8,128)(2,1)}, s32[8,8,512]{2,1,0:T(8,128)}, ...), branch_computations={%region_22.23_spmd, %region_24.24_spmd, %region_25.25_spmd, %regio... | conditional | flops 906146816 | bytes 26460760 | solution.py:246
  1124.8 29.2 %collective-permute-done.3 = bf16[512,128]{1,0:T(8,128)(2,1)S(1)} collective-permute-done((bf16[512,128]{1,0:T(8,128)(2,1)}, bf16[512,128]{1,0:T(8,128)(2,1)S(1)}, u32[]{:S(2)}, u32[]{:S(2)}) %collective-permute-start.3) | collective-permute-done | bytes 131104 | tf_op jit(solution)/shard_map/while/body/eval_jaxpr/ppermute | solution.py:12
  1154.7 26.8 %collective-permute-done.2 = bf16[512,128]{1,0:T(8,128)(2,1)S(1)} collective-permute-done((bf16[512,128]{1,0:T(8,128)(2,1)}, bf16[512,128]{1,0:T(8,128)(2,1)S(1)}, u32[]{:S(2)}, u32[]{:S(2)}) %collective-permute-start.2) | collective-permute-done | bytes 131104 | tf_op jit(solution)/shard_map/while/body/eval_jaxpr/ppermute | solution.py:12
  1215.2 30.0 %conditional.10 = (f32[27,128,128]{2,1,0:T(8,128)S(1)}, f32[8,64,128]{2,1,0:T(8,128)}, bf16[512,128]{1,0:T(8,128)(2,1)}, bf16[2048,64]{1,0:T(8,128)(2,1)}) conditional(s32[]{:T(128)} %get-tuple-element.2146, (s32[]{:T(128)}, bf16[8,2048,64]{2,1,0:T(8,128)(2,1)}, s32[8,8,512]{2,1,0:T(8,128)}, ...), branch_computations={%region_22.23_spmd, %region_24.24_spmd, %region_25.25_spmd, %regio... | conditional | flops 906146816 | bytes 26460760 | solution.py:246
  1255.4 29.2 %collective-permute-done.3 = bf16[512,128]{1,0:T(8,128)(2,1)S(1)} collective-permute-done((bf16[512,128]{1,0:T(8,128)(2,1)}, bf16[512,128]{1,0:T(8,128)(2,1)S(1)}, u32[]{:S(2)}, u32[]{:S(2)}) %collective-permute-start.3) | collective-permute-done | bytes 131104 | tf_op jit(solution)/shard_map/while/body/eval_jaxpr/ppermute | solution.py:12
  1285.2 26.8 %collective-permute-done.2 = bf16[512,128]{1,0:T(8,128)(2,1)S(1)} collective-permute-done((bf16[512,128]{1,0:T(8,128)(2,1)}, bf16[512,128]{1,0:T(8,128)(2,1)S(1)}, u32[]{:S(2)}, u32[]{:S(2)}) %collective-permute-start.2) | collective-permute-done | bytes 131104 | tf_op jit(solution)/shard_map/while/body/eval_jaxpr/ppermute | solution.py:12
  1345.8 30.0 %conditional.10 = (f32[27,128,128]{2,1,0:T(8,128)S(1)}, f32[8,64,128]{2,1,0:T(8,128)}, bf16[512,128]{1,0:T(8,128)(2,1)}, bf16[2048,64]{1,0:T(8,128)(2,1)}) conditional(s32[]{:T(128)} %get-tuple-element.2146, (s32[]{:T(128)}, bf16[8,2048,64]{2,1,0:T(8,128)(2,1)}, s32[8,8,512]{2,1,0:T(8,128)}, ...), branch_computations={%region_22.23_spmd, %region_24.24_spmd, %region_25.25_spmd, %regio... | conditional | flops 906146816 | bytes 26460760 | solution.py:246
  1385.9 29.2 %collective-permute-done.3 = bf16[512,128]{1,0:T(8,128)(2,1)S(1)} collective-permute-done((bf16[512,128]{1,0:T(8,128)(2,1)}, bf16[512,128]{1,0:T(8,128)(2,1)S(1)}, u32[]{:S(2)}, u32[]{:S(2)}) %collective-permute-start.3) | collective-permute-done | bytes 131104 | tf_op jit(solution)/shard_map/while/body/eval_jaxpr/ppermute | solution.py:12
  1415.8 26.8 %collective-permute-done.2 = bf16[512,128]{1,0:T(8,128)(2,1)S(1)} collective-permute-done((bf16[512,128]{1,0:T(8,128)(2,1)}, bf16[512,128]{1,0:T(8,128)(2,1)S(1)}, u32[]{:S(2)}, u32[]{:S(2)}) %collective-permute-start.2) | collective-permute-done | bytes 131104 | tf_op jit(solution)/shard_map/while/body/eval_jaxpr/ppermute | solution.py:12
  1476.3 30.0 %conditional.10 = (f32[27,128,128]{2,1,0:T(8,128)S(1)}, f32[8,64,128]{2,1,0:T(8,128)}, bf16[512,128]{1,0:T(8,128)(2,1)}, bf16[2048,64]{1,0:T(8,128)(2,1)}) conditional(s32[]{:T(128)} %get-tuple-element.2146, (s32[]{:T(128)}, bf16[8,2048,64]{2,1,0:T(8,128)(2,1)}, s32[8,8,512]{2,1,0:T(8,128)}, ...), branch_computations={%region_22.23_spmd, %region_24.24_spmd, %region_25.25_spmd, %regio... | conditional | flops 906146816 | bytes 26460760 | solution.py:246
  1516.5 29.2 %collective-permute-done.3 = bf16[512,128]{1,0:T(8,128)(2,1)S(1)} collective-permute-done((bf16[512,128]{1,0:T(8,128)(2,1)}, bf16[512,128]{1,0:T(8,128)(2,1)S(1)}, u32[]{:S(2)}, u32[]{:S(2)}) %collective-permute-start.3) | collective-permute-done | bytes 131104 | tf_op jit(solution)/shard_map/while/body/eval_jaxpr/ppermute | solution.py:12
  1546.4 26.8 %collective-permute-done.2 = bf16[512,128]{1,0:T(8,128)(2,1)S(1)} collective-permute-done((bf16[512,128]{1,0:T(8,128)(2,1)}, bf16[512,128]{1,0:T(8,128)(2,1)S(1)}, u32[]{:S(2)}, u32[]{:S(2)}) %collective-permute-start.2) | collective-permute-done | bytes 131104 | tf_op jit(solution)/shard_map/while/body/eval_jaxpr/ppermute | solution.py:12
  1606.9 30.0 %conditional.10 = (f32[27,128,128]{2,1,0:T(8,128)S(1)}, f32[8,64,128]{2,1,0:T(8,128)}, bf16[512,128]{1,0:T(8,128)(2,1)}, bf16[2048,64]{1,0:T(8,128)(2,1)}) conditional(s32[]{:T(128)} %get-tuple-element.2146, (s32[]{:T(128)}, bf16[8,2048,64]{2,1,0:T(8,128)(2,1)}, s32[8,8,512]{2,1,0:T(8,128)}, ...), branch_computations={%region_22.23_spmd, %region_24.24_spmd, %region_25.25_spmd, %regio... | conditional | flops 906146816 | bytes 26460760 | solution.py:246
  1647.1 29.1 %collective-permute-done.3 = bf16[512,128]{1,0:T(8,128)(2,1)S(1)} collective-permute-done((bf16[512,128]{1,0:T(8,128)(2,1)}, bf16[512,128]{1,0:T(8,128)(2,1)S(1)}, u32[]{:S(2)}, u32[]{:S(2)}) %collective-permute-start.3) | collective-permute-done | bytes 131104 | tf_op jit(solution)/shard_map/while/body/eval_jaxpr/ppermute | solution.py:12
  1676.9 26.8 %collective-permute-done.2 = bf16[512,128]{1,0:T(8,128)(2,1)S(1)} collective-permute-done((bf16[512,128]{1,0:T(8,128)(2,1)}, bf16[512,128]{1,0:T(8,128)(2,1)S(1)}, u32[]{:S(2)}, u32[]{:S(2)}) %collective-permute-start.2) | collective-permute-done | bytes 131104 | tf_op jit(solution)/shard_map/while/body/eval_jaxpr/ppermute | solution.py:12
  1737.5 30.0 %conditional.10 = (f32[27,128,128]{2,1,0:T(8,128)S(1)}, f32[8,64,128]{2,1,0:T(8,128)}, bf16[512,128]{1,0:T(8,128)(2,1)}, bf16[2048,64]{1,0:T(8,128)(2,1)}) conditional(s32[]{:T(128)} %get-tuple-element.2146, (s32[]{:T(128)}, bf16[8,2048,64]{2,1,0:T(8,128)(2,1)}, s32[8,8,512]{2,1,0:T(8,128)}, ...), branch_computations={%region_22.23_spmd, %region_24.24_spmd, %region_25.25_spmd, %regio... | conditional | flops 906146816 | bytes 26460760 | solution.py:246
  1777.6 29.2 %collective-permute-done.3 = bf16[512,128]{1,0:T(8,128)(2,1)S(1)} collective-permute-done((bf16[512,128]{1,0:T(8,128)(2,1)}, bf16[512,128]{1,0:T(8,128)(2,1)S(1)}, u32[]{:S(2)}, u32[]{:S(2)}) %collective-permute-start.3) | collective-permute-done | bytes 131104 | tf_op jit(solution)/shard_map/while/body/eval_jaxpr/ppermute | solution.py:12
  1807.5 26.8 %collective-permute-done.2 = bf16[512,128]{1,0:T(8,128)(2,1)S(1)} collective-permute-done((bf16[512,128]{1,0:T(8,128)(2,1)}, bf16[512,128]{1,0:T(8,128)(2,1)S(1)}, u32[]{:S(2)}, u32[]{:S(2)}) %collective-permute-start.2) | collective-permute-done | bytes 131104 | tf_op jit(solution)/shard_map/while/body/eval_jaxpr/ppermute | solution.py:12
  1868.0 30.0 %conditional.10 = (f32[27,128,128]{2,1,0:T(8,128)S(1)}, f32[8,64,128]{2,1,0:T(8,128)}, bf16[512,128]{1,0:T(8,128)(2,1)}, bf16[2048,64]{1,0:T(8,128)(2,1)}) conditional(s32[]{:T(128)} %get-tuple-element.2146, (s32[]{:T(128)}, bf16[8,2048,64]{2,1,0:T(8,128)(2,1)}, s32[8,8,512]{2,1,0:T(8,128)}, ...), branch_computations={%region_22.23_spmd, %region_24.24_spmd, %region_25.25_spmd, %regio... | conditional | flops 906146816 | bytes 26460760 | solution.py:246
  1908.2 29.2 %collective-permute-done.3 = bf16[512,128]{1,0:T(8,128)(2,1)S(1)} collective-permute-done((bf16[512,128]{1,0:T(8,128)(2,1)}, bf16[512,128]{1,0:T(8,128)(2,1)S(1)}, u32[]{:S(2)}, u32[]{:S(2)}) %collective-permute-start.3) | collective-permute-done | bytes 131104 | tf_op jit(solution)/shard_map/while/body/eval_jaxpr/ppermute | solution.py:12
  1938.1 26.8 %collective-permute-done.2 = bf16[512,128]{1,0:T(8,128)(2,1)S(1)} collective-permute-done((bf16[512,128]{1,0:T(8,128)(2,1)}, bf16[512,128]{1,0:T(8,128)(2,1)S(1)}, u32[]{:S(2)}, u32[]{:S(2)}) %collective-permute-start.2) | collective-permute-done | bytes 131104 | tf_op jit(solution)/shard_map/while/body/eval_jaxpr/ppermute | solution.py:12
  1998.6 30.0 %conditional.10 = (f32[27,128,128]{2,1,0:T(8,128)S(1)}, f32[8,64,128]{2,1,0:T(8,128)}, bf16[512,128]{1,0:T(8,128)(2,1)}, bf16[2048,64]{1,0:T(8,128)(2,1)}) conditional(s32[]{:T(128)} %get-tuple-element.2146, (s32[]{:T(128)}, bf16[8,2048,64]{2,1,0:T(8,128)(2,1)}, s32[8,8,512]{2,1,0:T(8,128)}, ...), branch_computations={%region_22.23_spmd, %region_24.24_spmd, %region_25.25_spmd, %regio... | conditional | flops 906146816 | bytes 26460760 | solution.py:246
  2038.8 28.1 %collective-permute-done.3 = bf16[512,128]{1,0:T(8,128)(2,1)S(1)} collective-permute-done((bf16[512,128]{1,0:T(8,128)(2,1)}, bf16[512,128]{1,0:T(8,128)(2,1)S(1)}, u32[]{:S(2)}, u32[]{:S(2)}) %collective-permute-start.3) | collective-permute-done | bytes 131104 | tf_op jit(solution)/shard_map/while/body/eval_jaxpr/ppermute | solution.py:12
  2067.6 27.8 %collective-permute-done.2 = bf16[512,128]{1,0:T(8,128)(2,1)S(1)} collective-permute-done((bf16[512,128]{1,0:T(8,128)(2,1)}, bf16[512,128]{1,0:T(8,128)(2,1)S(1)}, u32[]{:S(2)}, u32[]{:S(2)}) %collective-permute-start.2) | collective-permute-done | bytes 131104 | tf_op jit(solution)/shard_map/while/body/eval_jaxpr/ppermute | solution.py:12
  2101.1 41.2 %all-reduce.12 = (f32[3,128]{1,0:T(4,128)}, f32[3,128]{1,0:T(4,128)}) all-reduce(f32[3,128]{1,0:T(4,128)S(1)} %get-tuple-element.1598, f32[3,128]{1,0:T(4,128)S(1)} %get-tuple-element.1597), channel_id=1, replica_groups=mesh['section'=4,'dp'=8] {'section','dp'}, use_global_device_ids=true, to_apply=%region_32.33 | all-reduce | flops 768 | bytes 6144 | tf_op jit(solution)/shard_map/psum | solution.py:87
  2142.4 99.1 %all-reduce.20.cloned.1.call-done = (f32[8,64,128]{2,1,0:T(8,128)}, f32[27,128,128]{2,1,0:T(8,128)}, f32[27,128,128]{2,1,0:T(8,128)}) async-done(((f32[8,64,128]{2,1,0:T(8,128)}, f32[27,128,128]{2,1,0:T(8,128)}, f32[27,128,128]{2,1,0:T(8,128)}), (f32[8,64,128]{2,1,0:T(8,128)}, f32[27,128,128]{2,1,0:T(8,128)}, f32[27,128,128]{2,1,0:T(8,128)})) %all-reduce.20.cloned.1.call-update) | async-done | bytes 3801104 | tf_op jit(solution)/shard_map/psum | solution.py:87
  (1169 shorter events, 1556.4 us)
Async XLA Ops:
  8.0 2233.5 %all-reduce.20.cloned.1.call-start = ((), (), s32[]{:S(2)}) async-start(), calls=%async_computation.4 | async-start | bytes 7602176 | tf_op jit(solution)/shard_map/psum | solution.py:87
  50.4 26.4 %collective-permute-start = (bf16[512,128]{1,0:T(8,128)(2,1)S(1)}, bf16[512,128]{1,0:T(8,128)(2,1)S(1)}, u32[]{:S(2)}, u32[]{:S(2)}) collective-permute-start(bf16[512,128]{1,0:T(8,128)(2,1)S(1)} %get-tuple-element.1915), channel_id=1, source_target_pairs={{0,8},{8,16},{16,24},{1,9},{9,17},{17,25},{2,10},{10,18},{18,26},{... | collective-permute-start | bytes 393224 | tf_op jit(solution)/shard_map/while/body/eval_jaxpr/ppermute | solution.py:12
  71.7 5.1 collective-permute-start.1
  111.9 25.7 %collective-permute-start = (bf16[512,128]{1,0:T(8,128)(2,1)S(1)}, bf16[512,128]{1,0:T(8,128)(2,1)S(1)}, u32[]{:S(2)}, u32[]{:S(2)}) collective-permute-start(bf16[512,128]{1,0:T(8,128)(2,1)S(1)} %get-tuple-element.1915), channel_id=1, source_target_pairs={{0,8},{8,16},{16,24},{1,9},{9,17},{17,25},{2,10},{10,18},{18,26},{... | collective-permute-start | bytes 393224 | tf_op jit(solution)/shard_map/while/body/eval_jaxpr/ppermute | solution.py:12
  132.6 5.1 collective-permute-start.1
  170.4 25.7 %collective-permute-start = (bf16[512,128]{1,0:T(8,128)(2,1)S(1)}, bf16[512,128]{1,0:T(8,128)(2,1)S(1)}, u32[]{:S(2)}, u32[]{:S(2)}) collective-permute-start(bf16[512,128]{1,0:T(8,128)(2,1)S(1)} %get-tuple-element.1915), channel_id=1, source_target_pairs={{0,8},{8,16},{16,24},{1,9},{9,17},{17,25},{2,10},{10,18},{18,26},{... | collective-permute-start | bytes 393224 | tf_op jit(solution)/shard_map/while/body/eval_jaxpr/ppermute | solution.py:12
  191.0 5.1 collective-permute-start.1
  228.8 25.7 %collective-permute-start = (bf16[512,128]{1,0:T(8,128)(2,1)S(1)}, bf16[512,128]{1,0:T(8,128)(2,1)S(1)}, u32[]{:S(2)}, u32[]{:S(2)}) collective-permute-start(bf16[512,128]{1,0:T(8,128)(2,1)S(1)} %get-tuple-element.1915), channel_id=1, source_target_pairs={{0,8},{8,16},{16,24},{1,9},{9,17},{17,25},{2,10},{10,18},{18,26},{... | collective-permute-start | bytes 393224 | tf_op jit(solution)/shard_map/while/body/eval_jaxpr/ppermute | solution.py:12
  249.4 5.1 collective-permute-start.1
  287.2 25.7 %collective-permute-start = (bf16[512,128]{1,0:T(8,128)(2,1)S(1)}, bf16[512,128]{1,0:T(8,128)(2,1)S(1)}, u32[]{:S(2)}, u32[]{:S(2)}) collective-permute-start(bf16[512,128]{1,0:T(8,128)(2,1)S(1)} %get-tuple-element.1915), channel_id=1, source_target_pairs={{0,8},{8,16},{16,24},{1,9},{9,17},{17,25},{2,10},{10,18},{18,26},{... | collective-permute-start | bytes 393224 | tf_op jit(solution)/shard_map/while/body/eval_jaxpr/ppermute | solution.py:12
  307.8 5.1 collective-permute-start.1
  345.6 25.6 %collective-permute-start = (bf16[512,128]{1,0:T(8,128)(2,1)S(1)}, bf16[512,128]{1,0:T(8,128)(2,1)S(1)}, u32[]{:S(2)}, u32[]{:S(2)}) collective-permute-start(bf16[512,128]{1,0:T(8,128)(2,1)S(1)} %get-tuple-element.1915), channel_id=1, source_target_pairs={{0,8},{8,16},{16,24},{1,9},{9,17},{17,25},{2,10},{10,18},{18,26},{... | collective-permute-start | bytes 393224 | tf_op jit(solution)/shard_map/while/body/eval_jaxpr/ppermute | solution.py:12
  366.2 5.1 collective-permute-start.1
  404.0 25.7 %collective-permute-start = (bf16[512,128]{1,0:T(8,128)(2,1)S(1)}, bf16[512,128]{1,0:T(8,128)(2,1)S(1)}, u32[]{:S(2)}, u32[]{:S(2)}) collective-permute-start(bf16[512,128]{1,0:T(8,128)(2,1)S(1)} %get-tuple-element.1915), channel_id=1, source_target_pairs={{0,8},{8,16},{16,24},{1,9},{9,17},{17,25},{2,10},{10,18},{18,26},{... | collective-permute-start | bytes 393224 | tf_op jit(solution)/shard_map/while/body/eval_jaxpr/ppermute | solution.py:12
  424.6 5.1 collective-permute-start.1
  462.4 25.7 %collective-permute-start = (bf16[512,128]{1,0:T(8,128)(2,1)S(1)}, bf16[512,128]{1,0:T(8,128)(2,1)S(1)}, u32[]{:S(2)}, u32[]{:S(2)}) collective-permute-start(bf16[512,128]{1,0:T(8,128)(2,1)S(1)} %get-tuple-element.1915), channel_id=1, source_target_pairs={{0,8},{8,16},{16,24},{1,9},{9,17},{17,25},{2,10},{10,18},{18,26},{... | collective-permute-start | bytes 393224 | tf_op jit(solution)/shard_map/while/body/eval_jaxpr/ppermute | solution.py:12
  483.0 5.1 collective-permute-start.1
  520.8 25.7 %collective-permute-start = (bf16[512,128]{1,0:T(8,128)(2,1)S(1)}, bf16[512,128]{1,0:T(8,128)(2,1)S(1)}, u32[]{:S(2)}, u32[]{:S(2)}) collective-permute-start(bf16[512,128]{1,0:T(8,128)(2,1)S(1)} %get-tuple-element.1915), channel_id=1, source_target_pairs={{0,8},{8,16},{16,24},{1,9},{9,17},{17,25},{2,10},{10,18},{18,26},{... | collective-permute-start | bytes 393224 | tf_op jit(solution)/shard_map/while/body/eval_jaxpr/ppermute | solution.py:12
  541.4 5.1 collective-permute-start.1
  579.2 25.7 %collective-permute-start = (bf16[512,128]{1,0:T(8,128)(2,1)S(1)}, bf16[512,128]{1,0:T(8,128)(2,1)S(1)}, u32[]{:S(2)}, u32[]{:S(2)}) collective-permute-start(bf16[512,128]{1,0:T(8,128)(2,1)S(1)} %get-tuple-element.1915), channel_id=1, source_target_pairs={{0,8},{8,16},{16,24},{1,9},{9,17},{17,25},{2,10},{10,18},{18,26},{... | collective-permute-start | bytes 393224 | tf_op jit(solution)/shard_map/while/body/eval_jaxpr/ppermute | solution.py:12
  599.8 5.1 collective-permute-start.1
  637.6 25.7 %collective-permute-start = (bf16[512,128]{1,0:T(8,128)(2,1)S(1)}, bf16[512,128]{1,0:T(8,128)(2,1)S(1)}, u32[]{:S(2)}, u32[]{:S(2)}) collective-permute-start(bf16[512,128]{1,0:T(8,128)(2,1)S(1)} %get-tuple-element.1915), channel_id=1, source_target_pairs={{0,8},{8,16},{16,24},{1,9},{9,17},{17,25},{2,10},{10,18},{18,26},{... | collective-permute-start | bytes 393224 | tf_op jit(solution)/shard_map/while/body/eval_jaxpr/ppermute | solution.py:12
  658.2 5.1 collective-permute-start.1
  730.8 62.4 %collective-permute-start.2 = (bf16[512,128]{1,0:T(8,128)(2,1)}, bf16[512,128]{1,0:T(8,128)(2,1)S(1)}, u32[]{:S(2)}, u32[]{:S(2)}) collective-permute-start(bf16[512,128]{1,0:T(8,128)(2,1)} %get-tuple-element.1956), channel_id=1, source_target_pairs={{8,0},{16,8},{24,16},{9,1},{17,9},{25,17},{10,2},{18,10},{26,18},{... | collective-permute-start | bytes 393224 | tf_op jit(solution)/shard_map/while/body/eval_jaxpr/ppermute | solution.py:12
  732.1 30.8 %collective-permute-start.3 = (bf16[512,128]{1,0:T(8,128)(2,1)}, bf16[512,128]{1,0:T(8,128)(2,1)S(1)}, u32[]{:S(2)}, u32[]{:S(2)}) collective-permute-start(bf16[512,128]{1,0:T(8,128)(2,1)} %get-tuple-element.1957), channel_id=1, source_target_pairs={{24,0},{25,1},{26,2},{27,3},{28,4},{29,5},{30,6},{31,7}} | collective-permute-start | bytes 393224 | tf_op jit(solution)/shard_map/while/body/eval_jaxpr/ppermute | solution.py:12
  856.9 64.4 %collective-permute-start.2 = (bf16[512,128]{1,0:T(8,128)(2,1)}, bf16[512,128]{1,0:T(8,128)(2,1)S(1)}, u32[]{:S(2)}, u32[]{:S(2)}) collective-permute-start(bf16[512,128]{1,0:T(8,128)(2,1)} %get-tuple-element.1956), channel_id=1, source_target_pairs={{8,0},{16,8},{24,16},{9,1},{17,9},{25,17},{10,2},{18,10},{26,18},{... | collective-permute-start | bytes 393224 | tf_op jit(solution)/shard_map/while/body/eval_jaxpr/ppermute | solution.py:12
  858.2 35.6 %collective-permute-start.3 = (bf16[512,128]{1,0:T(8,128)(2,1)}, bf16[512,128]{1,0:T(8,128)(2,1)S(1)}, u32[]{:S(2)}, u32[]{:S(2)}) collective-permute-start(bf16[512,128]{1,0:T(8,128)(2,1)} %get-tuple-element.1957), channel_id=1, source_target_pairs={{24,0},{25,1},{26,2},{27,3},{28,4},{29,5},{30,6},{31,7}} | collective-permute-start | bytes 393224 | tf_op jit(solution)/shard_map/while/body/eval_jaxpr/ppermute | solution.py:12
  985.0 65.8 %collective-permute-start.2 = (bf16[512,128]{1,0:T(8,128)(2,1)}, bf16[512,128]{1,0:T(8,128)(2,1)S(1)}, u32[]{:S(2)}, u32[]{:S(2)}) collective-permute-start(bf16[512,128]{1,0:T(8,128)(2,1)} %get-tuple-element.1956), channel_id=1, source_target_pairs={{8,0},{16,8},{24,16},{9,1},{17,9},{25,17},{10,2},{18,10},{26,18},{... | collective-permute-start | bytes 393224 | tf_op jit(solution)/shard_map/while/body/eval_jaxpr/ppermute | solution.py:12
  986.3 38.1 %collective-permute-start.3 = (bf16[512,128]{1,0:T(8,128)(2,1)}, bf16[512,128]{1,0:T(8,128)(2,1)S(1)}, u32[]{:S(2)}, u32[]{:S(2)}) collective-permute-start(bf16[512,128]{1,0:T(8,128)(2,1)} %get-tuple-element.1957), channel_id=1, source_target_pairs={{24,0},{25,1},{26,2},{27,3},{28,4},{29,5},{30,6},{31,7}} | collective-permute-start | bytes 393224 | tf_op jit(solution)/shard_map/while/body/eval_jaxpr/ppermute | solution.py:12
  1114.6 66.8 %collective-permute-start.2 = (bf16[512,128]{1,0:T(8,128)(2,1)}, bf16[512,128]{1,0:T(8,128)(2,1)S(1)}, u32[]{:S(2)}, u32[]{:S(2)}) collective-permute-start(bf16[512,128]{1,0:T(8,128)(2,1)} %get-tuple-element.1956), channel_id=1, source_target_pairs={{8,0},{16,8},{24,16},{9,1},{17,9},{25,17},{10,2},{18,10},{26,18},{... | collective-permute-start | bytes 393224 | tf_op jit(solution)/shard_map/while/body/eval_jaxpr/ppermute | solution.py:12
  1115.9 38.1 %collective-permute-start.3 = (bf16[512,128]{1,0:T(8,128)(2,1)}, bf16[512,128]{1,0:T(8,128)(2,1)S(1)}, u32[]{:S(2)}, u32[]{:S(2)}) collective-permute-start(bf16[512,128]{1,0:T(8,128)(2,1)} %get-tuple-element.1957), channel_id=1, source_target_pairs={{24,0},{25,1},{26,2},{27,3},{28,4},{29,5},{30,6},{31,7}} | collective-permute-start | bytes 393224 | tf_op jit(solution)/shard_map/while/body/eval_jaxpr/ppermute | solution.py:12
  1245.2 66.8 %collective-permute-start.2 = (bf16[512,128]{1,0:T(8,128)(2,1)}, bf16[512,128]{1,0:T(8,128)(2,1)S(1)}, u32[]{:S(2)}, u32[]{:S(2)}) collective-permute-start(bf16[512,128]{1,0:T(8,128)(2,1)} %get-tuple-element.1956), channel_id=1, source_target_pairs={{8,0},{16,8},{24,16},{9,1},{17,9},{25,17},{10,2},{18,10},{26,18},{... | collective-permute-start | bytes 393224 | tf_op jit(solution)/shard_map/while/body/eval_jaxpr/ppermute | solution.py:12
  1246.5 38.0 %collective-permute-start.3 = (bf16[512,128]{1,0:T(8,128)(2,1)}, bf16[512,128]{1,0:T(8,128)(2,1)S(1)}, u32[]{:S(2)}, u32[]{:S(2)}) collective-permute-start(bf16[512,128]{1,0:T(8,128)(2,1)} %get-tuple-element.1957), channel_id=1, source_target_pairs={{24,0},{25,1},{26,2},{27,3},{28,4},{29,5},{30,6},{31,7}} | collective-permute-start | bytes 393224 | tf_op jit(solution)/shard_map/while/body/eval_jaxpr/ppermute | solution.py:12
  1375.8 66.8 %collective-permute-start.2 = (bf16[512,128]{1,0:T(8,128)(2,1)}, bf16[512,128]{1,0:T(8,128)(2,1)S(1)}, u32[]{:S(2)}, u32[]{:S(2)}) collective-permute-start(bf16[512,128]{1,0:T(8,128)(2,1)} %get-tuple-element.1956), channel_id=1, source_target_pairs={{8,0},{16,8},{24,16},{9,1},{17,9},{25,17},{10,2},{18,10},{26,18},{... | collective-permute-start | bytes 393224 | tf_op jit(solution)/shard_map/while/body/eval_jaxpr/ppermute | solution.py:12
  1377.1 38.1 %collective-permute-start.3 = (bf16[512,128]{1,0:T(8,128)(2,1)}, bf16[512,128]{1,0:T(8,128)(2,1)S(1)}, u32[]{:S(2)}, u32[]{:S(2)}) collective-permute-start(bf16[512,128]{1,0:T(8,128)(2,1)} %get-tuple-element.1957), channel_id=1, source_target_pairs={{24,0},{25,1},{26,2},{27,3},{28,4},{29,5},{30,6},{31,7}} | collective-permute-start | bytes 393224 | tf_op jit(solution)/shard_map/while/body/eval_jaxpr/ppermute | solution.py:12
  1506.3 66.8 %collective-permute-start.2 = (bf16[512,128]{1,0:T(8,128)(2,1)}, bf16[512,128]{1,0:T(8,128)(2,1)S(1)}, u32[]{:S(2)}, u32[]{:S(2)}) collective-permute-start(bf16[512,128]{1,0:T(8,128)(2,1)} %get-tuple-element.1956), channel_id=1, source_target_pairs={{8,0},{16,8},{24,16},{9,1},{17,9},{25,17},{10,2},{18,10},{26,18},{... | collective-permute-start | bytes 393224 | tf_op jit(solution)/shard_map/while/body/eval_jaxpr/ppermute | solution.py:12
  1507.6 38.1 %collective-permute-start.3 = (bf16[512,128]{1,0:T(8,128)(2,1)}, bf16[512,128]{1,0:T(8,128)(2,1)S(1)}, u32[]{:S(2)}, u32[]{:S(2)}) collective-permute-start(bf16[512,128]{1,0:T(8,128)(2,1)} %get-tuple-element.1957), channel_id=1, source_target_pairs={{24,0},{25,1},{26,2},{27,3},{28,4},{29,5},{30,6},{31,7}} | collective-permute-start | bytes 393224 | tf_op jit(solution)/shard_map/while/body/eval_jaxpr/ppermute | solution.py:12
  1636.9 66.8 %collective-permute-start.2 = (bf16[512,128]{1,0:T(8,128)(2,1)}, bf16[512,128]{1,0:T(8,128)(2,1)S(1)}, u32[]{:S(2)}, u32[]{:S(2)}) collective-permute-start(bf16[512,128]{1,0:T(8,128)(2,1)} %get-tuple-element.1956), channel_id=1, source_target_pairs={{8,0},{16,8},{24,16},{9,1},{17,9},{25,17},{10,2},{18,10},{26,18},{... | collective-permute-start | bytes 393224 | tf_op jit(solution)/shard_map/while/body/eval_jaxpr/ppermute | solution.py:12
  1638.2 38.0 %collective-permute-start.3 = (bf16[512,128]{1,0:T(8,128)(2,1)}, bf16[512,128]{1,0:T(8,128)(2,1)S(1)}, u32[]{:S(2)}, u32[]{:S(2)}) collective-permute-start(bf16[512,128]{1,0:T(8,128)(2,1)} %get-tuple-element.1957), channel_id=1, source_target_pairs={{24,0},{25,1},{26,2},{27,3},{28,4},{29,5},{30,6},{31,7}} | collective-permute-start | bytes 393224 | tf_op jit(solution)/shard_map/while/body/eval_jaxpr/ppermute | solution.py:12
  1767.5 66.8 %collective-permute-start.2 = (bf16[512,128]{1,0:T(8,128)(2,1)}, bf16[512,128]{1,0:T(8,128)(2,1)S(1)}, u32[]{:S(2)}, u32[]{:S(2)}) collective-permute-start(bf16[512,128]{1,0:T(8,128)(2,1)} %get-tuple-element.1956), channel_id=1, source_target_pairs={{8,0},{16,8},{24,16},{9,1},{17,9},{25,17},{10,2},{18,10},{26,18},{... | collective-permute-start | bytes 393224 | tf_op jit(solution)/shard_map/while/body/eval_jaxpr/ppermute | solution.py:12
  1768.8 38.0 %collective-permute-start.3 = (bf16[512,128]{1,0:T(8,128)(2,1)}, bf16[512,128]{1,0:T(8,128)(2,1)S(1)}, u32[]{:S(2)}, u32[]{:S(2)}) collective-permute-start(bf16[512,128]{1,0:T(8,128)(2,1)} %get-tuple-element.1957), channel_id=1, source_target_pairs={{24,0},{25,1},{26,2},{27,3},{28,4},{29,5},{30,6},{31,7}} | collective-permute-start | bytes 393224 | tf_op jit(solution)/shard_map/while/body/eval_jaxpr/ppermute | solution.py:12
  1773.5 60.9 %copy-start.21 = (f32[8]{0:T(128)S(1)}, f32[8]{0:T(128)}, u32[]{:S(2)}) copy-start(f32[8]{0:T(128)} %copy-done.20) | copy-start | bytes 100 | tf_op jit(solution)/shard_map/while
  1898.1 66.8 %collective-permute-start.2 = (bf16[512,128]{1,0:T(8,128)(2,1)}, bf16[512,128]{1,0:T(8,128)(2,1)S(1)}, u32[]{:S(2)}, u32[]{:S(2)}) collective-permute-start(bf16[512,128]{1,0:T(8,128)(2,1)} %get-tuple-element.1956), channel_id=1, source_target_pairs={{8,0},{16,8},{24,16},{9,1},{17,9},{25,17},{10,2},{18,10},{26,18},{... | collective-permute-start | bytes 393224 | tf_op jit(solution)/shard_map/while/body/eval_jaxpr/ppermute | solution.py:12
  1899.3 38.0 %collective-permute-start.3 = (bf16[512,128]{1,0:T(8,128)(2,1)}, bf16[512,128]{1,0:T(8,128)(2,1)S(1)}, u32[]{:S(2)}, u32[]{:S(2)}) collective-permute-start(bf16[512,128]{1,0:T(8,128)(2,1)} %get-tuple-element.1957), channel_id=1, source_target_pairs={{24,0},{25,1},{26,2},{27,3},{28,4},{29,5},{30,6},{31,7}} | collective-permute-start | bytes 393224 | tf_op jit(solution)/shard_map/while/body/eval_jaxpr/ppermute | solution.py:12
  2028.6 66.8 %collective-permute-start.2 = (bf16[512,128]{1,0:T(8,128)(2,1)}, bf16[512,128]{1,0:T(8,128)(2,1)S(1)}, u32[]{:S(2)}, u32[]{:S(2)}) collective-permute-start(bf16[512,128]{1,0:T(8,128)(2,1)} %get-tuple-element.1956), channel_id=1, source_target_pairs={{8,0},{16,8},{24,16},{9,1},{17,9},{25,17},{10,2},{18,10},{26,18},{... | collective-permute-start | bytes 393224 | tf_op jit(solution)/shard_map/while/body/eval_jaxpr/ppermute | solution.py:12
  2029.9 37.0 %collective-permute-start.3 = (bf16[512,128]{1,0:T(8,128)(2,1)}, bf16[512,128]{1,0:T(8,128)(2,1)S(1)}, u32[]{:S(2)}, u32[]{:S(2)}) collective-permute-start(bf16[512,128]{1,0:T(8,128)(2,1)} %get-tuple-element.1957), channel_id=1, source_target_pairs={{24,0},{25,1},{26,2},{27,3},{28,4},{29,5},{30,6},{31,7}} | collective-permute-start | bytes 393224 | tf_op jit(solution)/shard_map/while/body/eval_jaxpr/ppermute | solution.py:12
  2099.3 142.2 %reduce-scatter.3.cloned.1.call-start = ((), (), s32[]{:S(2)}) async-start(), calls=%async_computation.2 | async-start | bytes 1310720 | tf_op jit(solution)/shard_map/reduce_scatter | solution.py:292
  2100.4 141.1 %reduce-scatter.5.cloned.1.call-start = ((), (), s32[]{:S(2)}) async-start(), calls=%async_computation.3 | async-start | bytes 2621440 | tf_op jit(solution)/shard_map/reduce_scatter | solution.py:293
  (171 other events, 4759.0 us)
Sparse Core Ops, SparseCore 0:
  2099.4 142.0 all-reduce.19
Sparse Core Ops, SparseCore 1:
  2103.2 31.8 reduce-scatter.2
  2138.7 35.0 reduce-scatter.4
where the time goes:
time: 2270 us; the launch traced here: 2250 us
  waiting for transfers between devices  712 us (31%)
  local copies, waits for them, and re-layouts  668 us (29%)
  blocking collectives  363 us (16%)
  starting transfers between devices  270 us (12%)
  other arithmetic  182 us (8%)
  matrix products  23.8 us (1%)
    ppermute x44, waiting for transfers between devices, from_behind(): lax.ppermute(value, axis, [(source, source + steps) for source in range(f...  612 us
    ppermute x44, starting transfers between devices, from_behind(): lax.ppermute(value, axis, [(source, source + steps) for source in range(f...  270 us
    gather x22, local copies, waits for them, and re-layouts, offset_conv(): gathered = with_zero(inputs)[offset_map]  267 us
    psum x11, blocking collectives, norm_stats(): lax.psum((jnp.sum(live_rows * hidden, axis=0), jnp.sum(live_rows * hidden...  166 us
    psum x11, blocking collectives, norm_back(): lax.psum((jnp.sum(upstream, axis=0), jnp.sum(upstream * centred, axis=0))...  156 us
    gather x11, local copies, waits for them, and re-layouts, offset_grad(): gathered = with_zero(inputs)[offset_map]  133 us
    scatter x11, local copies, waits for them, and re-layouts, down_back(): blank.at[places].set(pieces.reshape(-1, weight.shape[1]), mode='drop')  120 us
    psum x1, waiting for transfers between devices, total_grads(): lax.psum((down_sum, first_sum, second_sum, gain_grid, shift_grid), ('sect...  99.1 us
  transfers between devices with their start and end apart: 47, of which 23 were waited for; matrix products, arithmetic and copies ran while one was open for 5% of the time, Pallas kernels for 0%

commit v1 on v0

v1 whole, which is shorter than its diff:
```python
import functools

import jax
import jax.numpy as jnp
from jax import lax
from jax.experimental import pallas as pl
from jax.experimental.pallas import tpu as pltpu
from jax.sharding import PartitionSpec as P

EPSILON = 1e-05
F32 = jnp.float32
BF16 = jnp.bfloat16
VMEM_BYTES = 48 << 20


def mm(left, right):
    return jnp.dot(left, right, preferred_element_type=F32)


def mm_t(left, right):
    return lax.dot_general(left, right, (((1,), (1,)), ((), ())), preferred_element_type=F32)


def hits(index_row, rows):
    places = lax.broadcasted_iota(jnp.int16, (rows, index_row.shape[1]), 0)
    return jnp.where(places == index_row, jnp.bfloat16(1), jnp.bfloat16(0))


def near_hits(near_ref, offset):
    rows = near_ref.shape[2]
    return hits(near_ref[0, offset : offset + 1, :].astype(jnp.int16), rows)


def live_mask(near_ref, channels):
    rows = near_ref.shape[2]
    centre = near_ref[0, 13:14, :]
    count = jnp.sum((centre < rows).astype(F32), axis=1, keepdims=True)
    places = lax.broadcasted_iota(jnp.int32, (rows, channels), 0).astype(F32)
    return (places < count).astype(F32), count


def tree_sum(parts):
    parts = list(parts)
    while len(parts) > 1:
        parts = [parts[i] + parts[i + 1] for i in range(0, len(parts), 2)]
    return parts[0]


def moments(totals):
    count = totals[2:3]
    mean_row = totals[0:1] / count
    inv_std = lax.rsqrt(totals[1:2] / count - mean_row * mean_row + EPSILON)
    return mean_row, inv_std, count


def sigmoid(values):
    return 1.0 / (1.0 + jnp.exp(-values))


def put_sums(out_ref, first, second, count):
    channels = first.shape[1]
    third = jnp.broadcast_to(count, (1, channels))
    out_ref[0] = jnp.concatenate(
        [first, second, third, jnp.zeros((5, channels), F32)], axis=0
    )


def col_sum(values):
    return jnp.sum(values, axis=0, keepdims=True)


def parent_rows(down_ref, fine_rows):
    table = down_ref[0]
    first = jnp.min(table, axis=0, keepdims=True)
    children = jnp.sum((table < fine_rows).astype(jnp.int32), axis=0, keepdims=True)
    return table, first, first + children


def parent_hits(first, last, fine_rows, at, size):
    places = lax.broadcasted_iota(jnp.int16, (size, first.shape[1]), 0) + jnp.int16(at)
    inside = (places >= first.astype(jnp.int16)) & (places < last.astype(jnp.int16))
    return jnp.where(inside, jnp.bfloat16(1), jnp.bfloat16(0))


def down_kernel(where_ref, feats_ref, down_ref, near_ref, weight_ref, hidden_ref, sums_ref, kids_ref, which_ref, spread_ref):
    fine_rows, in_channels = feats_ref.shape[1], feats_ref.shape[2]
    offsets, coarse_rows = down_ref.shape[1], down_ref.shape[2]
    channels = weight_ref.shape[1]
    table, first, last = parent_rows(down_ref, fine_rows)
    rank = table - first
    numbers = lax.broadcasted_iota(jnp.int32, (offsets, coarse_rows), 0) + 1
    rows = [
        jnp.sum(jnp.where(rank == r, numbers, 0), axis=0, keepdims=True) for r in range(8)
    ]
    safe_first = jnp.where(first < fine_rows, first, 0)
    rows += [(safe_first // 16) * 16, safe_first % 16] + [jnp.zeros_like(first)] * 6
    lookup = jnp.concatenate(rows, axis=0).astype(F32).astype(BF16)
    step = 512
    for at in range(0, fine_rows, step):
        found = mm_t(parent_hits(first, last, fine_rows, at, step), lookup)
        begin = found[:, 8:9] + found[:, 9:10]
        place = lax.broadcasted_iota(jnp.int32, (step, 16), 0).astype(F32) + float(at)
        column = lax.broadcasted_iota(jnp.int32, (step, 16), 1).astype(F32)
        which = jnp.sum(
            jnp.where((column == place - begin) & (column < 8.0), found, 0.0), axis=1, keepdims=True
        )
        lane_half = (lax.broadcasted_iota(jnp.int32, (step, 2 * in_channels), 1) // in_channels).astype(F32)
        code = jnp.broadcast_to(which, (step, 2 * in_channels)) - lane_half
        which_ref[0, at : at + step] = code.astype(BF16)
        pair = jnp.concatenate([feats_ref[0, at : at + step]] * 2, axis=1)
        blank = jnp.zeros_like(pair)
        for j in range(offsets // 2):
            spread_ref[at : at + step, 2 * in_channels * j : 2 * in_channels * (j + 1)] = jnp.where(
                code == float(2 * j + 1), pair, blank
            )
    edges = jnp.concatenate([first, last, jnp.zeros((6, coarse_rows), jnp.int32)], axis=0).astype(F32)
    edges = jnp.transpose(edges)
    lanes = lax.broadcasted_iota(jnp.int32, (1, fine_rows), 1).astype(F32)
    part = 128
    total = jnp.zeros((1, channels), F32)
    square = jnp.zeros((1, channels), F32)
    for at in range(0, coarse_rows, part):
        low, high = edges[at : at + part, 0:1], edges[at : at + part, 1:2]
        owns = jnp.where((lanes >= low) & (lanes < high), 1.0, 0.0).astype(BF16)
        kids = mm(owns, spread_ref[...]).astype(BF16)
        kids_ref[0, at : at + part] = kids
        hidden = mm(kids, weight_ref[...])
        hidden_ref[0, at : at + part] = hidden
        total = total + col_sum(hidden)
        square = square + col_sum(hidden * hidden)
    _, count = live_mask(near_ref, channels)
    put_sums(sums_ref, total, square, count)


def conv_all(source, near_ref, weight_ref):
    out = mm(source, weight_ref[13])
    for j in range(0, 13):
        rows = [
            mm(near_hits(near_ref, 26 - k), source).astype(BF16) for k in (j, 26 - j)
        ]
        weight = jnp.concatenate([weight_ref[j], weight_ref[26 - j]], axis=0)
        out = out + mm(jnp.concatenate(rows, axis=1), weight)
    return out


def forward_kernel(norm_at, rounded, where_ref, hidden_ref, near_ref, weight_ref, scale_ref, shift_ref, *refs):
    part_refs, (act_ref, next_ref, sums_ref) = refs[:-3], refs[-3:]
    mean_row, inv_std, _ = moments(tree_sum([ref[0] for ref in part_refs]))
    live, count = live_mask(near_ref, hidden_ref.shape[2])
    value = (hidden_ref[0] - mean_row) * inv_std * scale_ref[norm_at : norm_at + 1] + shift_ref[norm_at : norm_at + 1]
    act = (live * (value * sigmoid(value))).astype(BF16)
    act_ref[0] = act
    hidden = conv_all(act, near_ref, weight_ref)
    if rounded:
        hidden = hidden.astype(BF16)
    next_ref[0] = hidden
    hidden = hidden.astype(F32)
    put_sums(sums_ref, col_sum(hidden), col_sum(hidden * hidden), count)


def output_kernel(where_ref, hidden_ref, act_ref, grad_ref, near_ref, scale_ref, shift_ref, *refs):
    part_refs, (features_ref, slope_ref, sums_ref) = refs[:-3], refs[-3:]
    mean_row, inv_std, _ = moments(tree_sum([ref[0] for ref in part_refs]))
    live, count = live_mask(near_ref, hidden_ref.shape[2])
    centred = (hidden_ref[0].astype(F32) - mean_row) * inv_std
    value = centred * scale_ref[2:3] + shift_ref[2:3] + act_ref[0].astype(F32)
    gate = sigmoid(value)
    features_ref[0] = (live * (value * gate)).astype(BF16)
    upstream = grad_ref[0].astype(F32) * live * (gate * (1.0 + value * (1.0 - gate)))
    slope_ref[0] = upstream
    put_sums(sums_ref, col_sum(upstream), col_sum(upstream * centred), count)


def norm_back(upstream, centred, live, inv_std, gain_row, back, count):
    return live * (inv_std * gain_row) * (upstream - back[0:1] / count - centred * (back[1:2] / count))


def backward_kernel(norm_at, with_skip, ways, where_ref, *refs):
    upstream_ref, hidden_ref, lower_ref, act_ref, near_ref, weight_ref, scale_ref, shift_ref = refs[:8]
    own_refs = refs[8 : 8 + ways]
    back_refs = refs[8 + ways : 8 + 2 * ways]
    below_refs = refs[8 + 2 * ways : 8 + 3 * ways]
    rest = refs[8 + 3 * ways :]
    skip_ref = rest[0] if with_skip else None
    next_ref, sums_ref, grad_ref = rest[-3:]
    mean_row, inv_std, count = moments(tree_sum([ref[0] for ref in own_refs]))
    back = tree_sum([ref[0] for ref in back_refs])
    live, own_count = live_mask(near_ref, hidden_ref.shape[2])
    centred = (hidden_ref[0].astype(F32) - mean_row) * inv_std
    rows_grad = norm_back(
        upstream_ref[0], centred, live, inv_std, scale_ref[norm_at : norm_at + 1], back, count
    ).astype(BF16)

    @pl.when(pl.program_id(0) == 0)
    def _():
        grad_ref[...] = jnp.zeros_like(grad_ref)

    channels = hidden_ref.shape[2]
    act_t = jnp.transpose(act_ref[0])
    below = mm_t(rows_grad, weight_ref[13])
    grad_ref[13] += mm(act_t, rows_grad)
    for j in range(13):
        moved = jnp.concatenate(
            [mm(near_hits(near_ref, k), rows_grad).astype(BF16) for k in (j, 26 - j)], axis=1
        )
        weight = jnp.concatenate([weight_ref[j], weight_ref[26 - j]], axis=1)
        below = below + mm_t(moved, weight)
        pair = mm(act_t, moved)
        grad_ref[j] += pair[:, :channels]
        grad_ref[26 - j] += pair[:, channels:]
    below = below.astype(BF16).astype(F32)
    if with_skip:
        below = below + skip_ref[0].astype(BF16).astype(F32)
    low_mean, low_std, _ = moments(tree_sum([ref[0] for ref in below_refs]))
    low_centred = (lower_ref[0] - low_mean) * low_std
    value = low_centred * scale_ref[norm_at - 1 : norm_at] + shift_ref[norm_at - 1 : norm_at]
    gate = sigmoid(value)
    upstream = below * live * (gate * (1.0 + value * (1.0 - gate)))
    next_ref[0] = upstream
    put_sums(sums_ref, col_sum(upstream), col_sum(upstream * low_centred), own_count)


def input_kernel(ways, where_ref, upstream_ref, hidden_ref, kids_ref, which_ref, down_ref, near_ref, weight_ref, scale_ref, *refs):
    own_refs, back_refs = refs[:ways], refs[ways : 2 * ways]
    input_ref, grad_ref = refs[2 * ways :]
    mean_row, inv_std, count = moments(tree_sum([ref[0] for ref in own_refs]))
    back = tree_sum([ref[0] for ref in back_refs])
    live, _ = live_mask(near_ref, hidden_ref.shape[2])
    centred = (hidden_ref[0] - mean_row) * inv_std
    rows_grad = norm_back(
        upstream_ref[0], centred, live, inv_std, scale_ref[0:1], back, count
    ).astype(BF16)

    @pl.when(pl.program_id(0) == 0)
    def _():
        grad_ref[...] = jnp.zeros_like(grad_ref)

    grad_ref[...] += jnp.transpose(mm(jnp.transpose(rows_grad), kids_ref[0]))
    pieces = mm_t(rows_grad, weight_ref[...]).astype(BF16)
    fine_rows, in_channels = input_ref.shape[1], input_ref.shape[2]
    _, first, last = parent_rows(down_ref, fine_rows)
    wide = 2 * in_channels
    step = 256
    for at in range(0, fine_rows, step):
        full = mm(parent_hits(first, last, fine_rows, at, step), pieces)
        code = which_ref[0, at : at + step].astype(F32)
        out = jnp.zeros((step, wide), F32)
        for j in range(full.shape[1] // wide):
            out = out + jnp.where(code == float(2 * j + 1), full[:, wide * j : wide * (j + 1)], 0.0)
        input_ref[0, at : at + step] = (out[:, :in_channels] + out[:, in_channels:]).astype(BF16)


def whole(array):
    return pl.BlockSpec(array.shape, lambda b, where: (0,) * array.ndim)


def per_micro(array, picked):
    block = (1,) + array.shape[1:]
    rest = (0,) * (array.ndim - 1)
    if picked:
        return pl.BlockSpec(block, lambda b, where: (where[0] + b,) + rest)
    return pl.BlockSpec(block, lambda b, where: (b,) + rest)


def call(kernel, steps, where, operands, kinds, outs, out_kinds, scratch=()):
    def spec(array, kind):
        if kind == "all":
            return whole(array)
        return per_micro(array, kind == "pick")

    return pl.pallas_call(
        kernel,
        grid_spec=pltpu.PrefetchScalarGridSpec(
            num_scalar_prefetch=1,
            grid=(steps,),
            in_specs=[spec(a, k) for a, k in zip(operands, kinds)],
            out_specs=[spec(a, k) for a, k in zip(outs, out_kinds)],
            scratch_shapes=list(scratch),
        ),
        out_shape=outs,
        compiler_params=pltpu.CompilerParams(
            vmem_limit_bytes=VMEM_BYTES, dimension_semantics=("arbitrary",)
        ),
    )(where, *operands)


def bucket_sums(value, axis):
    count = lax.axis_size(axis)
    value = value + lax.ppermute(value, axis, [(i, i ^ 1) for i in range(count)])
    return [value] + [
        lax.ppermute(value, axis, [(i, i ^ step) for i in range(count)])
        for step in range(2, count, 2)
    ]


def local(
    voxel_feats, down_map, neighbours, w_down, w_first, w_second, bn_scale, bn_shift, out_grad
):
    sections = lax.axis_size("section")
    mine = voxel_feats.shape[0] // sections
    where = jnp.reshape(lax.axis_index("section") * mine, (1,)).astype(jnp.int32)
    fine_rows, in_channels = voxel_feats.shape[1:]
    coarse_rows = neighbours.shape[2]
    channels = w_first.shape[2]
    offsets = down_map.shape[1]
    wide = offsets * in_channels
    flat_down = w_down.reshape(wide, channels)
    shape = jax.ShapeDtypeStruct
    rows_f32 = shape((mine, coarse_rows, channels), F32)
    rows_bf16 = shape((mine, coarse_rows, channels), BF16)
    sums = shape((mine, 8, channels), F32)

    hidden_zero, part_zero, kids, which = call(
        down_kernel, mine, where,
        [voxel_feats, down_map, neighbours, flat_down],
        ["pick", "pick", "pick", "all"],
        [rows_f32, sums, shape((mine, coarse_rows, wide), BF16), shape((mine, fine_rows, 2 * in_channels), BF16)],
        ["own"] * 4,
        [pltpu.VMEM((fine_rows, wide), BF16)],
    )
    stats_zero = bucket_sums(part_zero, "dp")
    ways = len(stats_zero)
    act_zero, hidden_one, part_one = call(
        functools.partial(forward_kernel, 0, False), mine, where,
        [hidden_zero, neighbours, w_first, bn_scale, bn_shift] + stats_zero,
        ["own", "pick", "all", "all", "all"] + ["own"] * ways,
        [rows_bf16, rows_f32, sums], ["own"] * 3,
    )
    stats_one = bucket_sums(part_one, "dp")
    act_one, hidden_two, part_two = call(
        functools.partial(forward_kernel, 1, True), mine, where,
        [hidden_one, neighbours, w_second, bn_scale, bn_shift] + stats_one,
        ["own", "pick", "all", "all", "all"] + ["own"] * ways,
        [rows_bf16, rows_bf16, sums], ["own"] * 3,
    )
    stats_two = bucket_sums(part_two, "dp")
    features, up_two, back_part = call(
        output_kernel, mine, where,
        [hidden_two, act_zero, out_grad, neighbours, bn_scale, bn_shift] + stats_two,
        ["own", "own", "pick", "pick", "all", "all"] + ["own"] * ways,
        [rows_bf16, rows_f32, sums], ["own"] * 3,
    )
    back_two = bucket_sums(back_part, "dp")
    grad_shape = shape(w_first.shape, F32)
    up_one, back_part, grad_second = call(
        functools.partial(backward_kernel, 2, False, ways), mine, where,
        [up_two, hidden_two, hidden_one, act_one, neighbours, w_second, bn_scale, bn_shift]
        + stats_two + back_two + stats_one,
        ["own"] * 4 + ["pick"] + ["all"] * 3 + ["own"] * (3 * ways),
        [rows_f32, sums, grad_shape], ["own", "own", "all"],
    )
    back_one = bucket_sums(back_part, "dp")
    up_zero, back_part, grad_first = call(
        functools.partial(backward_kernel, 1, True, ways), mine, where,
        [up_one, hidden_one, hidden_zero, act_zero, neighbours, w_first, bn_scale, bn_shift]
        + stats_one + back_one + stats_zero + [up_two],
        ["own"] * 4 + ["pick"] + ["all"] * 3 + ["own"] * (3 * ways + 1),
        [rows_f32, sums, grad_shape], ["own", "own", "all"],
    )
    back_zero = bucket_sums(back_part, "dp")
    input_grad, grad_down = call(
        functools.partial(input_kernel, ways), mine, where,
        [up_zero, hidden_zero, kids, which, down_map, neighbours, flat_down, bn_scale]
        + stats_zero + back_zero,
        ["own"] * 4 + ["pick"] * 2 + ["all"] * 2 + ["own"] * (2 * ways),
        [shape((mine, fine_rows, in_channels), BF16), shape((wide, channels), F32)], ["own", "all"],
    )
    norm_sums = jnp.stack(
        [jnp.sum(tree_sum(parts)[:, :2], axis=0) for parts in (back_zero, back_one, back_two)]
    )
    norm_sums = lax.psum(norm_sums, "section")
    grad_down, grad_first, grad_second = lax.psum((grad_down, grad_first, grad_second), ("section", "dp"))
    return (
        features,
        input_grad,
        grad_down.reshape(w_down.shape),
        grad_first,
        grad_second,
        norm_sums[:, 1],
        norm_sums[:, 0],
    )


def solution(mesh):
    in_specs = (
        P(None, "dp", None),
        P(None, None, "dp"),
        P(None, None, "dp"),
        P(),
        P(),
        P(),
        P(),
        P(),
        P(None, "dp", None),
    )
    out_specs = (P("section", "dp", None), P("section", "dp", None), P(), P(), P(), P(), P())
    return jax.shard_map(local, mesh=mesh, in_specs=in_specs, out_specs=out_specs, check_vma=False)
```

time: 2270 us -> 295 us (0.13)
  local copies, waits for them, and re-layouts: 668 us -> 13.7 us
  waiting for transfers between devices: 712 us -> 148 us
  blocking collectives: 363 us -> 8 us
  starting transfers between devices: 270 us -> 31.2 us
  other arithmetic: 182 us -> 0.07 us
  Pallas kernels: 0 us -> 77.5 us
  matrix products: 23.8 us -> 0 us
    ppermute x44 -> x24, waiting for transfers between devices: 612 us -> 16.6 us  [the longest x18 11.4 us: bucket_sums(): lax.ppermute(value, axis, [(i, i ^ step) for i in range(count)])]
    gather x33 -> x0, local copies, waits for them, and re-layouts: 400 us -> none  [the longest x22 267 us: offset_conv(): gathered = with_zero(inputs)[offset_map]]
    psum x23 -> x1, blocking collectives: 363 us -> 8 us  [local(): norm_sums = lax.psum(norm_sums, 'section')]
    ppermute x44 -> x24, starting transfers between devices: 270 us -> 31.2 us  [the longest x18 22.5 us: bucket_sums(): lax.ppermute(value, axis, [(i, i ^ step) for i in range(count)])]
    scatter x11 -> x0, local copies, waits for them, and re-layouts: 120 us -> none  [down_back(): blank.at[places].set(pieces.reshape(-1, weight.shape[1]), mode='drop')]
    pallas_call x0 -> x7, Pallas kernels: none -> 77.5 us  [call(): pl.pallas_call(kernel, grid_spec=pltpu.PrefetchScalarGridSpec(num_scalar_...]
    dynamic_update_slice x44 -> x0, other arithmetic: 46.1 us -> none  [store_at(): lax.dynamic_update_index_in_dim(buffer, jnp.where(keep_it, update, buffer...]
    squeeze x44 -> x1, local copies, waits for them, and re-layouts: 45.7 us -> 0.59 us  [local(): norm_sums[:, 0]]
  transfers between devices with their start and end apart: 47 -> 25, of which waited for: 23 -> 22; matrix products, arithmetic and copies ran while one was open for 5% -> 1% of each run, Pallas kernels for 0% -> 0%
where the time goes in v1:
time: 295 us; the launch traced here: 292 us
  waiting for transfers between devices  148 us (50%)
  Pallas kernels  77.5 us (26%)
  starting transfers between devices  31.2 us (11%)
  between operations  14.2 us (5%)
  local copies, waits for them, and re-layouts  13.7 us (5%)
  blocking collectives  8 us (3%)
    psum x1, waiting for transfers between devices, local(): lax.psum((grad_down, grad_first, grad_second), ('section', 'dp'))  131 us
    pallas_call x7, Pallas kernels, call(): pl.pallas_call(kernel, grid_spec=pltpu.PrefetchScalarGridSpec(num_scalar_...  77.5 us
    ppermute x18, starting transfers between devices, bucket_sums(): lax.ppermute(value, axis, [(i, i ^ step) for i in range(count)])  22.5 us
    unnamed x22, local copies, waits for them, and re-layouts  13.1 us
    ppermute x18, waiting for transfers between devices, bucket_sums(): lax.ppermute(value, axis, [(i, i ^ step) for i in range(count)])  11.4 us
    ppermute x6, starting transfers between devices, bucket_sums(): lax.ppermute(value, axis, [(i, i ^ 1) for i in range(count)])  8.68 us
    psum x1, blocking collectives, local(): norm_sums = lax.psum(norm_sums, 'section')  8 us
  transfers between devices with their start and end apart: 25, of which 22 were waited for; matrix products, arithmetic and copies ran while one was open for 1% of the time, Pallas kernels for 0%

profile of v1, /device:TPU:1, one launch (start us, length us, event | category | flops | bytes accessed | tf_op | source)
XLA Modules:
  0.0 292.4 jit_solution(11841225207525441264)
XLA Ops:
  7.2 1.3 copy.17.near_ref.refs_4_
  8.5 4.8 %copy.16.feats_ref = bf16[8,2048,64]{2,1,0:T(8,128)(2,1)} copy(bf16[8,2048,64]{1,2,0:T(8,128)(2,1)} %param.9) | data formatting | bytes 4194304 | tf_op args[0]
  13.4 23.9 %shard_map.144 = (f32[2,512,128]{2,1,0:T(8,128)S(1)}, f32[2,8,128]{2,1,0:T(8,128)S(1)}, bf16[2,512,512]{2,1,0:T(8,128)(2,1)S(1)}, bf16[2,2048,128]{2,1,0:T(8,128)(2,1)S(1)}) custom-call(s32[1]{0:T(128)} %bitcast.where_ref, bf16[8,2048,64]{2,1,0:T(8,128)(2,1)} %copy.16.feats_ref, s32[8,8,512]{2,1,0:T(8,128)S(1)} %copy-done.3, ...), custom_call_target="tpu_custom_call" | custom-call | tf_op jit(solution)/shard_map/pallas_call | solution.py:271
  37.5 1.1 collective-permute-done
  38.6 4.5 %collective-permute-start.3 = (f32[2,8,128]{2,1,0:T(8,128)S(1)}, f32[2,8,128]{2,1,0:T(8,128)S(1)}, u32[]{:S(2)}, u32[]{:S(2)}) collective-permute-start(f32[2,8,128]{2,1,0:T(8,128)S(1)} %add.53.refs_0_.refs_16_), channel_id=1, source_target_pairs={{0,6},{1,7},{2,4},{3,5},{4,2},{5,3},{6,0},{7,1},{8,14},{9,15},{10,... | collective-permute-start | bytes 24584 | tf_op jit(solution)/shard_map/ppermute | solution.py:291
  43.3 0.8 collective-permute-done.3.refs_3_.refs_19_
  44.1 2.3 collective-permute-done.2.refs_2_.refs_18_
  46.5 9.9 %shard_map.145 = (bf16[2,512,128]{2,1,0:T(8,128)(2,1)S(1)}, f32[2,512,128]{2,1,0:T(8,128)S(1)}, f32[2,8,128]{2,1,0:T(8,128)S(1)}) custom-call(s32[1]{0:T(128)} %bitcast.where_ref, f32[2,512,128]{2,1,0:T(8,128)S(1)} %get-tuple-element.28.hidden_ref.refs_2_, s32[8,27,512]{2,1,0:T(8,128)S(1)} %copy.17.near_ref.refs_4_, bf16[27,128,128]{2,1,0:T(8,128)(2,1)S(1)} %copy-done.1, ...), custom_call_target="tpu_custom_call" | custom-call | tf_op jit(solution)/shard_map/pallas_call | solution.py:271
  56.4 1.8 collective-permute-start.4
  58.2 0.8 collective-permute-done.4
  59.1 1.2 collective-permute-start.7
  60.8 1.8 collective-permute-start.5
  62.6 0.8 collective-permute-done.7.refs_3_.refs_19_.refs_11_
  64.0 9.9 %shard_map.146 = (bf16[2,512,128]{2,1,0:T(8,128)(2,1)S(1)}, bf16[2,512,128]{2,1,0:T(8,128)(2,1)S(1)}, f32[2,8,128]{2,1,0:T(8,128)S(1)}) custom-call(s32[1]{0:T(128)} %bitcast.where_ref, f32[2,512,128]{2,1,0:T(8,128)S(1)} %get-tuple-element.30.hidden_ref.refs_2_.refs_1_, s32[8,27,512]{2,1,0:T(8,128)S(1)} %copy.17.near_ref.refs_4_, ...), custom_call_target="tpu_custom_call" | custom-call | tf_op jit(solution)/shard_map/pallas_call | solution.py:271
  73.9 1.5 collective-permute-start.8
  75.5 0.8 collective-permute-done.8
  76.3 2.2 collective-permute-start.11
  79.2 0.7 collective-permute-start.9
  79.9 0.8 collective-permute-done.11.refs_3_.refs_11_
  80.6 1.3 collective-permute-done.10.refs_2_.refs_10_
  82.0 1.3 shard_map.147
  83.2 1.9 collective-permute-start.12
  85.1 0.8 collective-permute-done.12
  85.9 1.1 collective-permute-start.15
  87.0 0.7 collective-permute-start.14
  87.7 1.7 collective-permute-start.13
  89.5 0.8 collective-permute-done.15.refs_15_
  90.8 14.4 %shard_map.148 = (f32[2,512,128]{2,1,0:T(8,128)S(1)}, f32[2,8,128]{2,1,0:T(8,128)S(1)}, f32[27,128,128]{2,1,0:T(8,128)}) custom-call(s32[1]{0:T(128)} %bitcast.where_ref, f32[2,512,128]{2,1,0:T(8,128)S(1)} %get-tuple-element.36.refs_0_.refs_20_, bf16[2,512,128]{2,1,0:T(8,128)(2,1)S(1)} %get-tuple-element.32.hidden_ref.refs_1_, ...), custom_call_target="tpu_custom_call" | custom-call | tf_op jit(solution)/shard_map/pallas_call | solution.py:271
  105.2 1.5 collective-permute-start.16
  106.7 0.8 collective-permute-done.16
  107.5 2.2 collective-permute-start.19
  109.8 0.7 collective-permute-start.18
  111.1 0.8 collective-permute-done.19.refs_15_
  111.8 1.3 collective-permute-done.18.refs_14_
  113.2 14.4 %shard_map.149 = (f32[2,512,128]{2,1,0:T(8,128)S(1)}, f32[2,8,128]{2,1,0:T(8,128)S(1)}, f32[27,128,128]{2,1,0:T(8,128)}) custom-call(s32[1]{0:T(128)} %bitcast.where_ref, f32[2,512,128]{2,1,0:T(8,128)S(1)} %get-tuple-element.39.refs_0_, f32[2,512,128]{2,1,0:T(8,128)S(1)} %get-tuple-element.30.hidden_ref.refs_2_.refs_1_, ...), custom_call_target="tpu_custom_call" | custom-call | tf_op jit(solution)/shard_map/pallas_call | solution.py:271
  127.6 1.9 collective-permute-start.20
  129.5 0.8 collective-permute-done.20
  130.3 1.1 collective-permute-start.23
  131.4 0.7 collective-permute-start.22
  132.1 1.7 collective-permute-start.21
  133.8 0.8 collective-permute-done.23.refs_7_
  135.2 3.6 %shard_map.150 = (bf16[2,2048,64]{2,1,0:T(8,128)(2,1)S(1)}, f32[512,128]{1,0:T(8,128)}) custom-call(s32[1]{0:T(128)} %bitcast.where_ref, f32[2,512,128]{2,1,0:T(8,128)S(1)} %get-tuple-element.41.upstream_ref, f32[2,512,128]{2,1,0:T(8,128)S(1)} %get-tuple-element.28.hidden_ref.refs_2_, bf16[2,512,512]{2,1,0:T(8,128)(2,1)S(1)} %get-tuple-element.42.kids_ref, ...), custom_call_target="tpu_custom_call" | custom-call | tf_op jit(solution)/shard_map/pallas_call | solution.py:271
  138.8 1.1 copy.24
  140.0 8.0 %psum.31 = f32[3,2,128]{2,0,1:T(4,128)S(1)} all-reduce(f32[3,2,128]{2,0,1:T(4,128)S(1)} %pad_maximum_fusion), channel_id=1, replica_groups=mesh['section'=4,'dp'=8] {'section'}, use_global_device_ids=true, to_apply=%region_6.0 | all-reduce | flops 768 | bytes 6144 | tf_op jit(solution)/shard_map/psum | solution.py:371
  148.6 131.0 %all-reduce.3.cloned.1.call-done = (f32[8,64,128]{2,1,0:T(8,128)}, f32[27,128,128]{2,1,0:T(8,128)}, f32[27,128,128]{2,1,0:T(8,128)}) async-done(((f32[8,64,128]{2,1,0:T(8,128)}, f32[27,128,128]{2,1,0:T(8,128)}, f32[27,128,128]{2,1,0:T(8,128)}), (f32[8,64,128]{2,1,0:T(8,128)}, f32[27,128,128]{2,1,0:T(8,128)}, f32[27,128,128]{2,1,0:T(8,128)})) %all-reduce.3.cloned.1.call-update) | async-done | bytes 3801104 | tf_op jit(solution)/shard_map/psum | solution.py:372
  279.6 1.7 copy.28
  281.3 3.0 %copy.29 = f32[27,128,128]{2,1,0:T(8,128)} copy(f32[27,128,128]{2,1,0:T(8,128)} %get-tuple-element.64) | data formatting | bytes 3538944
  284.3 1.2 copy.30
  (44 shorter events, 4.8 us)
Async XLA Ops:
  7.2 272.5 %all-reduce.3.cloned.1.call-start = ((), (), s32[]{:S(2)}) async-start(), calls=%async_computation | async-start | bytes 7602176 | tf_op jit(solution)/shard_map/psum | solution.py:372
  8.5 4.8 %copy-start.3 = (s32[8,8,512]{2,1,0:T(8,128)S(1)}, s32[8,8,512]{2,1,0:T(8,128)}, u32[]{:S(2)}) copy-start(s32[8,8,512]{2,1,0:T(8,128)} %down_ref.3) | copy-start | bytes 393220
  8.5 4.8 %copy-start.4 = (bf16[8,64,128]{2,1,0:T(8,128)(2,1)S(1)}, bf16[8,64,128]{2,1,0:T(8,128)(2,1)}, u32[]{:S(2)}) copy-start(bf16[8,64,128]{2,1,0:T(8,128)(2,1)} %param.12) | copy-start | bytes 393220
  13.3 33.1 %copy-start.1 = (bf16[27,128,128]{2,1,0:T(8,128)(2,1)S(1)}, bf16[27,128,128]{2,1,0:T(8,128)(2,1)}, u32[]{:S(2)}) copy-start(bf16[27,128,128]{2,1,0:T(8,128)(2,1)} %refs_5_.3) | copy-start | bytes 2654212
  13.3 33.1 %copy-start.5 = (f32[3,128]{1,0:T(4,128)S(1)}, f32[3,128]{1,0:T(4,128)}, u32[]{:S(2)}) copy-start(f32[3,128]{1,0:T(4,128)} %scale_ref.7) | copy-start | bytes 4612
  13.3 33.1 %copy-start.6 = (f32[3,128]{1,0:T(4,128)S(1)}, f32[3,128]{1,0:T(4,128)}, u32[]{:S(2)}) copy-start(f32[3,128]{1,0:T(4,128)} %refs_7_.3) | copy-start | bytes 4612
  37.3 26.7 %copy-start = (bf16[27,128,128]{2,1,0:T(8,128)(2,1)S(1)}, bf16[27,128,128]{2,1,0:T(8,128)(2,1)}, u32[]{:S(2)}) copy-start(bf16[27,128,128]{2,1,0:T(8,128)(2,1)} %refs_5_.2) | copy-start | bytes 2654212
  37.3 1.2 collective-permute-start
  38.6 5.6 %collective-permute-start.3 = (f32[2,8,128]{2,1,0:T(8,128)S(1)}, f32[2,8,128]{2,1,0:T(8,128)S(1)}, u32[]{:S(2)}, u32[]{:S(2)}) collective-permute-start(f32[2,8,128]{2,1,0:T(8,128)S(1)} %add.53.refs_0_.refs_16_), channel_id=1, source_target_pairs={{0,6},{1,7},{2,4},{3,5},{4,2},{5,3},{6,0},{7,1},{8,14},{9,15},{10,... | collective-permute-start | bytes 24584 | tf_op jit(solution)/shard_map/ppermute | solution.py:291
  43.1 3.4 %collective-permute-start.2 = (f32[2,8,128]{2,1,0:T(8,128)S(1)}, f32[2,8,128]{2,1,0:T(8,128)S(1)}, u32[]{:S(2)}, u32[]{:S(2)}) collective-permute-start(f32[2,8,128]{2,1,0:T(8,128)S(1)} %add.53.refs_0_.refs_16_), channel_id=1, source_target_pairs={{0,4},{1,5},{2,6},{3,7},{4,0},{5,1},{6,2},{7,3},{8,12},{9,13},{10,... | collective-permute-start | bytes 24584 | tf_op jit(solution)/shard_map/ppermute | solution.py:291
  43.1 3.4 %collective-permute-start.1 = (f32[2,8,128]{2,1,0:T(8,128)S(1)}, f32[2,8,128]{2,1,0:T(8,128)S(1)}, u32[]{:S(2)}, u32[]{:S(2)}) collective-permute-start(f32[2,8,128]{2,1,0:T(8,128)S(1)} %add.53.refs_0_.refs_16_), channel_id=1, source_target_pairs={{0,2},{1,3},{2,0},{3,1},{4,6},{5,7},{6,4},{7,5},{8,10},{9,11},{10,... | collective-permute-start | bytes 24584 | tf_op jit(solution)/shard_map/ppermute | solution.py:291
  46.5 35.5 %copy-start.2 = (bf16[8,512,128]{2,1,0:T(8,128)(2,1)S(1)}, bf16[8,512,128]{2,1,0:T(8,128)(2,1)}, u32[]{:S(2)}) copy-start(bf16[8,512,128]{2,1,0:T(8,128)(2,1)} %grad_ref.1) | copy-start | bytes 3145732
  56.4 2.7 collective-permute-start.4
  59.1 4.3 %collective-permute-start.7 = (f32[2,8,128]{2,1,0:T(8,128)S(1)}, f32[2,8,128]{2,1,0:T(8,128)S(1)}, u32[]{:S(2)}, u32[]{:S(2)}) collective-permute-start(f32[2,8,128]{2,1,0:T(8,128)S(1)} %add.54.refs_0_.refs_16_.refs_8_), channel_id=1, source_target_pairs={{0,6},{1,7},{2,4},{3,5},{4,2},{5,3},{6,0},{7,1},{8,14},{9,15},{10,... | collective-permute-start | bytes 24584 | tf_op jit(solution)/shard_map/ppermute | solution.py:291
  60.3 3.4 %collective-permute-start.6 = (f32[2,8,128]{2,1,0:T(8,128)S(1)}, f32[2,8,128]{2,1,0:T(8,128)S(1)}, u32[]{:S(2)}, u32[]{:S(2)}) collective-permute-start(f32[2,8,128]{2,1,0:T(8,128)S(1)} %add.54.refs_0_.refs_16_.refs_8_), channel_id=1, source_target_pairs={{0,4},{1,5},{2,6},{3,7},{4,0},{5,1},{6,2},{7,3},{8,12},{9,13},{10,... | collective-permute-start | bytes 24584 | tf_op jit(solution)/shard_map/ppermute | solution.py:291
  60.8 3.2 %collective-permute-start.5 = (f32[2,8,128]{2,1,0:T(8,128)S(1)}, f32[2,8,128]{2,1,0:T(8,128)S(1)}, u32[]{:S(2)}, u32[]{:S(2)}) collective-permute-start(f32[2,8,128]{2,1,0:T(8,128)S(1)} %add.54.refs_0_.refs_16_.refs_8_), channel_id=1, source_target_pairs={{0,2},{1,3},{2,0},{3,1},{4,6},{5,7},{6,4},{7,5},{8,10},{9,11},{10,... | collective-permute-start | bytes 24584 | tf_op jit(solution)/shard_map/ppermute | solution.py:291
  73.9 2.4 collective-permute-start.8
  76.3 4.3 %collective-permute-start.11 = (f32[2,8,128]{2,1,0:T(8,128)S(1)}, f32[2,8,128]{2,1,0:T(8,128)S(1)}, u32[]{:S(2)}, u32[]{:S(2)}) collective-permute-start(f32[2,8,128]{2,1,0:T(8,128)S(1)} %add.55.refs_0_.refs_8_), channel_id=1, source_target_pairs={{0,6},{1,7},{2,4},{3,5},{4,2},{5,3},{6,0},{7,1},{8,14},{9,15},{10,... | collective-permute-start | bytes 24584 | tf_op jit(solution)/shard_map/ppermute | solution.py:291
  78.5 3.4 %collective-permute-start.10 = (f32[2,8,128]{2,1,0:T(8,128)S(1)}, f32[2,8,128]{2,1,0:T(8,128)S(1)}, u32[]{:S(2)}, u32[]{:S(2)}) collective-permute-start(f32[2,8,128]{2,1,0:T(8,128)S(1)} %add.55.refs_0_.refs_8_), channel_id=1, source_target_pairs={{0,4},{1,5},{2,6},{3,7},{4,0},{5,1},{6,2},{7,3},{8,12},{9,13},{10,... | collective-permute-start | bytes 24584 | tf_op jit(solution)/shard_map/ppermute | solution.py:291
  79.2 2.8 collective-permute-start.9
  83.2 2.7 collective-permute-start.12
  85.9 4.3 %collective-permute-start.15 = (f32[2,8,128]{2,1,0:T(8,128)S(1)}, f32[2,8,128]{2,1,0:T(8,128)S(1)}, u32[]{:S(2)}, u32[]{:S(2)}) collective-permute-start(f32[2,8,128]{2,1,0:T(8,128)S(1)} %add.56.refs_12_), channel_id=1, source_target_pairs={{0,6},{1,7},{2,4},{3,5},{4,2},{5,3},{6,0},{7,1},{8,14},{9,15},{10,... | collective-permute-start | bytes 24584 | tf_op jit(solution)/shard_map/ppermute | solution.py:291
  87.0 3.4 %collective-permute-start.14 = (f32[2,8,128]{2,1,0:T(8,128)S(1)}, f32[2,8,128]{2,1,0:T(8,128)S(1)}, u32[]{:S(2)}, u32[]{:S(2)}) collective-permute-start(f32[2,8,128]{2,1,0:T(8,128)S(1)} %add.56.refs_12_), channel_id=1, source_target_pairs={{0,4},{1,5},{2,6},{3,7},{4,0},{5,1},{6,2},{7,3},{8,12},{9,13},{10,... | collective-permute-start | bytes 24584 | tf_op jit(solution)/shard_map/ppermute | solution.py:291
  87.7 3.1 %collective-permute-start.13 = (f32[2,8,128]{2,1,0:T(8,128)S(1)}, f32[2,8,128]{2,1,0:T(8,128)S(1)}, u32[]{:S(2)}, u32[]{:S(2)}) collective-permute-start(f32[2,8,128]{2,1,0:T(8,128)S(1)} %add.56.refs_12_), channel_id=1, source_target_pairs={{0,2},{1,3},{2,0},{3,1},{4,6},{5,7},{6,4},{7,5},{8,10},{9,11},{10,... | collective-permute-start | bytes 24584 | tf_op jit(solution)/shard_map/ppermute | solution.py:291
  105.2 2.3 collective-permute-start.16
  107.5 4.3 %collective-permute-start.19 = (f32[2,8,128]{2,1,0:T(8,128)S(1)}, f32[2,8,128]{2,1,0:T(8,128)S(1)}, u32[]{:S(2)}, u32[]{:S(2)}) collective-permute-start(f32[2,8,128]{2,1,0:T(8,128)S(1)} %add.57.refs_12_), channel_id=1, source_target_pairs={{0,6},{1,7},{2,4},{3,5},{4,2},{5,3},{6,0},{7,1},{8,14},{9,15},{10,... | collective-permute-start | bytes 24584 | tf_op jit(solution)/shard_map/ppermute | solution.py:291
  109.8 3.4 %collective-permute-start.18 = (f32[2,8,128]{2,1,0:T(8,128)S(1)}, f32[2,8,128]{2,1,0:T(8,128)S(1)}, u32[]{:S(2)}, u32[]{:S(2)}) collective-permute-start(f32[2,8,128]{2,1,0:T(8,128)S(1)} %add.57.refs_12_), channel_id=1, source_target_pairs={{0,4},{1,5},{2,6},{3,7},{4,0},{5,1},{6,2},{7,3},{8,12},{9,13},{10,... | collective-permute-start | bytes 24584 | tf_op jit(solution)/shard_map/ppermute | solution.py:291
  110.5 2.7 collective-permute-start.17
  127.6 2.7 collective-permute-start.20
  130.3 4.3 %collective-permute-start.23 = (f32[2,8,128]{2,1,0:T(8,128)S(1)}, f32[2,8,128]{2,1,0:T(8,128)S(1)}, u32[]{:S(2)}, u32[]{:S(2)}) collective-permute-start(f32[2,8,128]{2,1,0:T(8,128)S(1)} %add.58.refs_4_), channel_id=1, source_target_pairs={{0,6},{1,7},{2,4},{3,5},{4,2},{5,3},{6,0},{7,1},{8,14},{9,15},{10,... | collective-permute-start | bytes 24584 | tf_op jit(solution)/shard_map/ppermute | solution.py:291
  131.4 3.4 %collective-permute-start.22 = (f32[2,8,128]{2,1,0:T(8,128)S(1)}, f32[2,8,128]{2,1,0:T(8,128)S(1)}, u32[]{:S(2)}, u32[]{:S(2)}) collective-permute-start(f32[2,8,128]{2,1,0:T(8,128)S(1)} %add.58.refs_4_), channel_id=1, source_target_pairs={{0,4},{1,5},{2,6},{3,7},{4,0},{5,1},{6,2},{7,3},{8,12},{9,13},{10,... | collective-permute-start | bytes 24584 | tf_op jit(solution)/shard_map/ppermute | solution.py:291
  132.1 3.1 %collective-permute-start.21 = (f32[2,8,128]{2,1,0:T(8,128)S(1)}, f32[2,8,128]{2,1,0:T(8,128)S(1)}, u32[]{:S(2)}, u32[]{:S(2)}) collective-permute-start(f32[2,8,128]{2,1,0:T(8,128)S(1)} %add.58.refs_4_), channel_id=1, source_target_pairs={{0,2},{1,3},{2,0},{3,1},{4,6},{5,7},{6,4},{7,5},{8,10},{9,11},{10,... | collective-permute-start | bytes 24584 | tf_op jit(solution)/shard_map/ppermute | solution.py:291
  281.3 3.0 %copy-start.7 = (f32[27,128,128]{2,1,0:T(8,128)S(1)}, f32[27,128,128]{2,1,0:T(8,128)}, u32[]{:S(2)}) copy-start(f32[27,128,128]{2,1,0:T(8,128)} %get-tuple-element.65) | copy-start | bytes 5308420
Sparse Core Ops, SparseCore 0:
  138.9 140.6 all-reduce.2

commit v2 on v1

v2 whole, which is shorter than its diff:
```python
import functools

import jax
import jax.numpy as jnp
from jax import lax
from jax.experimental import pallas as pl
from jax.experimental.pallas import tpu as pltpu
from jax.sharding import PartitionSpec as P

EPSILON = 1e-05
F32 = jnp.float32
BF16 = jnp.bfloat16
VMEM_BYTES = 48 << 20


def mm(left, right):
    return jnp.dot(left, right, preferred_element_type=F32)


def mm_t(left, right):
    return lax.dot_general(left, right, (((1,), (1,)), ((), ())), preferred_element_type=F32)


def hits(index_row, rows):
    places = lax.broadcasted_iota(jnp.int16, (rows, index_row.shape[1]), 0)
    return jnp.where(places == index_row, jnp.bfloat16(1), jnp.bfloat16(0))


def near_row(where_ref, near_ref, offset):
    return near_ref[offset, pl.ds(where_ref[0] + pl.program_id(0), 1), :]


def near_hits(where_ref, near_ref, offset):
    row = near_row(where_ref, near_ref, offset)
    return hits(row.astype(jnp.int16), row.shape[1])


def live_mask(where_ref, near_ref, channels):
    rows = near_ref.shape[2]
    centre = near_row(where_ref, near_ref, 13)
    count = jnp.sum((centre < rows).astype(F32), axis=1, keepdims=True)
    places = lax.broadcasted_iota(jnp.int32, (rows, channels), 0).astype(F32)
    return (places < count).astype(F32), count


def tree_sum(parts):
    parts = list(parts)
    while len(parts) > 1:
        parts = [parts[i] + parts[i + 1] for i in range(0, len(parts), 2)]
    return parts[0]


def moments(totals):
    count = totals[2:3]
    mean_row = totals[0:1] / count
    inv_std = lax.rsqrt(totals[1:2] / count - mean_row * mean_row + EPSILON)
    return mean_row, inv_std, count


def sigmoid(values):
    return 1.0 / (1.0 + jnp.exp(-values))


def put_sums(out_ref, first, second, count):
    channels = first.shape[1]
    third = jnp.broadcast_to(count, (1, channels))
    out_ref[0] = jnp.concatenate(
        [first, second, third, jnp.zeros((5, channels), F32)], axis=0
    )


def col_sum(values):
    return jnp.sum(values, axis=0, keepdims=True)


def parent_rows(down_ref, fine_rows):
    table = down_ref[0]
    first = jnp.min(table, axis=0, keepdims=True)
    children = jnp.sum((table < fine_rows).astype(jnp.int32), axis=0, keepdims=True)
    return table, first, first + children


def parent_hits(first, last, fine_rows, at, size):
    places = lax.broadcasted_iota(jnp.int16, (size, first.shape[1]), 0) + jnp.int16(at)
    inside = (places >= first.astype(jnp.int16)) & (places < last.astype(jnp.int16))
    return jnp.where(inside, jnp.bfloat16(1), jnp.bfloat16(0))


def down_kernel(where_ref, feats_ref, down_ref, near_ref, weight_ref, hidden_ref, sums_ref, kids_ref, which_ref, spread_ref, parent_ref):
    in_channels, fine_rows = feats_ref.shape[1], feats_ref.shape[2]
    offsets, coarse_rows = down_ref.shape[1], down_ref.shape[2]
    channels = weight_ref.shape[1]
    table, first, last = parent_rows(down_ref, fine_rows)
    rank = table - first
    numbers = lax.broadcasted_iota(jnp.int32, (offsets, coarse_rows), 0) + 1
    rows = [
        jnp.sum(jnp.where(rank == r, numbers, 0), axis=0, keepdims=True) for r in range(8)
    ]
    safe_first = jnp.where(first < fine_rows, first, 0)
    rows += [(safe_first // 16) * 16, safe_first % 16] + [jnp.zeros_like(first)] * 6
    lookup = jnp.concatenate(rows, axis=0).astype(F32).astype(BF16)
    step = 512
    for at in range(0, fine_rows, step):
        parent_ref[at : at + step] = parent_hits(first, last, fine_rows, at, step)
    found = mm_t(lookup, parent_ref[...])
    place = lax.broadcasted_iota(jnp.int32, (8, fine_rows), 1).astype(F32) - (found[8:9] + found[9:10])
    column = lax.broadcasted_iota(jnp.int32, (8, fine_rows), 0).astype(F32)
    which = jnp.sum(jnp.where(column == place, found[:8], 0.0), axis=0, keepdims=True)
    which_ref[0] = jnp.broadcast_to(which, (8, fine_rows))
    code = jnp.broadcast_to(which, (in_channels, fine_rows)).astype(BF16)
    feats = feats_ref[0]
    for k in range(offsets):
        spread_ref[in_channels * k : in_channels * (k + 1)] = jnp.where(
            code == jnp.bfloat16(k + 1), feats, jnp.zeros_like(feats)
        )
    kids = mm(spread_ref[...], parent_ref[...]).astype(BF16)
    kids_ref[0] = kids
    hidden = jnp.transpose(mm(jnp.transpose(weight_ref[...]), kids))
    hidden_ref[0] = hidden
    _, count = live_mask(where_ref, near_ref, channels)
    put_sums(sums_ref, col_sum(hidden), col_sum(hidden * hidden), count)


def conv_all(where_ref, source, near_ref, weight_ref):
    out = mm(source, weight_ref[13])
    for j in range(0, 13):
        rows = [
            mm(near_hits(where_ref, near_ref, 26 - k), source).astype(BF16) for k in (j, 26 - j)
        ]
        weight = jnp.concatenate([weight_ref[j], weight_ref[26 - j]], axis=0)
        out = out + mm(jnp.concatenate(rows, axis=1), weight)
    return out


def forward_kernel(norm_at, rounded, where_ref, hidden_ref, near_ref, weight_ref, scale_ref, shift_ref, *refs):
    part_refs, (act_ref, next_ref, sums_ref) = refs[:-3], refs[-3:]
    mean_row, inv_std, _ = moments(tree_sum([ref[0] for ref in part_refs]))
    live, count = live_mask(where_ref, near_ref, hidden_ref.shape[2])
    value = (hidden_ref[0] - mean_row) * inv_std * scale_ref[norm_at : norm_at + 1] + shift_ref[norm_at : norm_at + 1]
    act = (live * (value * sigmoid(value))).astype(BF16)
    act_ref[0] = act
    hidden = conv_all(where_ref, act, near_ref, weight_ref)
    if rounded:
        hidden = hidden.astype(BF16)
    next_ref[0] = hidden
    hidden = hidden.astype(F32)
    put_sums(sums_ref, col_sum(hidden), col_sum(hidden * hidden), count)


def output_kernel(where_ref, hidden_ref, act_ref, grad_ref, near_ref, scale_ref, shift_ref, *refs):
    part_refs, (features_ref, slope_ref, sums_ref) = refs[:-3], refs[-3:]
    mean_row, inv_std, _ = moments(tree_sum([ref[0] for ref in part_refs]))
    live, count = live_mask(where_ref, near_ref, hidden_ref.shape[2])
    centred = (hidden_ref[0].astype(F32) - mean_row) * inv_std
    value = centred * scale_ref[2:3] + shift_ref[2:3] + act_ref[0].astype(F32)
    gate = sigmoid(value)
    features_ref[0] = (live * (value * gate)).astype(BF16)
    upstream = grad_ref[0].astype(F32) * live * (gate * (1.0 + value * (1.0 - gate)))
    slope_ref[0] = upstream
    put_sums(sums_ref, col_sum(upstream), col_sum(upstream * centred), count)


def norm_back(upstream, centred, live, inv_std, gain_row, back, count):
    return live * (inv_std * gain_row) * (upstream - back[0:1] / count - centred * (back[1:2] / count))


def backward_kernel(norm_at, with_skip, ways, where_ref, *refs):
    upstream_ref, hidden_ref, lower_ref, act_ref, near_ref, weight_ref, scale_ref, shift_ref = refs[:8]
    own_refs = refs[8 : 8 + ways]
    back_refs = refs[8 + ways : 8 + 2 * ways]
    below_refs = refs[8 + 2 * ways : 8 + 3 * ways]
    rest = refs[8 + 3 * ways :]
    skip_ref = rest[0] if with_skip else None
    next_ref, sums_ref, keep_ref, send_ref, grad_ref = rest[-5:]
    mean_row, inv_std, count = moments(tree_sum([ref[0] for ref in own_refs]))
    back = tree_sum([ref[0] for ref in back_refs])
    live, own_count = live_mask(where_ref, near_ref, hidden_ref.shape[2])
    centred = (hidden_ref[0].astype(F32) - mean_row) * inv_std
    rows_grad = norm_back(
        upstream_ref[0], centred, live, inv_std, scale_ref[norm_at : norm_at + 1], back, count
    ).astype(BF16)

    @pl.when(pl.program_id(0) == 0)
    def _():
        grad_ref[...] = jnp.zeros_like(grad_ref)

    channels = hidden_ref.shape[2]
    act_t = jnp.transpose(act_ref[0])
    below = mm_t(rows_grad, weight_ref[13])
    grad_ref[13 * channels : 14 * channels] += mm(act_t, rows_grad)
    for j in range(13):
        moved = jnp.concatenate(
            [mm(near_hits(where_ref, near_ref, k), rows_grad).astype(BF16) for k in (j, 26 - j)], axis=1
        )
        weight = jnp.concatenate([weight_ref[j], weight_ref[26 - j]], axis=1)
        below = below + mm_t(moved, weight)
        pair = mm(act_t, moved)
        grad_ref[j * channels : (j + 1) * channels] += pair[:, :channels]
        grad_ref[(26 - j) * channels : (27 - j) * channels] += pair[:, channels:]
    below = below.astype(BF16).astype(F32)
    if with_skip:
        below = below + skip_ref[0].astype(BF16).astype(F32)
    low_mean, low_std, _ = moments(tree_sum([ref[0] for ref in below_refs]))
    low_centred = (lower_ref[0] - low_mean) * low_std
    value = low_centred * scale_ref[norm_at - 1 : norm_at] + shift_ref[norm_at - 1 : norm_at]
    gate = sigmoid(value)
    upstream = below * live * (gate * (1.0 + value * (1.0 - gate)))
    next_ref[0] = upstream
    put_sums(sums_ref, col_sum(upstream), col_sum(upstream * low_centred), own_count)
    put_halves(where_ref, grad_ref, keep_ref, send_ref)


def put_halves(where_ref, grad_ref, keep_ref, send_ref):
    half = keep_ref.shape[0]
    core = where_ref[1]

    @pl.when(pl.program_id(0) == pl.num_programs(0) - 1)
    def _():
        keep_ref[...] = grad_ref[pl.ds(pl.multiple_of(core * half, 16), half)].astype(BF16)
        send_ref[...] = grad_ref[pl.ds(pl.multiple_of((1 - core) * half, 16), half)].astype(BF16)


def last_kernel(ways, where_ref, upstream_ref, hidden_ref, kids_ref, near_ref, scale_ref, *refs):
    own_refs, back_refs = refs[:ways], refs[ways : 2 * ways]
    rows_ref, keep_ref, send_ref, grad_ref = refs[2 * ways :]
    mean_row, inv_std, count = moments(tree_sum([ref[0] for ref in own_refs]))
    back = tree_sum([ref[0] for ref in back_refs])
    live, _ = live_mask(where_ref, near_ref, hidden_ref.shape[2])
    centred = (hidden_ref[0] - mean_row) * inv_std
    rows_grad = norm_back(
        upstream_ref[0], centred, live, inv_std, scale_ref[0:1], back, count
    ).astype(BF16)

    @pl.when(pl.program_id(0) == 0)
    def _():
        grad_ref[...] = jnp.zeros_like(grad_ref)

    rows_ref[0] = rows_grad
    grad_ref[: kids_ref.shape[1]] += mm(kids_ref[0], rows_grad)
    put_halves(where_ref, grad_ref, keep_ref, send_ref)


def input_kernel(where_ref, rows_ref, which_ref, down_ref, weight_ref, input_ref):
    pieces = mm_t(weight_ref[...], rows_ref[0]).astype(BF16)
    in_channels, fine_rows = input_ref.shape[1], input_ref.shape[2]
    _, first, last = parent_rows(down_ref, fine_rows)
    step = 256
    for at in range(0, fine_rows, step):
        full = mm_t(pieces, parent_hits(first, last, fine_rows, at, step))
        code = jnp.broadcast_to(which_ref[0, 0:1, at : at + step], (in_channels, step))
        out = jnp.zeros((in_channels, step), F32)
        for k in range(full.shape[0] // in_channels):
            out = out + jnp.where(code == float(k + 1), full[in_channels * k : in_channels * (k + 1)], 0.0)
        input_ref[0, :, at : at + step] = out.astype(BF16)


def as_f32(ref):
    return ref[...].astype(F32)


def split_kernel(sections, depths, parts, where_ref, *refs):
    pairs, outs = refs[: 2 * len(parts)], refs[2 * len(parts) :]
    section = where_ref[2]
    total = sum(parts)
    for j in range(sections):
        block = section ^ j
        base = 0
        for i, size in enumerate(parts):
            wide = depths * size
            rows = pl.ds(pl.multiple_of(block * wide, 16), wide)
            both = (pairs[2 * i][rows].astype(F32) + pairs[2 * i + 1][rows].astype(F32)).astype(BF16)
            for z in range(depths):
                outs[j][z * total + base : z * total + base + size] = both[z * size : (z + 1) * size]
            base += size


def spread_kernel(count, at, where_ref, *refs):
    sources, outs = refs[:-count], refs[-count:]
    place = where_ref[at]
    size = outs[0].shape[0]
    for j in range(count):
        rows = pl.ds(pl.multiple_of((place ^ j) * size, 16), size)
        outs[j][...] = tree_sum([ref[rows].astype(F32) for ref in sources]).astype(BF16)


def add_kernel(where_ref, *refs):
    refs[-1][...] = tree_sum([as_f32(ref) for ref in refs[:-1]]).astype(BF16)


def join_kernel(ways, where_ref, *refs):
    pieces, sums_refs, out_ref = refs[: -3 * ways - 1], refs[-3 * ways - 1 : -1], refs[-1]
    size = pieces[0].shape[0]
    for j, ref in enumerate(pieces):
        out_ref[pl.ds(pl.multiple_of((where_ref[3] ^ j) * size, 16), size)] = ref[...]
    rows = []
    for t in range(3):
        totals = tree_sum([ref[...] for ref in sums_refs[t * ways : (t + 1) * ways]])
        rows.append(jnp.sum(totals, axis=0)[0:2])
    exact = jnp.concatenate(rows + [jnp.zeros((2, rows[0].shape[1]), F32)], axis=0)
    high = exact.astype(BF16)
    low = (exact - high.astype(F32)).astype(BF16)
    out_ref[len(pieces) * size :] = jnp.concatenate([high, low], axis=0)


def gather_kernel(where_ref, *refs):
    pieces, (out_ref, sums_ref) = refs[:-2], refs[-2:]
    size = pieces[0].shape[0] - 16
    for j, ref in enumerate(pieces):
        out_ref[pl.ds(pl.multiple_of((where_ref[2] ^ j) * size, 16), size)] = ref[:size]
    tails = [ref[size:].astype(F32) for ref in pieces]
    sums_ref[...] = tree_sum([tail[:8] + tail[8:] for tail in tails])


def final_kernel(parts, where_ref, own_ref, other_ref, *outs):
    first_core = where_ref[1] == 0
    total = sum(parts)
    half = own_ref.shape[0]
    blocks = half // total
    for core in range(2):
        base = 0
        for size, out in zip(parts, outs):
            for t in range(blocks):
                start = (core * blocks + t) * size
                count = min(size, out.shape[0] - start)
                if count > 0:
                    rows = slice(t * total + base, t * total + base + count)
                    mine, theirs = own_ref[rows], other_ref[rows]
                    pick = first_core if core == 0 else jnp.logical_not(first_core)
                    out[start : start + count] = jnp.where(pick, mine, theirs).astype(F32)
            base += size


def whole(array):
    return pl.BlockSpec(array.shape, lambda b, where: (0,) * array.ndim)


def per_micro(array, picked):
    block = (1,) + array.shape[1:]
    rest = (0,) * (array.ndim - 1)
    if picked:
        return pl.BlockSpec(block, lambda b, where: (where[0] + b,) + rest)
    return pl.BlockSpec(block, lambda b, where: (b,) + rest)


def call(kernel, steps, where, operands, kinds, outs, out_kinds, scratch=()):
    def spec(array, kind):
        if kind == "all":
            return whole(array)
        return per_micro(array, kind == "pick")

    return pl.pallas_call(
        kernel,
        grid_spec=pltpu.PrefetchScalarGridSpec(
            num_scalar_prefetch=1,
            grid=(steps,),
            in_specs=[spec(a, k) for a, k in zip(operands, kinds)],
            out_specs=[spec(a, k) for a, k in zip(outs, out_kinds)],
            scratch_shapes=list(scratch),
        ),
        out_shape=outs,
        compiler_params=pltpu.CompilerParams(
            vmem_limit_bytes=VMEM_BYTES, dimension_semantics=("arbitrary",)
        ),
    )(where, *operands)


def simple(kernel, where, operands, outs, cost=None):
    return pl.pallas_call(
        kernel,
        in_specs=[pl.BlockSpec(memory_space=pltpu.SMEM)] + [pl.BlockSpec(memory_space=pltpu.VMEM)] * len(operands),
        out_specs=[pl.BlockSpec(memory_space=pltpu.VMEM)] * len(outs),
        out_shape=outs,
        compiler_params=pltpu.CompilerParams(vmem_limit_bytes=VMEM_BYTES),
    )(where, *operands)


def swapped(value, axis, step):
    count = lax.axis_size(axis)
    return lax.ppermute(value, axis, [(i, i ^ step) for i in range(count)])


def bucket_sums(value, axis):
    count = lax.axis_size(axis)
    value = value + lax.ppermute(value, axis, [(i, i ^ 1) for i in range(count)])
    return [value] + [
        lax.ppermute(value, axis, [(i, i ^ step) for i in range(count)])
        for step in range(2, count, 2)
    ]


def local(
    voxel_feats, down_map, neighbours, w_down, w_first, w_second, bn_scale, bn_shift, out_grad
):
    sections = lax.axis_size("section")
    mine = voxel_feats.shape[0] // sections
    voxel_feats = jnp.swapaxes(voxel_feats, 1, 2)
    neighbours = jnp.swapaxes(neighbours, 0, 1)
    section, bucket = lax.axis_index("section"), lax.axis_index("dp")
    depths = lax.axis_size("dp") // 2
    where = jnp.stack([section * mine, bucket % 2, section, bucket // 2]).astype(jnp.int32)
    in_channels, fine_rows = voxel_feats.shape[1:]
    coarse_rows = neighbours.shape[2]
    channels = w_first.shape[2]
    offsets = down_map.shape[1]
    wide = offsets * in_channels
    flat_down = w_down.reshape(wide, channels)
    shape = jax.ShapeDtypeStruct
    rows_f32 = shape((mine, coarse_rows, channels), F32)
    rows_bf16 = shape((mine, coarse_rows, channels), BF16)
    sums = shape((mine, 8, channels), F32)

    hidden_zero, part_zero, kids, which = call(
        down_kernel, mine, where,
        [voxel_feats, down_map, neighbours, flat_down],
        ["pick", "pick", "all", "all"],
        [rows_f32, sums, shape((mine, wide, coarse_rows), BF16), shape((mine, 8, fine_rows), F32)],
        ["own"] * 4,
        [pltpu.VMEM((wide, fine_rows), BF16), pltpu.VMEM((fine_rows, coarse_rows), BF16)],
    )
    stats_zero = bucket_sums(part_zero, "dp")
    ways = len(stats_zero)
    act_zero, hidden_one, part_one = call(
        functools.partial(forward_kernel, 0, False), mine, where,
        [hidden_zero, neighbours, w_first, bn_scale, bn_shift] + stats_zero,
        ["own", "all", "all", "all", "all"] + ["own"] * ways,
        [rows_bf16, rows_f32, sums], ["own"] * 3,
    )
    stats_one = bucket_sums(part_one, "dp")
    act_one, hidden_two, part_two = call(
        functools.partial(forward_kernel, 1, True), mine, where,
        [hidden_one, neighbours, w_second, bn_scale, bn_shift] + stats_one,
        ["own", "all", "all", "all", "all"] + ["own"] * ways,
        [rows_bf16, rows_bf16, sums], ["own"] * 3,
    )
    stats_two = bucket_sums(part_two, "dp")
    features, up_two, back_part = call(
        output_kernel, mine, where,
        [hidden_two, act_zero, out_grad, neighbours, bn_scale, bn_shift] + stats_two,
        ["own", "own", "pick", "all", "all", "all"] + ["own"] * ways,
        [rows_bf16, rows_f32, sums], ["own"] * 3,
    )
    back_two = bucket_sums(back_part, "dp")

    def part_rows(rows):
        return -(-rows // (2 * sections * depths * 16)) * 16

    conv_rows = w_first.shape[0] * channels
    parts = [part_rows(conv_rows), part_rows(conv_rows), part_rows(wide)]

    def halves(size):
        return shape((sections * depths * size, channels), BF16)

    def accumulator(size):
        return [pltpu.VMEM((2 * sections * depths * size, channels), F32)]

    up_one, back_part, keep_second, send_second = call(
        functools.partial(backward_kernel, 2, False, ways), mine, where,
        [up_two, hidden_two, hidden_one, act_one, neighbours, w_second, bn_scale, bn_shift]
        + stats_two + back_two + stats_one,
        ["own"] * 4 + ["all"] * 4 + ["own"] * (3 * ways),
        [rows_f32, sums, halves(parts[0]), halves(parts[0])], ["own", "own", "all", "all"],
        accumulator(parts[0]),
    )
    back_one = bucket_sums(back_part, "dp")
    got_second = swapped(send_second, "dp", 1)
    up_zero, back_part, keep_first, send_first = call(
        functools.partial(backward_kernel, 1, True, ways), mine, where,
        [up_one, hidden_one, hidden_zero, act_zero, neighbours, w_first, bn_scale, bn_shift]
        + stats_one + back_one + stats_zero + [up_two],
        ["own"] * 4 + ["all"] * 4 + ["own"] * (3 * ways + 1),
        [rows_f32, sums, halves(parts[1]), halves(parts[1])], ["own", "own", "all", "all"],
        accumulator(parts[1]),
    )
    back_zero = bucket_sums(back_part, "dp")
    got_first = swapped(send_first, "dp", 1)
    rows_zero, keep_down, send_down = call(
        functools.partial(last_kernel, ways), mine, where,
        [up_zero, hidden_zero, kids, neighbours, bn_scale] + stats_zero + back_zero,
        ["own"] * 3 + ["all"] * 2 + ["own"] * (2 * ways),
        [rows_bf16, halves(parts[2]), halves(parts[2])], ["own", "all", "all"],
        accumulator(parts[2]),
    )
    got_down = swapped(send_down, "dp", 1)
    total = sum(parts)
    sections_out = simple(
        functools.partial(split_kernel, sections, depths, parts), where,
        [keep_second, got_second, keep_first, got_first, keep_down, got_down],
        [shape((depths * total, channels), BF16)] * sections,
    )
    arrived = [sections_out[0]] + [swapped(sections_out[j], "section", j) for j in range(1, sections)]
    (input_grad,) = call(
        input_kernel, mine, where,
        [rows_zero, which, down_map, flat_down],
        ["own", "own", "pick", "all"],
        [shape((mine, in_channels, fine_rows), BF16)], ["own"],
    )
    depth_out = simple(
        functools.partial(spread_kernel, depths, 3), where, arrived,
        [shape((total, channels), BF16)] * depths,
    )
    arrived = [depth_out[0]] + [swapped(depth_out[j], "dp", 2 * j) for j in range(1, depths)]
    (summed,) = simple(add_kernel, where, arrived, [shape((total, channels), BF16)])
    arrived = [summed] + [swapped(summed, "dp", 2 * j) for j in range(1, depths)]
    (joined,) = simple(
        functools.partial(join_kernel, ways), where, arrived + back_zero + back_one + back_two,
        [shape((depths * total + 16, channels), BF16)],
    )
    arrived = [joined] + [swapped(joined, "section", j) for j in range(1, sections)]
    half, norm_sums = simple(
        gather_kernel, where, arrived,
        [shape((sections * depths * total, channels), BF16), shape((8, channels), F32)],
    )
    other = swapped(half, "dp", 1)
    grad_second, grad_first, grad_down = simple(
        functools.partial(final_kernel, parts), where, [half, other],
        [shape((conv_rows, channels), F32), shape((conv_rows, channels), F32), shape((wide, channels), F32)],
    )
    return (
        features,
        jnp.swapaxes(input_grad, 1, 2),
        grad_down.reshape(w_down.shape),
        grad_first.reshape(w_first.shape),
        grad_second.reshape(w_second.shape),
        norm_sums[1:6:2],
        norm_sums[0:6:2],
    )


def solution(mesh):
    in_specs = (
        P(None, "dp", None),
        P(None, None, "dp"),
        P(None, None, "dp"),
        P(),
        P(),
        P(),
        P(),
        P(),
        P(None, "dp", None),
    )
    out_specs = (P("section", "dp", None), P("section", "dp", None), P(), P(), P(), P(), P())
    return jax.shard_map(local, mesh=mesh, in_specs=in_specs, out_specs=out_specs, check_vma=False)
```

time: 295 us -> 174 us (0.59)
  waiting for transfers between devices: 148 us -> 45.5 us
  starting transfers between devices: 31.2 us -> 54.5 us
  between operations: 14.2 us -> 0.85 us
  Pallas kernels: 77.5 us -> 67.2 us
  local copies, waits for them, and re-layouts: 13.7 us -> 5.63 us
  blocking collectives: 8 us -> 0 us
    psum x1 -> x0, waiting for transfers between devices: 131 us -> none  [local(): lax.psum((grad_down, grad_first, grad_second), ('section', 'dp'))]
    ppermute x0 -> x16, waiting for transfers between devices: none -> 25.4 us  [swapped(): return lax.ppermute(value, axis, [(i, i ^ step) for i in range(count)])]
    ppermute x0 -> x16, starting transfers between devices: none -> 23.8 us  [swapped(): return lax.ppermute(value, axis, [(i, i ^ step) for i in range(count)])]
    pallas_call x7 -> x8, Pallas kernels: 77.5 us -> 61.1 us  [call(): pl.pallas_call(kernel, grid_spec=pltpu.PrefetchScalarGridSpec(num_scalar_...]
    unnamed x22 -> x24, local copies, waits for them, and re-layouts: 13.1 us -> 4.45 us
    psum x1 -> x0, blocking collectives: 8 us -> none  [local(): norm_sums = lax.psum(norm_sums, 'section')]
    pallas_call x0 -> x6, Pallas kernels: none -> 6.05 us  [simple(): pl.pallas_call(kernel, in_specs=[pl.BlockSpec(memory_space=pltpu.SMEM)] +...]
    ppermute x18, waiting for transfers between devices: 11.4 us -> 14.3 us  [bucket_sums(): lax.ppermute(value, axis, [(i, i ^ step) for i in range(count)])]
  transfers between devices with their start and end apart: 25 -> 40, of which waited for: 22 -> 26; matrix products, arithmetic and copies ran while one was open for 1% -> 1% of each run, Pallas kernels for 0% -> 11%
where the time goes in v2:
time: 174 us
  Pallas kernels  67.2 us (39%)
  starting transfers between devices  54.5 us (31%)
  waiting for transfers between devices  45.5 us (26%)
  local copies, waits for them, and re-layouts  5.63 us (3%)
    pallas_call x8, Pallas kernels, call(): pl.pallas_call(kernel, grid_spec=pltpu.PrefetchScalarGridSpec(num_scalar_...  61.1 us
    ppermute x16, waiting for transfers between devices, swapped(): return lax.ppermute(value, axis, [(i, i ^ step) for i in range(count)])  25.4 us
    ppermute x16, starting transfers between devices, swapped(): return lax.ppermute(value, axis, [(i, i ^ step) for i in range(count)])  23.8 us
    ppermute x18, starting transfers between devices, bucket_sums(): lax.ppermute(value, axis, [(i, i ^ step) for i in range(count)])  22.7 us
    ppermute x18, waiting for transfers between devices, bucket_sums(): lax.ppermute(value, axis, [(i, i ^ step) for i in range(count)])  14.3 us
    ppermute x6, starting transfers between devices, bucket_sums(): lax.ppermute(value, axis, [(i, i ^ 1) for i in range(count)])  8.04 us
    pallas_call x6, Pallas kernels, simple(): pl.pallas_call(kernel, in_specs=[pl.BlockSpec(memory_space=pltpu.SMEM)] +...  6.05 us
    ppermute x6, waiting for transfers between devices, bucket_sums(): lax.ppermute(value, axis, [(i, i ^ 1) for i in range(count)])  5.81 us
  transfers between devices with their start and end apart: 40, of which 26 were waited for; matrix products, arithmetic and copies ran while one was open for 1% of the time, Pallas kernels for 11%

profile of v2, /device:TPU:1, one launch (start us, length us, event | category | flops | bytes accessed | tf_op | source)
XLA Modules:
  0.0 173.8 jit_solution(12403914464876671739)
XLA Ops:
  1.8 1.6 copy-done.4
  5.2 4.8 %shard_map.144 = (f32[2,512,128]{2,1,0:T(8,128)S(1)}, f32[2,8,128]{2,1,0:T(8,128)S(1)}, bf16[2,512,512]{2,1,0:T(8,128)(2,1)S(1)}, f32[2,8,2048]{2,1,0:T(8,128)S(1)}) custom-call(s32[4]{0:T(128)S(1)} %pad_add_fusion.where_ref, bf16[8,64,2048]{2,1,0:T(8,128)(2,1)S(1)} %bitcast.18, s32[8,8,512]{2,1,0:T(8,128)S(1)} %copy-done.6, s32[27,8,512]{2,1,0:T(8,128)S(1)} %bitcast.11, ...), custom_call_target="tpu_custom_call" | custom-call | tf_op jit(solution)/shard_map/pallas_call | solution.py:351
  10.1 1.1 collective-permute-done
  11.3 2.4 %collective-permute-start.1 = (f32[2,8,128]{2,1,0:T(8,128)S(1)}, f32[2,8,128]{2,1,0:T(8,128)S(1)}, u32[]{:S(2)}, u32[]{:S(2)}) collective-permute-start(f32[2,8,128]{2,1,0:T(8,128)S(1)} %add.24.refs_0_.refs_16_), channel_id=1, source_target_pairs={{0,2},{1,3},{2,0},{3,1},{4,6},{5,7},{6,4},{7,5},{8,10},{9,11},{10,... | collective-permute-start | bytes 24584 | tf_op jit(solution)/shard_map/ppermute | solution.py:386
  13.7 2.3 %collective-permute-start.2 = (f32[2,8,128]{2,1,0:T(8,128)S(1)}, f32[2,8,128]{2,1,0:T(8,128)S(1)}, u32[]{:S(2)}, u32[]{:S(2)}) collective-permute-start(f32[2,8,128]{2,1,0:T(8,128)S(1)} %add.24.refs_0_.refs_16_), channel_id=1, source_target_pairs={{0,4},{1,5},{2,6},{3,7},{4,0},{5,1},{6,2},{7,3},{8,12},{9,13},{10,... | collective-permute-start | bytes 24584 | tf_op jit(solution)/shard_map/ppermute | solution.py:386
  17.1 3.2 %collective-permute-done.3.refs_3_.refs_19_ = f32[2,8,128]{2,1,0:T(8,128)S(1)} collective-permute-done((f32[2,8,128]{2,1,0:T(8,128)S(1)}, f32[2,8,128]{2,1,0:T(8,128)S(1)}, u32[]{:S(2)}, u32[]{:S(2)}) %collective-permute-start.3) | collective-permute-done | bytes 8224 | tf_op jit(solution)/shard_map/ppermute | solution.py:386
  20.4 10.4 %shard_map.145 = (bf16[2,512,128]{2,1,0:T(8,128)(2,1)S(1)}, f32[2,512,128]{2,1,0:T(8,128)S(1)}, f32[2,8,128]{2,1,0:T(8,128)S(1)}) custom-call(s32[4]{0:T(128)S(1)} %pad_add_fusion.where_ref, f32[2,512,128]{2,1,0:T(8,128)S(1)} %get-tuple-element.44.hidden_ref.refs_2_, s32[27,8,512]{2,1,0:T(8,128)S(1)} %bitcast.12, bf16[27,128,128]{2,1,0:T(8,128)(2,1)S(1)} %copy-done.3, ...), custom_call_target="tpu_custom_call" | custom-call | tf_op jit(solution)/shard_map/pallas_call | solution.py:351
  30.8 2.1 %collective-permute-start.4 = (f32[2,8,128]{2,1,0:T(8,128)S(1)}, f32[2,8,128]{2,1,0:T(8,128)S(1)}, u32[]{:S(2)}, u32[]{:S(2)}) collective-permute-start(f32[2,8,128]{2,1,0:T(8,128)S(1)} %get-tuple-element.47), channel_id=1, source_target_pairs={{0,1},{1,0},{2,3},{3,2},{4,5},{5,4},{6,7},{7,6},{8,9},{9,8},{10,11... | collective-permute-start | bytes 24584 | tf_op jit(solution)/shard_map/ppermute | solution.py:384
  33.8 3.5 %collective-permute-start.7 = (f32[2,8,128]{2,1,0:T(8,128)S(1)}, f32[2,8,128]{2,1,0:T(8,128)S(1)}, u32[]{:S(2)}, u32[]{:S(2)}) collective-permute-start(f32[2,8,128]{2,1,0:T(8,128)S(1)} %add.25.refs_0_.refs_16_.refs_8_), channel_id=1, source_target_pairs={{0,6},{1,7},{2,4},{3,5},{4,2},{5,3},{6,0},{7,1},{8,14},{9,15},{10,... | collective-permute-start | bytes 24584 | tf_op jit(solution)/shard_map/ppermute | solution.py:386
  38.4 10.4 %shard_map.146 = (bf16[2,512,128]{2,1,0:T(8,128)(2,1)S(1)}, bf16[2,512,128]{2,1,0:T(8,128)(2,1)S(1)}, f32[2,8,128]{2,1,0:T(8,128)S(1)}) custom-call(s32[4]{0:T(128)S(1)} %pad_add_fusion.where_ref, f32[2,512,128]{2,1,0:T(8,128)S(1)} %get-tuple-element.46.hidden_ref.refs_2_.refs_1_, s32[27,8,512]{2,1,0:T(8,128)S(1)} %bitcast.13, ...), custom_call_target="tpu_custom_call" | custom-call | tf_op jit(solution)/shard_map/pallas_call | solution.py:351
  48.8 1.8 %collective-permute-start.8 = (f32[2,8,128]{2,1,0:T(8,128)S(1)}, f32[2,8,128]{2,1,0:T(8,128)S(1)}, u32[]{:S(2)}, u32[]{:S(2)}) collective-permute-start(f32[2,8,128]{2,1,0:T(8,128)S(1)} %get-tuple-element.50), channel_id=1, source_target_pairs={{0,1},{1,0},{2,3},{3,2},{4,5},{5,4},{6,7},{7,6},{8,9},{9,8},{10,11... | collective-permute-start | bytes 24584 | tf_op jit(solution)/shard_map/ppermute | solution.py:384
  51.7 3.3 %collective-permute-start.11 = (f32[2,8,128]{2,1,0:T(8,128)S(1)}, f32[2,8,128]{2,1,0:T(8,128)S(1)}, u32[]{:S(2)}, u32[]{:S(2)}) collective-permute-start(f32[2,8,128]{2,1,0:T(8,128)S(1)} %add.26.refs_0_.refs_8_), channel_id=1, source_target_pairs={{0,6},{1,7},{2,4},{3,5},{4,2},{5,3},{6,0},{7,1},{8,14},{9,15},{10,... | collective-permute-start | bytes 24584 | tf_op jit(solution)/shard_map/ppermute | solution.py:386
  56.1 1.4 collective-permute-done.9.refs_1_.refs_9_
  57.5 1.8 %shard_map.147 = (bf16[2,512,128]{2,1,0:T(8,128)(2,1)}, f32[2,512,128]{2,1,0:T(8,128)S(1)}, f32[2,8,128]{2,1,0:T(8,128)S(1)}) custom-call(s32[4]{0:T(128)S(1)} %pad_add_fusion.where_ref, bf16[2,512,128]{2,1,0:T(8,128)(2,1)S(1)} %get-tuple-element.48.hidden_ref.refs_1_, bf16[2,512,128]{2,1,0:T(8,128)(2,1)S(1)} %get-tuple-element.49.act_ref.refs_3_, ...), custom_call_target="tpu_custom_call" | custom-call | tf_op jit(solution)/shard_map/pallas_call | solution.py:351
  59.3 1.8 %collective-permute-start.12 = (f32[2,8,128]{2,1,0:T(8,128)S(1)}, f32[2,8,128]{2,1,0:T(8,128)S(1)}, u32[]{:S(2)}, u32[]{:S(2)}) collective-permute-start(f32[2,8,128]{2,1,0:T(8,128)S(1)} %get-tuple-element.54), channel_id=1, source_target_pairs={{0,1},{1,0},{2,3},{3,2},{4,5},{5,4},{6,7},{7,6},{8,9},{9,8},{10,11... | collective-permute-start | bytes 24584 | tf_op jit(solution)/shard_map/ppermute | solution.py:384
  62.2 1.5 collective-permute-start.14
  63.7 1.7 %collective-permute-start.15 = (f32[2,8,128]{2,1,0:T(8,128)S(1)}, f32[2,8,128]{2,1,0:T(8,128)S(1)}, u32[]{:S(2)}, u32[]{:S(2)}) collective-permute-start(f32[2,8,128]{2,1,0:T(8,128)S(1)} %add.27.refs_12_), channel_id=1, source_target_pairs={{0,6},{1,7},{2,4},{3,5},{4,2},{5,3},{6,0},{7,1},{8,14},{9,15},{10,... | collective-permute-start | bytes 24584 | tf_op jit(solution)/shard_map/ppermute | solution.py:386
  65.6 2.4 %collective-permute-done.15.refs_15_ = f32[2,8,128]{2,1,0:T(8,128)S(1)} collective-permute-done((f32[2,8,128]{2,1,0:T(8,128)S(1)}, f32[2,8,128]{2,1,0:T(8,128)S(1)}, u32[]{:S(2)}, u32[]{:S(2)}) %collective-permute-start.15) | collective-permute-done | bytes 8224 | tf_op jit(solution)/shard_map/ppermute | solution.py:386
  68.0 13.9 %shard_map.148 = (f32[2,512,128]{2,1,0:T(8,128)S(1)}, f32[2,8,128]{2,1,0:T(8,128)S(1)}, bf16[1792,128]{1,0:T(8,128)(2,1)S(1)}, bf16[1792,128]{1,0:T(8,128)(2,1)S(1)}) custom-call(s32[4]{0:T(128)S(1)} %pad_add_fusion.where_ref, f32[2,512,128]{2,1,0:T(8,128)S(1)} %get-tuple-element.52.refs_0_.refs_20_, ...), custom_call_target="tpu_custom_call" | custom-call | tf_op jit(solution)/shard_map/pallas_call | solution.py:351
  81.9 2.1 %collective-permute-start.16 = (f32[2,8,128]{2,1,0:T(8,128)S(1)}, f32[2,8,128]{2,1,0:T(8,128)S(1)}, u32[]{:S(2)}, u32[]{:S(2)}) collective-permute-start(f32[2,8,128]{2,1,0:T(8,128)S(1)} %get-tuple-element.56), channel_id=1, source_target_pairs={{0,1},{1,0},{2,3},{3,2},{4,5},{5,4},{6,7},{7,6},{8,9},{9,8},{10,11... | collective-permute-start | bytes 24584 | tf_op jit(solution)/shard_map/ppermute | solution.py:384
  84.9 2.0 %collective-permute-start.18 = (f32[2,8,128]{2,1,0:T(8,128)S(1)}, f32[2,8,128]{2,1,0:T(8,128)S(1)}, u32[]{:S(2)}, u32[]{:S(2)}) collective-permute-start(f32[2,8,128]{2,1,0:T(8,128)S(1)} %add.28.refs_12_.refs_8_), channel_id=1, source_target_pairs={{0,4},{1,5},{2,6},{3,7},{4,0},{5,1},{6,2},{7,3},{8,12},{9,13},{10,... | collective-permute-start | bytes 24584 | tf_op jit(solution)/shard_map/ppermute | solution.py:386
  86.9 1.5 collective-permute-start.19
  88.4 1.2 collective-permute-start.24
  89.6 1.6 collective-permute-done.19.refs_15_.refs_11_
  91.2 13.9 %shard_map.149 = (f32[2,512,128]{2,1,0:T(8,128)S(1)}, f32[2,8,128]{2,1,0:T(8,128)S(1)}, bf16[1792,128]{1,0:T(8,128)(2,1)S(1)}, bf16[1792,128]{1,0:T(8,128)(2,1)S(1)}) custom-call(s32[4]{0:T(128)S(1)} %pad_add_fusion.where_ref, f32[2,512,128]{2,1,0:T(8,128)S(1)} %get-tuple-element.55.refs_0_, f32[2,512,128]{2,1,0:T(8,128)S(1)} %get-tuple-element.46.hidden_ref.refs_2_.refs_1_, ...), custom_call_target="tpu_custom_call" | custom-call | tf_op jit(solution)/shard_map/pallas_call | solution.py:351
  105.1 2.1 %collective-permute-start.25 = (bf16[1792,128]{1,0:T(8,128)(2,1)S(1)}, bf16[1792,128]{1,0:T(8,128)(2,1)S(1)}, u32[]{:S(2)}, u32[]{:S(2)}) collective-permute-start(bf16[1792,128]{1,0:T(8,128)(2,1)S(1)} %get-tuple-element.65), channel_id=1, source_target_pairs={{0,1},{1,0},{2,3},{3,2},{4,5},{5,4},{6,7},{7,6},{8,9},{9,8},{10,11... | collective-permute-start | bytes 1376264 | tf_op jit(solution)/shard_map/ppermute | solution.py:379
  107.3 1.4 collective-permute-done.20
  108.7 1.8 %collective-permute-start.22 = (f32[2,8,128]{2,1,0:T(8,128)S(1)}, f32[2,8,128]{2,1,0:T(8,128)S(1)}, u32[]{:S(2)}, u32[]{:S(2)}) collective-permute-start(f32[2,8,128]{2,1,0:T(8,128)S(1)} %add.29.refs_4_), channel_id=1, source_target_pairs={{0,4},{1,5},{2,6},{3,7},{4,0},{5,1},{6,2},{7,3},{8,12},{9,13},{10,... | collective-permute-start | bytes 24584 | tf_op jit(solution)/shard_map/ppermute | solution.py:386
  110.5 1.7 %collective-permute-start.23 = (f32[2,8,128]{2,1,0:T(8,128)S(1)}, f32[2,8,128]{2,1,0:T(8,128)S(1)}, u32[]{:S(2)}, u32[]{:S(2)}) collective-permute-start(f32[2,8,128]{2,1,0:T(8,128)S(1)} %add.29.refs_4_), channel_id=1, source_target_pairs={{0,6},{1,7},{2,4},{3,5},{4,2},{5,3},{6,0},{7,1},{8,14},{9,15},{10,... | collective-permute-start | bytes 24584 | tf_op jit(solution)/shard_map/ppermute | solution.py:386
  112.3 2.6 %collective-permute-done.23.refs_7_ = f32[2,8,128]{2,1,0:T(8,128)S(1)} collective-permute-done((f32[2,8,128]{2,1,0:T(8,128)S(1)}, f32[2,8,128]{2,1,0:T(8,128)S(1)}, u32[]{:S(2)}, u32[]{:S(2)}) %collective-permute-start.23) | collective-permute-done | bytes 8224 | tf_op jit(solution)/shard_map/ppermute | solution.py:386
  114.8 1.7 shard_map.150
  116.5 2.1 %collective-permute-start.26 = (bf16[256,128]{1,0:T(8,128)(2,1)S(1)}, bf16[256,128]{1,0:T(8,128)(2,1)S(1)}, u32[]{:S(2)}, u32[]{:S(2)}) collective-permute-start(bf16[256,128]{1,0:T(8,128)(2,1)S(1)} %get-tuple-element.67), channel_id=1, source_target_pairs={{0,1},{1,0},{2,3},{3,2},{4,5},{5,4},{6,7},{7,6},{8,9},{9,8},{10,11... | collective-permute-start | bytes 196616 | tf_op jit(solution)/shard_map/ppermute | solution.py:379
  120.4 1.3 collective-permute-start.27
  121.7 1.2 collective-permute-start.28
  123.1 4.5 %collective-permute-done.27.refs_1_ = bf16[960,128]{1,0:T(8,128)(2,1)S(1)} collective-permute-done((bf16[960,128]{1,0:T(8,128)(2,1)S(1)}, bf16[960,128]{1,0:T(8,128)(2,1)S(1)}, u32[]{:S(2)}, u32[]{:S(2)}) %collective-permute-start.27) | collective-permute-done | bytes 245792 | tf_op jit(solution)/shard_map/ppermute | solution.py:379
  128.5 5.4 %collective-permute-done.29.refs_3_ = bf16[960,128]{1,0:T(8,128)(2,1)S(1)} collective-permute-done((bf16[960,128]{1,0:T(8,128)(2,1)S(1)}, bf16[960,128]{1,0:T(8,128)(2,1)S(1)}, u32[]{:S(2)}, u32[]{:S(2)}) %collective-permute-start.29) | collective-permute-done | bytes 245792 | tf_op jit(solution)/shard_map/ppermute | solution.py:379
  134.7 2.0 %collective-permute-start.31 = (bf16[240,128]{1,0:T(8,128)(2,1)S(1)}, bf16[240,128]{1,0:T(8,128)(2,1)S(1)}, u32[]{:S(2)}, u32[]{:S(2)}) collective-permute-start(bf16[240,128]{1,0:T(8,128)(2,1)S(1)} %get-tuple-element.74), channel_id=1, source_target_pairs={{0,4},{1,5},{2,6},{3,7},{4,0},{5,1},{6,2},{7,3},{8,12},{9,13},{10,... | collective-permute-start | bytes 184328 | tf_op jit(solution)/shard_map/ppermute | solution.py:379
  136.7 1.5 collective-permute-start.32
  138.7 3.3 %collective-permute-done.32.refs_3_ = bf16[240,128]{1,0:T(8,128)(2,1)S(1)} collective-permute-done((bf16[240,128]{1,0:T(8,128)(2,1)S(1)}, bf16[240,128]{1,0:T(8,128)(2,1)S(1)}, u32[]{:S(2)}, u32[]{:S(2)}) %collective-permute-start.32) | collective-permute-done | bytes 61472 | tf_op jit(solution)/shard_map/ppermute | solution.py:379
  142.6 1.5 collective-permute-start.34
  144.2 2.0 %collective-permute-start.35 = (bf16[240,128]{1,0:T(8,128)(2,1)S(1)}, bf16[240,128]{1,0:T(8,128)(2,1)S(1)}, u32[]{:S(2)}, u32[]{:S(2)}) collective-permute-start(bf16[240,128]{1,0:T(8,128)(2,1)S(1)} %shard_map.154.refs_0_), channel_id=1, source_target_pairs={{0,6},{1,7},{2,4},{3,5},{4,2},{5,3},{6,0},{7,1},{8,14},{9,15},{10,... | collective-permute-start | bytes 184328 | tf_op jit(solution)/shard_map/ppermute | solution.py:379
  146.7 2.7 %collective-permute-done.35.refs_3_ = bf16[240,128]{1,0:T(8,128)(2,1)S(1)} collective-permute-done((bf16[240,128]{1,0:T(8,128)(2,1)S(1)}, bf16[240,128]{1,0:T(8,128)(2,1)S(1)}, u32[]{:S(2)}, u32[]{:S(2)}) %collective-permute-start.35) | collective-permute-done | bytes 61472 | tf_op jit(solution)/shard_map/ppermute | solution.py:379
  149.9 1.3 collective-permute-start.36
  152.6 2.4 %collective-permute-done.36.refs_1_ = bf16[976,128]{1,0:T(8,128)(2,1)S(1)} collective-permute-done((bf16[976,128]{1,0:T(8,128)(2,1)S(1)}, bf16[976,128]{1,0:T(8,128)(2,1)S(1)}, u32[]{:S(2)}, u32[]{:S(2)}) %collective-permute-start.36) | collective-permute-done | bytes 249888 | tf_op jit(solution)/shard_map/ppermute | solution.py:379
  155.1 3.7 %collective-permute-done.37.refs_2_ = bf16[976,128]{1,0:T(8,128)(2,1)S(1)} collective-permute-done((bf16[976,128]{1,0:T(8,128)(2,1)S(1)}, bf16[976,128]{1,0:T(8,128)(2,1)S(1)}, u32[]{:S(2)}, u32[]{:S(2)}) %collective-permute-start.37) | collective-permute-done | bytes 249888 | tf_op jit(solution)/shard_map/ppermute | solution.py:379
  160.0 5.7 %collective-permute-start.39 = (bf16[3840,128]{1,0:T(8,128)(2,1)S(1)}, bf16[3840,128]{1,0:T(8,128)(2,1)S(1)}, u32[]{:S(2)}, u32[]{:S(2)}) collective-permute-start(bf16[3840,128]{1,0:T(8,128)(2,1)S(1)} %get-tuple-element.76.own_ref), channel_id=1, source_target_pairs={{0,1},{1,0},{2,3},{3,2},{4,5},{5,4},{6,7},{7,6},{8,9},{9,8},{10,11... | collective-permute-start | bytes 2949128 | tf_op jit(solution)/shard_map/ppermute | solution.py:379
  165.7 4.1 %shard_map.151 = bf16[2,64,2048]{2,1,0:T(8,128)(2,1)} custom-call(s32[4]{0:T(128)S(1)} %pad_add_fusion.where_ref, bf16[2,512,128]{2,1,0:T(8,128)(2,1)S(1)} %get-tuple-element.60.rows_ref, f32[2,8,2048]{2,1,0:T(8,128)S(1)} %get-tuple-element.61.which_ref, s32[8,8,512]{2,1,0:T(8,128)S(1)} %copy-done.7, bf16[512,128]{1,0:T(8,128)(2,1)S(1)} %bitcast.20), custom_call_target="tpu_custom_call" | custom-call | tf_op jit(solution)/shard_map/pallas_call | solution.py:351
  170.9 2.8 %shard_map.157 = (f32[3456,128]{1,0:T(8,128)}, f32[3456,128]{1,0:T(8,128)}, f32[512,128]{1,0:T(8,128)}) custom-call(s32[4]{0:T(128)S(1)} %pad_add_fusion.where_ref, bf16[3840,128]{1,0:T(8,128)(2,1)S(1)} %get-tuple-element.76.own_ref, bf16[3840,128]{1,0:T(8,128)(2,1)S(1)} %collective-permute-done.39.other_ref), custom_call_target="tpu_custom_call" | custom-call | tf_op jit(solution)/shard_map/pallas_call | solution.py:368
  (79 shorter events, 20.1 us)
Async XLA Ops:
  0.6 19.7 %copy-start.10 = (f32[3,128]{1,0:T(4,128)S(1)}, f32[3,128]{1,0:T(4,128)}, u32[]{:S(2)}) copy-start(f32[3,128]{1,0:T(4,128)} %scale_ref.7) | copy-start | bytes 4612
  0.6 19.7 %copy-start.11 = (f32[3,128]{1,0:T(4,128)S(1)}, f32[3,128]{1,0:T(4,128)}, u32[]{:S(2)}) copy-start(f32[3,128]{1,0:T(4,128)} %refs_7_.3) | copy-start | bytes 4612
  5.2 15.2 %copy-start.1 = (s32[8,27,512]{2,0,1:T(8,128)S(1)}, s32[8,27,512]{2,0,1:T(8,128)}, u32[]{:S(2)}) copy-start(s32[8,27,512]{2,0,1:T(8,128)} %param.11) | copy-start | bytes 1327108
  5.2 15.2 %copy-start.3 = (bf16[27,128,128]{2,1,0:T(8,128)(2,1)S(1)}, bf16[27,128,128]{2,1,0:T(8,128)(2,1)}, u32[]{:S(2)}) copy-start(bf16[27,128,128]{2,1,0:T(8,128)(2,1)} %refs_5_.3) | copy-start | bytes 2654212
  5.2 33.2 %copy-start.2 = (bf16[27,128,128]{2,1,0:T(8,128)(2,1)S(1)}, bf16[27,128,128]{2,1,0:T(8,128)(2,1)}, u32[]{:S(2)}) copy-start(bf16[27,128,128]{2,1,0:T(8,128)(2,1)} %refs_5_.2) | copy-start | bytes 2654212
  10.0 1.2 collective-permute-start
  11.3 4.8 %collective-permute-start.1 = (f32[2,8,128]{2,1,0:T(8,128)S(1)}, f32[2,8,128]{2,1,0:T(8,128)S(1)}, u32[]{:S(2)}, u32[]{:S(2)}) collective-permute-start(f32[2,8,128]{2,1,0:T(8,128)S(1)} %add.24.refs_0_.refs_16_), channel_id=1, source_target_pairs={{0,2},{1,3},{2,0},{3,1},{4,6},{5,7},{6,4},{7,5},{8,10},{9,11},{10,... | collective-permute-start | bytes 24584 | tf_op jit(solution)/shard_map/ppermute | solution.py:386
  13.7 3.4 %collective-permute-start.2 = (f32[2,8,128]{2,1,0:T(8,128)S(1)}, f32[2,8,128]{2,1,0:T(8,128)S(1)}, u32[]{:S(2)}, u32[]{:S(2)}) collective-permute-start(f32[2,8,128]{2,1,0:T(8,128)S(1)} %add.24.refs_0_.refs_16_), channel_id=1, source_target_pairs={{0,4},{1,5},{2,6},{3,7},{4,0},{5,1},{6,2},{7,3},{8,12},{9,13},{10,... | collective-permute-start | bytes 24584 | tf_op jit(solution)/shard_map/ppermute | solution.py:386
  16.0 4.3 %collective-permute-start.3 = (f32[2,8,128]{2,1,0:T(8,128)S(1)}, f32[2,8,128]{2,1,0:T(8,128)S(1)}, u32[]{:S(2)}, u32[]{:S(2)}) collective-permute-start(f32[2,8,128]{2,1,0:T(8,128)S(1)} %add.24.refs_0_.refs_16_), channel_id=1, source_target_pairs={{0,6},{1,7},{2,4},{3,5},{4,2},{5,3},{6,0},{7,1},{8,14},{9,15},{10,... | collective-permute-start | bytes 24584 | tf_op jit(solution)/shard_map/ppermute | solution.py:386
  20.4 37.1 %copy-start.5 = (bf16[8,512,128]{2,1,0:T(8,128)(2,1)S(1)}, bf16[8,512,128]{2,1,0:T(8,128)(2,1)}, u32[]{:S(2)}) copy-start(bf16[8,512,128]{2,1,0:T(8,128)(2,1)} %grad_ref.1) | copy-start | bytes 3145732
  30.8 2.9 %collective-permute-start.4 = (f32[2,8,128]{2,1,0:T(8,128)S(1)}, f32[2,8,128]{2,1,0:T(8,128)S(1)}, u32[]{:S(2)}, u32[]{:S(2)}) collective-permute-start(f32[2,8,128]{2,1,0:T(8,128)S(1)} %get-tuple-element.47), channel_id=1, source_target_pairs={{0,1},{1,0},{2,3},{3,2},{4,5},{5,4},{6,7},{7,6},{8,9},{9,8},{10,11... | collective-permute-start | bytes 24584 | tf_op jit(solution)/shard_map/ppermute | solution.py:384
  33.7 3.6 %collective-permute-start.5 = (f32[2,8,128]{2,1,0:T(8,128)S(1)}, f32[2,8,128]{2,1,0:T(8,128)S(1)}, u32[]{:S(2)}, u32[]{:S(2)}) collective-permute-start(f32[2,8,128]{2,1,0:T(8,128)S(1)} %add.25.refs_0_.refs_16_.refs_8_), channel_id=1, source_target_pairs={{0,2},{1,3},{2,0},{3,1},{4,6},{5,7},{6,4},{7,5},{8,10},{9,11},{10,... | collective-permute-start | bytes 24584 | tf_op jit(solution)/shard_map/ppermute | solution.py:386
  33.8 3.6 %collective-permute-start.6 = (f32[2,8,128]{2,1,0:T(8,128)S(1)}, f32[2,8,128]{2,1,0:T(8,128)S(1)}, u32[]{:S(2)}, u32[]{:S(2)}) collective-permute-start(f32[2,8,128]{2,1,0:T(8,128)S(1)} %add.25.refs_0_.refs_16_.refs_8_), channel_id=1, source_target_pairs={{0,4},{1,5},{2,6},{3,7},{4,0},{5,1},{6,2},{7,3},{8,12},{9,13},{10,... | collective-permute-start | bytes 24584 | tf_op jit(solution)/shard_map/ppermute | solution.py:386
  33.8 4.6 %collective-permute-start.7 = (f32[2,8,128]{2,1,0:T(8,128)S(1)}, f32[2,8,128]{2,1,0:T(8,128)S(1)}, u32[]{:S(2)}, u32[]{:S(2)}) collective-permute-start(f32[2,8,128]{2,1,0:T(8,128)S(1)} %add.25.refs_0_.refs_16_.refs_8_), channel_id=1, source_target_pairs={{0,6},{1,7},{2,4},{3,5},{4,2},{5,3},{6,0},{7,1},{8,14},{9,15},{10,... | collective-permute-start | bytes 24584 | tf_op jit(solution)/shard_map/ppermute | solution.py:386
  48.8 2.7 %collective-permute-start.8 = (f32[2,8,128]{2,1,0:T(8,128)S(1)}, f32[2,8,128]{2,1,0:T(8,128)S(1)}, u32[]{:S(2)}, u32[]{:S(2)}) collective-permute-start(f32[2,8,128]{2,1,0:T(8,128)S(1)} %get-tuple-element.50), channel_id=1, source_target_pairs={{0,1},{1,0},{2,3},{3,2},{4,5},{5,4},{6,7},{7,6},{8,9},{9,8},{10,11... | collective-permute-start | bytes 24584 | tf_op jit(solution)/shard_map/ppermute | solution.py:384
  51.5 3.7 %collective-permute-start.10 = (f32[2,8,128]{2,1,0:T(8,128)S(1)}, f32[2,8,128]{2,1,0:T(8,128)S(1)}, u32[]{:S(2)}, u32[]{:S(2)}) collective-permute-start(f32[2,8,128]{2,1,0:T(8,128)S(1)} %add.26.refs_0_.refs_8_), channel_id=1, source_target_pairs={{0,4},{1,5},{2,6},{3,7},{4,0},{5,1},{6,2},{7,3},{8,12},{9,13},{10,... | collective-permute-start | bytes 24584 | tf_op jit(solution)/shard_map/ppermute | solution.py:386
  51.7 4.4 %collective-permute-start.11 = (f32[2,8,128]{2,1,0:T(8,128)S(1)}, f32[2,8,128]{2,1,0:T(8,128)S(1)}, u32[]{:S(2)}, u32[]{:S(2)}) collective-permute-start(f32[2,8,128]{2,1,0:T(8,128)S(1)} %add.26.refs_0_.refs_8_), channel_id=1, source_target_pairs={{0,6},{1,7},{2,4},{3,5},{4,2},{5,3},{6,0},{7,1},{8,14},{9,15},{10,... | collective-permute-start | bytes 24584 | tf_op jit(solution)/shard_map/ppermute | solution.py:386
  55.0 2.5 %collective-permute-start.9 = (f32[2,8,128]{2,1,0:T(8,128)S(1)}, f32[2,8,128]{2,1,0:T(8,128)S(1)}, u32[]{:S(2)}, u32[]{:S(2)}) collective-permute-start(f32[2,8,128]{2,1,0:T(8,128)S(1)} %add.26.refs_0_.refs_8_), channel_id=1, source_target_pairs={{0,2},{1,3},{2,0},{3,1},{4,6},{5,7},{6,4},{7,5},{8,10},{9,11},{10,... | collective-permute-start | bytes 24584 | tf_op jit(solution)/shard_map/ppermute | solution.py:386
  59.3 2.6 %collective-permute-start.12 = (f32[2,8,128]{2,1,0:T(8,128)S(1)}, f32[2,8,128]{2,1,0:T(8,128)S(1)}, u32[]{:S(2)}, u32[]{:S(2)}) collective-permute-start(f32[2,8,128]{2,1,0:T(8,128)S(1)} %get-tuple-element.54), channel_id=1, source_target_pairs={{0,1},{1,0},{2,3},{3,2},{4,5},{5,4},{6,7},{7,6},{8,9},{9,8},{10,11... | collective-permute-start | bytes 24584 | tf_op jit(solution)/shard_map/ppermute | solution.py:384
  61.9 3.6 %collective-permute-start.13 = (f32[2,8,128]{2,1,0:T(8,128)S(1)}, f32[2,8,128]{2,1,0:T(8,128)S(1)}, u32[]{:S(2)}, u32[]{:S(2)}) collective-permute-start(f32[2,8,128]{2,1,0:T(8,128)S(1)} %add.27.refs_12_), channel_id=1, source_target_pairs={{0,2},{1,3},{2,0},{3,1},{4,6},{5,7},{6,4},{7,5},{8,10},{9,11},{10,... | collective-permute-start | bytes 24584 | tf_op jit(solution)/shard_map/ppermute | solution.py:386
  62.2 3.4 %collective-permute-start.14 = (f32[2,8,128]{2,1,0:T(8,128)S(1)}, f32[2,8,128]{2,1,0:T(8,128)S(1)}, u32[]{:S(2)}, u32[]{:S(2)}) collective-permute-start(f32[2,8,128]{2,1,0:T(8,128)S(1)} %add.27.refs_12_), channel_id=1, source_target_pairs={{0,4},{1,5},{2,6},{3,7},{4,0},{5,1},{6,2},{7,3},{8,12},{9,13},{10,... | collective-permute-start | bytes 24584 | tf_op jit(solution)/shard_map/ppermute | solution.py:386
  63.7 4.3 %collective-permute-start.15 = (f32[2,8,128]{2,1,0:T(8,128)S(1)}, f32[2,8,128]{2,1,0:T(8,128)S(1)}, u32[]{:S(2)}, u32[]{:S(2)}) collective-permute-start(f32[2,8,128]{2,1,0:T(8,128)S(1)} %add.27.refs_12_), channel_id=1, source_target_pairs={{0,6},{1,7},{2,4},{3,5},{4,2},{5,3},{6,0},{7,1},{8,14},{9,15},{10,... | collective-permute-start | bytes 24584 | tf_op jit(solution)/shard_map/ppermute | solution.py:386
  81.9 2.9 %collective-permute-start.16 = (f32[2,8,128]{2,1,0:T(8,128)S(1)}, f32[2,8,128]{2,1,0:T(8,128)S(1)}, u32[]{:S(2)}, u32[]{:S(2)}) collective-permute-start(f32[2,8,128]{2,1,0:T(8,128)S(1)} %get-tuple-element.56), channel_id=1, source_target_pairs={{0,1},{1,0},{2,3},{3,2},{4,5},{5,4},{6,7},{7,6},{8,9},{9,8},{10,11... | collective-permute-start | bytes 24584 | tf_op jit(solution)/shard_map/ppermute | solution.py:384
  84.9 4.7 %collective-permute-start.17 = (f32[2,8,128]{2,1,0:T(8,128)S(1)}, f32[2,8,128]{2,1,0:T(8,128)S(1)}, u32[]{:S(2)}, u32[]{:S(2)}) collective-permute-start(f32[2,8,128]{2,1,0:T(8,128)S(1)} %add.28.refs_12_.refs_8_), channel_id=1, source_target_pairs={{0,2},{1,3},{2,0},{3,1},{4,6},{5,7},{6,4},{7,5},{8,10},{9,11},{10,... | collective-permute-start | bytes 24584 | tf_op jit(solution)/shard_map/ppermute | solution.py:386
  84.9 4.7 %collective-permute-start.18 = (f32[2,8,128]{2,1,0:T(8,128)S(1)}, f32[2,8,128]{2,1,0:T(8,128)S(1)}, u32[]{:S(2)}, u32[]{:S(2)}) collective-permute-start(f32[2,8,128]{2,1,0:T(8,128)S(1)} %add.28.refs_12_.refs_8_), channel_id=1, source_target_pairs={{0,4},{1,5},{2,6},{3,7},{4,0},{5,1},{6,2},{7,3},{8,12},{9,13},{10,... | collective-permute-start | bytes 24584 | tf_op jit(solution)/shard_map/ppermute | solution.py:386
  86.9 4.3 %collective-permute-start.19 = (f32[2,8,128]{2,1,0:T(8,128)S(1)}, f32[2,8,128]{2,1,0:T(8,128)S(1)}, u32[]{:S(2)}, u32[]{:S(2)}) collective-permute-start(f32[2,8,128]{2,1,0:T(8,128)S(1)} %add.28.refs_12_.refs_8_), channel_id=1, source_target_pairs={{0,6},{1,7},{2,4},{3,5},{4,2},{5,3},{6,0},{7,1},{8,14},{9,15},{10,... | collective-permute-start | bytes 24584 | tf_op jit(solution)/shard_map/ppermute | solution.py:386
  88.4 31.1 %collective-permute-start.24 = (bf16[1792,128]{1,0:T(8,128)(2,1)S(1)}, bf16[1792,128]{1,0:T(8,128)(2,1)S(1)}, u32[]{:S(2)}, u32[]{:S(2)}) collective-permute-start(bf16[1792,128]{1,0:T(8,128)(2,1)S(1)} %get-tuple-element.63), channel_id=1, source_target_pairs={{0,1},{1,0},{2,3},{3,2},{4,5},{5,4},{6,7},{7,6},{8,9},{9,8},{10,11... | collective-permute-start | bytes 1376264 | tf_op jit(solution)/shard_map/ppermute | solution.py:379
  105.1 14.5 %collective-permute-start.25 = (bf16[1792,128]{1,0:T(8,128)(2,1)S(1)}, bf16[1792,128]{1,0:T(8,128)(2,1)S(1)}, u32[]{:S(2)}, u32[]{:S(2)}) collective-permute-start(bf16[1792,128]{1,0:T(8,128)(2,1)S(1)} %get-tuple-element.65), channel_id=1, source_target_pairs={{0,1},{1,0},{2,3},{3,2},{4,5},{5,4},{6,7},{7,6},{8,9},{9,8},{10,11... | collective-permute-start | bytes 1376264 | tf_op jit(solution)/shard_map/ppermute | solution.py:379
  107.2 1.5 collective-permute-start.20
  108.7 3.6 %collective-permute-start.21 = (f32[2,8,128]{2,1,0:T(8,128)S(1)}, f32[2,8,128]{2,1,0:T(8,128)S(1)}, u32[]{:S(2)}, u32[]{:S(2)}) collective-permute-start(f32[2,8,128]{2,1,0:T(8,128)S(1)} %add.29.refs_4_), channel_id=1, source_target_pairs={{0,2},{1,3},{2,0},{3,1},{4,6},{5,7},{6,4},{7,5},{8,10},{9,11},{10,... | collective-permute-start | bytes 24584 | tf_op jit(solution)/shard_map/ppermute | solution.py:386
  108.7 3.6 %collective-permute-start.22 = (f32[2,8,128]{2,1,0:T(8,128)S(1)}, f32[2,8,128]{2,1,0:T(8,128)S(1)}, u32[]{:S(2)}, u32[]{:S(2)}) collective-permute-start(f32[2,8,128]{2,1,0:T(8,128)S(1)} %add.29.refs_4_), channel_id=1, source_target_pairs={{0,4},{1,5},{2,6},{3,7},{4,0},{5,1},{6,2},{7,3},{8,12},{9,13},{10,... | collective-permute-start | bytes 24584 | tf_op jit(solution)/shard_map/ppermute | solution.py:386
  110.5 4.3 %collective-permute-start.23 = (f32[2,8,128]{2,1,0:T(8,128)S(1)}, f32[2,8,128]{2,1,0:T(8,128)S(1)}, u32[]{:S(2)}, u32[]{:S(2)}) collective-permute-start(f32[2,8,128]{2,1,0:T(8,128)S(1)} %add.29.refs_4_), channel_id=1, source_target_pairs={{0,6},{1,7},{2,4},{3,5},{4,2},{5,3},{6,0},{7,1},{8,14},{9,15},{10,... | collective-permute-start | bytes 24584 | tf_op jit(solution)/shard_map/ppermute | solution.py:386
  116.5 3.0 %collective-permute-start.26 = (bf16[256,128]{1,0:T(8,128)(2,1)S(1)}, bf16[256,128]{1,0:T(8,128)(2,1)S(1)}, u32[]{:S(2)}, u32[]{:S(2)}) collective-permute-start(bf16[256,128]{1,0:T(8,128)(2,1)S(1)} %get-tuple-element.67), channel_id=1, source_target_pairs={{0,1},{1,0},{2,3},{3,2},{4,5},{5,4},{6,7},{7,6},{8,9},{9,8},{10,11... | collective-permute-start | bytes 196616 | tf_op jit(solution)/shard_map/ppermute | solution.py:379
  120.4 45.3 %copy-start.7 = (s32[8,8,512]{2,1,0:T(8,128)S(1)}, s32[8,8,512]{2,1,0:T(8,128)}, u32[]{:S(2)}) copy-start(s32[8,8,512]{2,1,0:T(8,128)} %down_ref.3) | copy-start | bytes 393220
  120.4 45.3 %copy-start.9 = (bf16[8,64,128]{2,1,0:T(8,128)(2,1)S(1)}, bf16[8,64,128]{2,1,0:T(8,128)(2,1)}, u32[]{:S(2)}) copy-start(bf16[8,64,128]{2,1,0:T(8,128)(2,1)} %param.12) | copy-start | bytes 393220
  120.4 7.3 %collective-permute-start.27 = (bf16[960,128]{1,0:T(8,128)(2,1)S(1)}, bf16[960,128]{1,0:T(8,128)(2,1)S(1)}, u32[]{:S(2)}, u32[]{:S(2)}) collective-permute-start(bf16[960,128]{1,0:T(8,128)(2,1)S(1)} %get-tuple-element.69), channel_id=1, source_target_pairs={{0,8},{8,0},{16,24},{24,16},{1,9},{9,1},{17,25},{25,17},{2,10},{10... | collective-permute-start | bytes 737288 | tf_op jit(solution)/shard_map/ppermute | solution.py:379
  121.7 6.9 %collective-permute-start.28 = (bf16[960,128]{1,0:T(8,128)(2,1)S(1)}, bf16[960,128]{1,0:T(8,128)(2,1)S(1)}, u32[]{:S(2)}, u32[]{:S(2)}) collective-permute-start(bf16[960,128]{1,0:T(8,128)(2,1)S(1)} %get-tuple-element.70), channel_id=1, source_target_pairs={{0,16},{8,24},{16,0},{24,8},{1,17},{9,25},{17,1},{25,9},{2,18},{10... | collective-permute-start | bytes 737288 | tf_op jit(solution)/shard_map/ppermute | solution.py:379
  122.9 11.0 %collective-permute-start.29 = (bf16[960,128]{1,0:T(8,128)(2,1)S(1)}, bf16[960,128]{1,0:T(8,128)(2,1)S(1)}, u32[]{:S(2)}, u32[]{:S(2)}) collective-permute-start(bf16[960,128]{1,0:T(8,128)(2,1)S(1)} %get-tuple-element.71), channel_id=1, source_target_pairs={{0,24},{8,16},{16,8},{24,0},{1,25},{9,17},{17,9},{25,1},{2,26},{10... | collective-permute-start | bytes 737288 | tf_op jit(solution)/shard_map/ppermute | solution.py:379
  134.6 3.6 %collective-permute-start.30 = (bf16[240,128]{1,0:T(8,128)(2,1)S(1)}, bf16[240,128]{1,0:T(8,128)(2,1)S(1)}, u32[]{:S(2)}, u32[]{:S(2)}) collective-permute-start(bf16[240,128]{1,0:T(8,128)(2,1)S(1)} %get-tuple-element.73), channel_id=1, source_target_pairs={{0,2},{1,3},{2,0},{3,1},{4,6},{5,7},{6,4},{7,5},{8,10},{9,11},{10,... | collective-permute-start | bytes 184328 | tf_op jit(solution)/shard_map/ppermute | solution.py:379
  134.7 4.0 %collective-permute-start.31 = (bf16[240,128]{1,0:T(8,128)(2,1)S(1)}, bf16[240,128]{1,0:T(8,128)(2,1)S(1)}, u32[]{:S(2)}, u32[]{:S(2)}) collective-permute-start(bf16[240,128]{1,0:T(8,128)(2,1)S(1)} %get-tuple-element.74), channel_id=1, source_target_pairs={{0,4},{1,5},{2,6},{3,7},{4,0},{5,1},{6,2},{7,3},{8,12},{9,13},{10,... | collective-permute-start | bytes 184328 | tf_op jit(solution)/shard_map/ppermute | solution.py:379
  136.7 5.3 %collective-permute-start.32 = (bf16[240,128]{1,0:T(8,128)(2,1)S(1)}, bf16[240,128]{1,0:T(8,128)(2,1)S(1)}, u32[]{:S(2)}, u32[]{:S(2)}) collective-permute-start(bf16[240,128]{1,0:T(8,128)(2,1)S(1)} %get-tuple-element.75), channel_id=1, source_target_pairs={{0,6},{1,7},{2,4},{3,5},{4,2},{5,3},{6,0},{7,1},{8,14},{9,15},{10,... | collective-permute-start | bytes 184328 | tf_op jit(solution)/shard_map/ppermute | solution.py:379
  142.5 3.6 %collective-permute-start.33 = (bf16[240,128]{1,0:T(8,128)(2,1)S(1)}, bf16[240,128]{1,0:T(8,128)(2,1)S(1)}, u32[]{:S(2)}, u32[]{:S(2)}) collective-permute-start(bf16[240,128]{1,0:T(8,128)(2,1)S(1)} %shard_map.154.refs_0_), channel_id=1, source_target_pairs={{0,2},{1,3},{2,0},{3,1},{4,6},{5,7},{6,4},{7,5},{8,10},{9,11},{10,... | collective-permute-start | bytes 184328 | tf_op jit(solution)/shard_map/ppermute | solution.py:379
  142.6 4.0 %collective-permute-start.34 = (bf16[240,128]{1,0:T(8,128)(2,1)S(1)}, bf16[240,128]{1,0:T(8,128)(2,1)S(1)}, u32[]{:S(2)}, u32[]{:S(2)}) collective-permute-start(bf16[240,128]{1,0:T(8,128)(2,1)S(1)} %shard_map.154.refs_0_), channel_id=1, source_target_pairs={{0,4},{1,5},{2,6},{3,7},{4,0},{5,1},{6,2},{7,3},{8,12},{9,13},{10,... | collective-permute-start | bytes 184328 | tf_op jit(solution)/shard_map/ppermute | solution.py:379
  144.2 5.2 %collective-permute-start.35 = (bf16[240,128]{1,0:T(8,128)(2,1)S(1)}, bf16[240,128]{1,0:T(8,128)(2,1)S(1)}, u32[]{:S(2)}, u32[]{:S(2)}) collective-permute-start(bf16[240,128]{1,0:T(8,128)(2,1)S(1)} %shard_map.154.refs_0_), channel_id=1, source_target_pairs={{0,6},{1,7},{2,4},{3,5},{4,2},{5,3},{6,0},{7,1},{8,14},{9,15},{10,... | collective-permute-start | bytes 184328 | tf_op jit(solution)/shard_map/ppermute | solution.py:379
  149.9 5.2 %collective-permute-start.36 = (bf16[976,128]{1,0:T(8,128)(2,1)S(1)}, bf16[976,128]{1,0:T(8,128)(2,1)S(1)}, u32[]{:S(2)}, u32[]{:S(2)}) collective-permute-start(bf16[976,128]{1,0:T(8,128)(2,1)S(1)} %shard_map.155.refs_0_), channel_id=1, source_target_pairs={{0,8},{8,0},{16,24},{24,16},{1,9},{9,1},{17,25},{25,17},{2,10},{10... | collective-permute-start | bytes 749576 | tf_op jit(solution)/shard_map/ppermute | solution.py:379
  151.2 7.6 %collective-permute-start.37 = (bf16[976,128]{1,0:T(8,128)(2,1)S(1)}, bf16[976,128]{1,0:T(8,128)(2,1)S(1)}, u32[]{:S(2)}, u32[]{:S(2)}) collective-permute-start(bf16[976,128]{1,0:T(8,128)(2,1)S(1)} %shard_map.155.refs_0_), channel_id=1, source_target_pairs={{0,16},{8,24},{16,0},{24,8},{1,17},{9,25},{17,1},{25,9},{2,18},{10... | collective-permute-start | bytes 749576 | tf_op jit(solution)/shard_map/ppermute | solution.py:379
  151.5 7.9 %collective-permute-start.38 = (bf16[976,128]{1,0:T(8,128)(2,1)S(1)}, bf16[976,128]{1,0:T(8,128)(2,1)S(1)}, u32[]{:S(2)}, u32[]{:S(2)}) collective-permute-start(bf16[976,128]{1,0:T(8,128)(2,1)S(1)} %shard_map.155.refs_0_), channel_id=1, source_target_pairs={{0,24},{8,16},{16,8},{24,0},{1,25},{9,17},{17,9},{25,1},{2,26},{10... | collective-permute-start | bytes 749576 | tf_op jit(solution)/shard_map/ppermute | solution.py:379
  160.0 10.9 %collective-permute-start.39 = (bf16[3840,128]{1,0:T(8,128)(2,1)S(1)}, bf16[3840,128]{1,0:T(8,128)(2,1)S(1)}, u32[]{:S(2)}, u32[]{:S(2)}) collective-permute-start(bf16[3840,128]{1,0:T(8,128)(2,1)S(1)} %get-tuple-element.76.own_ref), channel_id=1, source_target_pairs={{0,1},{1,0},{2,3},{3,2},{4,5},{5,4},{6,7},{7,6},{8,9},{9,8},{10,11... | collective-permute-start | bytes 2949128 | tf_op jit(solution)/shard_map/ppermute | solution.py:379
  (4 other events, 4.4 us)

commit v3 on v2

--- a/solution.py
+++ b/solution.py
@@ -10,6 +10,7 @@
 EPSILON = 1e-05
 F32 = jnp.float32
 BF16 = jnp.bfloat16
+F8 = jnp.float8_e4m3fn
 VMEM_BYTES = 48 << 20
 
 
@@ -23,7 +24,27 @@
 
 def hits(index_row, rows):
     places = lax.broadcasted_iota(jnp.int16, (rows, index_row.shape[1]), 0)
-    return jnp.where(places == index_row, jnp.bfloat16(1), jnp.bfloat16(0))
+    return jnp.where(places == index_row, jnp.bfloat16(1), jnp.bfloat16(0)).astype(F8)
+
+
+def power_for(largest):
+    power = jnp.full_like(largest, 2.0**-60)
+    for exponent in (64, 32, 16, 8, 4, 2, 1):
+        raised = power * (2.0**exponent)
+        power = jnp.where(largest * raised <= 224.0, raised, power)
+    return power
+
+
+def two_parts(scaled):
+    high = scaled.astype(F8)
+    low = (scaled - high.astype(F32)).astype(F8)
+    return jnp.concatenate([high, low], axis=1)
+
+
+def moved_rows(where_ref, near_ref, offset, pair):
+    both = mm(near_hits(where_ref, near_ref, offset), pair)
+    channels = pair.shape[1] // 2
+    return (both[:, :channels] + both[:, channels:]).astype(BF16)
 
 
 def near_row(where_ref, near_ref, offset):
@@ -86,7 +107,24 @@
     return jnp.where(inside, jnp.bfloat16(1), jnp.bfloat16(0))
 
 
-def down_kernel(where_ref, feats_ref, down_ref, near_ref, weight_ref, hidden_ref, sums_ref, kids_ref, which_ref, spread_ref, parent_ref):
+def down_kernel(where_ref, feats_hbm, down_hbm, weight_ref, hidden_ref, sums_ref, kids_ref, which_ref, spread_ref, parent_ref, feats_all, down_all, arrivals):
+    micro = pl.program_id(0)
+
+    def copies(b):
+        return (
+            pltpu.make_async_copy(down_hbm.at[where_ref[0] + b], down_all.at[b], arrivals.at[b, 0]),
+            pltpu.make_async_copy(feats_hbm.at[where_ref[0] + b], feats_all.at[b], arrivals.at[b, 1]),
+        )
+
+    @pl.when(micro == 0)
+    def _():
+        for b in range(feats_all.shape[0]):
+            for copy in copies(b):
+                copy.start()
+
+    for copy in copies(micro):
+        copy.wait()
+    feats_ref, down_ref = feats_all.at[pl.ds(micro, 1)], down_all.at[pl.ds(micro, 1)]
     in_channels, fine_rows = feats_ref.shape[1], feats_ref.shape[2]
     offsets, coarse_rows = down_ref.shape[1], down_ref.shape[2]
     channels = weight_ref.shape[1]
@@ -117,19 +155,27 @@
     kids_ref[0] = kids
     hidden = jnp.transpose(mm(jnp.transpose(weight_ref[...]), kids))
     hidden_ref[0] = hidden
-    _, count = live_mask(where_ref, near_ref, channels)
+    count = jnp.sum((last > first).astype(F32), axis=1, keepdims=True)
     put_sums(sums_ref, col_sum(hidden), col_sum(hidden * hidden), count)
 
 
 def conv_all(where_ref, source, near_ref, weight_ref):
-    out = mm(source, weight_ref[13])
-    for j in range(0, 13):
+    values = source.astype(F32)
+    largest = jnp.max(jnp.max(jnp.abs(values), axis=0, keepdims=True), axis=1, keepdims=True)
+    power = power_for(largest)
+    scaled = values * power
+    pair = two_parts(scaled)
+    out = None
+    for group in ((0, 1), (2, 3), (4, 5), (6, 7), (8, 9), (10, 11), (12, 13)):
+        offsets = [k for j in group for k in ((j, 26 - j) if j < 13 else (13,))]
         rows = [
-            mm(near_hits(where_ref, near_ref, 26 - k), source).astype(BF16) for k in (j, 26 - j)
+            scaled.astype(BF16) if k == 13 else moved_rows(where_ref, near_ref, 26 - k, pair)
+            for k in offsets
         ]
-        weight = jnp.concatenate([weight_ref[j], weight_ref[26 - j]], axis=0)
-        out = out + mm(jnp.concatenate(rows, axis=1), weight)
-    return out
+        weight = jnp.concatenate([weight_ref[k] for k in offsets], axis=0)
+        term = mm(jnp.concatenate(rows, axis=1), weight)
+        out = term if out is None else out + term
+    return out * (1.0 / power)
 
 
 def forward_kernel(norm_at, rounded, where_ref, hidden_ref, near_ref, weight_ref, scale_ref, shift_ref, *refs):
@@ -186,17 +232,30 @@
 
     channels = hidden_ref.shape[2]
     act_t = jnp.transpose(act_ref[0])
-    below = mm_t(rows_grad, weight_ref[13])
-    grad_ref[13 * channels : 14 * channels] += mm(act_t, rows_grad)
-    for j in range(13):
+    values = rows_grad.astype(F32)
+    power = power_for(jnp.max(jnp.abs(values), axis=0, keepdims=True))
+    undo = 1.0 / power
+    undo_low = undo.astype(BF16)
+    scaled = values * power
+    pair = two_parts(scaled)
+    below = None
+    for group in ((0, 1), (2, 3), (4, 5), (6, 7), (8, 9), (10, 11), (12, 13)):
+        offsets = [k for j in group for k in ((j, 26 - j) if j < 13 else (13,))]
         moved = jnp.concatenate(
-            [mm(near_hits(where_ref, near_ref, k), rows_grad).astype(BF16) for k in (j, 26 - j)], axis=1
+            [
+                scaled.astype(BF16) if k == 13 else moved_rows(where_ref, near_ref, k, pair)
+                for k in offsets
+            ],
+            axis=1,
         )
-        weight = jnp.concatenate([weight_ref[j], weight_ref[26 - j]], axis=1)
-        below = below + mm_t(moved, weight)
-        pair = mm(act_t, moved)
-        grad_ref[j * channels : (j + 1) * channels] += pair[:, :channels]
-        grad_ref[(26 - j) * channels : (27 - j) * channels] += pair[:, channels:]
+        weight = jnp.concatenate([weight_ref[k] * undo_low for k in offsets], axis=1)
+        term = mm_t(moved, weight)
+        below = term if below is None else below + term
+        products = mm(act_t, moved)
+        for i, k in enumerate(offsets):
+            grad_ref[k * channels : (k + 1) * channels] += (
+                products[:, i * channels : (i + 1) * channels] * undo
+            )
     below = below.astype(BF16).astype(F32)
     if with_skip:
         below = below + skip_ref[0].astype(BF16).astype(F32)
@@ -274,24 +333,30 @@
             base += size
 
 
-def spread_kernel(count, at, where_ref, *refs):
-    sources, outs = refs[:-count], refs[-count:]
-    place = where_ref[at]
-    size = outs[0].shape[0]
-    for j in range(count):
+def spread_kernel(depths, sources, where_ref, *refs):
+    blocks, halves, outs = refs[:sources], refs[sources : sources + 2], refs[sources + 2 :]
+    place = where_ref[3]
+    small = halves[0].shape[0] // depths
+    size = outs[0].shape[0] - small
+    for j in range(depths):
         rows = pl.ds(pl.multiple_of((place ^ j) * size, 16), size)
-        outs[j][...] = tree_sum([ref[rows].astype(F32) for ref in sources]).astype(BF16)
+        outs[j][:size] = tree_sum([ref[rows].astype(F32) for ref in blocks]).astype(BF16)
+        rows = pl.ds(pl.multiple_of((place ^ j) * small, 16), small)
+        outs[j][size:] = (halves[0][rows].astype(F32) + halves[1][rows].astype(F32)).astype(BF16)
 
 
 def add_kernel(where_ref, *refs):
     refs[-1][...] = tree_sum([as_f32(ref) for ref in refs[:-1]]).astype(BF16)
 
 
-def join_kernel(ways, where_ref, *refs):
+def join_kernel(ways, small, where_ref, *refs):
     pieces, sums_refs, out_ref = refs[: -3 * ways - 1], refs[-3 * ways - 1 : -1], refs[-1]
-    size = pieces[0].shape[0]
+    size = pieces[0].shape[0] - small
+    base = len(pieces) * size
     for j, ref in enumerate(pieces):
-        out_ref[pl.ds(pl.multiple_of((where_ref[3] ^ j) * size, 16), size)] = ref[...]
+        place = where_ref[3] ^ j
+        out_ref[pl.ds(pl.multiple_of(place * size, 16), size)] = ref[:size]
+        out_ref[pl.ds(pl.multiple_of(base + place * small, 16), small)] = ref[size:]
     rows = []
     for t in range(3):
         totals = tree_sum([ref[...] for ref in sums_refs[t * ways : (t + 1) * ways]])
@@ -299,35 +364,40 @@
     exact = jnp.concatenate(rows + [jnp.zeros((2, rows[0].shape[1]), F32)], axis=0)
     high = exact.astype(BF16)
     low = (exact - high.astype(F32)).astype(BF16)
-    out_ref[len(pieces) * size :] = jnp.concatenate([high, low], axis=0)
-
-
-def gather_kernel(where_ref, *refs):
-    pieces, (out_ref, sums_ref) = refs[:-2], refs[-2:]
-    size = pieces[0].shape[0] - 16
+    out_ref[base + len(pieces) * small :] = jnp.concatenate([high, low], axis=0)
+
+
+def gather_kernel(size, where_ref, *refs):
+    pieces, (out_ref, scale_ref, shift_ref) = refs[:-3], refs[-3:]
     for j, ref in enumerate(pieces):
         out_ref[pl.ds(pl.multiple_of((where_ref[2] ^ j) * size, 16), size)] = ref[:size]
     tails = [ref[size:].astype(F32) for ref in pieces]
-    sums_ref[...] = tree_sum([tail[:8] + tail[8:] for tail in tails])
-
-
-def final_kernel(parts, where_ref, own_ref, other_ref, *outs):
+    middle = tails[0].shape[0] - 16
+    out_ref[len(pieces) * size :] = tree_sum([tail[:middle] for tail in tails]).astype(BF16)
+    sums = tree_sum([tail[middle : middle + 8] + tail[middle + 8 :] for tail in tails])
+    shift_ref[...] = jnp.concatenate([sums[2 * t : 2 * t + 1] for t in range(3)], axis=0)
+    scale_ref[...] = jnp.concatenate([sums[2 * t + 1 : 2 * t + 2] for t in range(3)], axis=0)
+
+
+def final_kernel(parts, blocks, where_ref, own_ref, other_ref, *outs):
     first_core = where_ref[1] == 0
     total = sum(parts)
-    half = own_ref.shape[0]
-    blocks = half // total
+    small = own_ref.shape[0] - blocks * total
     for core in range(2):
+        pick = first_core if core == 0 else jnp.logical_not(first_core)
+
+        def put(out, start, at, size):
+            count = min(size, out.shape[0] - start)
+            if count > 0:
+                rows = slice(at, at + count)
+                out[start : start + count] = jnp.where(pick, own_ref[rows], other_ref[rows]).astype(F32)
+
         base = 0
         for size, out in zip(parts, outs):
             for t in range(blocks):
-                start = (core * blocks + t) * size
-                count = min(size, out.shape[0] - start)
-                if count > 0:
-                    rows = slice(t * total + base, t * total + base + count)
-                    mine, theirs = own_ref[rows], other_ref[rows]
-                    pick = first_core if core == 0 else jnp.logical_not(first_core)
-                    out[start : start + count] = jnp.where(pick, mine, theirs).astype(F32)
+                put(out, (core * blocks + t) * size, t * total + base, size)
             base += size
+        put(outs[-1], core * small, blocks * total, small)
 
 
 def whole(array):
@@ -344,6 +414,8 @@
 
 def call(kernel, steps, where, operands, kinds, outs, out_kinds, scratch=()):
     def spec(array, kind):
+        if kind == "hbm":
+            return pl.BlockSpec(memory_space=pltpu.HBM)
         if kind == "all":
             return whole(array)
         return per_micro(array, kind == "pick")
@@ -411,11 +483,17 @@
 
     hidden_zero, part_zero, kids, which = call(
         down_kernel, mine, where,
-        [voxel_feats, down_map, neighbours, flat_down],
-        ["pick", "pick", "all", "all"],
+        [voxel_feats, down_map, flat_down],
+        ["hbm", "hbm", "all"],
         [rows_f32, sums, shape((mine, wide, coarse_rows), BF16), shape((mine, 8, fine_rows), F32)],
         ["own"] * 4,
-        [pltpu.VMEM((wide, fine_rows), BF16), pltpu.VMEM((fine_rows, coarse_rows), BF16)],
+        [
+            pltpu.VMEM((wide, fine_rows), BF16),
+            pltpu.VMEM((fine_rows, coarse_rows), BF16),
+            pltpu.VMEM((mine, in_channels, fine_rows), BF16),
+            pltpu.VMEM((mine, offsets, coarse_rows), jnp.int32),
+            pltpu.SemaphoreType.DMA((mine, 2)),
+        ],
     )
     stats_zero = bucket_sums(part_zero, "dp")
     ways = len(stats_zero)
@@ -441,25 +519,28 @@
     )
     back_two = bucket_sums(back_part, "dp")
 
-    def part_rows(rows):
-        return -(-rows // (2 * sections * depths * 16)) * 16
-
+    def part_rows(rows, pieces):
+        return -(-rows // (pieces * 16)) * 16
+
+    blocks = sections * depths
     conv_rows = w_first.shape[0] * channels
-    parts = [part_rows(conv_rows), part_rows(conv_rows), part_rows(wide)]
-
-    def halves(size):
-        return shape((sections * depths * size, channels), BF16)
-
-    def accumulator(size):
-        return [pltpu.VMEM((2 * sections * depths * size, channels), F32)]
-
+    parts = [part_rows(conv_rows, 2 * blocks)] * 2
+    small = part_rows(wide, 2 * depths)
+
+    def half_shape(rows):
+        return shape((rows, channels), BF16)
+
+    def accumulator(rows):
+        return [pltpu.VMEM((2 * rows, channels), F32)]
+
+    half = half_shape(blocks * parts[0])
     up_one, back_part, keep_second, send_second = call(
         functools.partial(backward_kernel, 2, False, ways), mine, where,
         [up_two, hidden_two, hidden_one, act_one, neighbours, w_second, bn_scale, bn_shift]
         + stats_two + back_two + stats_one,
         ["own"] * 4 + ["all"] * 4 + ["own"] * (3 * ways),
-        [rows_f32, sums, halves(parts[0]), halves(parts[0])], ["own", "own", "all", "all"],
-        accumulator(parts[0]),
+        [rows_f32, sums, half, half], ["own", "own", "all", "all"],
+        accumulator(half.shape[0]),
     )
     back_one = bucket_sums(back_part, "dp")
     got_second = swapped(send_second, "dp", 1)
@@ -468,26 +549,27 @@
         [up_one, hidden_one, hidden_zero, act_zero, neighbours, w_first, bn_scale, bn_shift]
         + stats_one + back_one + stats_zero + [up_two],
         ["own"] * 4 + ["all"] * 4 + ["own"] * (3 * ways + 1),
-        [rows_f32, sums, halves(parts[1]), halves(parts[1])], ["own", "own", "all", "all"],
-        accumulator(parts[1]),
-    )
+        [rows_f32, sums, half, half], ["own", "own", "all", "all"],
+        accumulator(half.shape[0]),
+    )
+    got_first = swapped(send_first, "dp", 1)
+    total = sum(parts)
+    section_out = simple(
+        functools.partial(split_kernel, sections, depths, parts), where,
+        [keep_second, got_second, keep_first, got_first],
+        [half_shape(depths * total)] * sections,
+    )
+    arrived = [section_out[0]] + [swapped(section_out[j], "section", j) for j in range(1, sections)]
     back_zero = bucket_sums(back_part, "dp")
-    got_first = swapped(send_first, "dp", 1)
+    small_half = half_shape(depths * small)
     rows_zero, keep_down, send_down = call(
         functools.partial(last_kernel, ways), mine, where,
         [up_zero, hidden_zero, kids, neighbours, bn_scale] + stats_zero + back_zero,
         ["own"] * 3 + ["all"] * 2 + ["own"] * (2 * ways),
-        [rows_bf16, halves(parts[2]), halves(parts[2])], ["own", "all", "all"],
-        accumulator(parts[2]),
+        [rows_bf16, small_half, small_half], ["own", "all", "all"],
+        accumulator(small_half.shape[0]),
     )
     got_down = swapped(send_down, "dp", 1)
-    total = sum(parts)
-    sections_out = simple(
-        functools.partial(split_kernel, sections, depths, parts), where,
-        [keep_second, got_second, keep_first, got_first, keep_down, got_down],
-        [shape((depths * total, channels), BF16)] * sections,
-    )
-    arrived = [sections_out[0]] + [swapped(sections_out[j], "section", j) for j in range(1, sections)]
     (input_grad,) = call(
         input_kernel, mine, where,
         [rows_zero, which, down_map, flat_down],
@@ -495,24 +577,25 @@
         [shape((mine, in_channels, fine_rows), BF16)], ["own"],
     )
     depth_out = simple(
-        functools.partial(spread_kernel, depths, 3), where, arrived,
-        [shape((total, channels), BF16)] * depths,
+        functools.partial(spread_kernel, depths, sections), where, arrived + [keep_down, got_down],
+        [half_shape(total + small)] * depths,
     )
     arrived = [depth_out[0]] + [swapped(depth_out[j], "dp", 2 * j) for j in range(1, depths)]
-    (summed,) = simple(add_kernel, where, arrived, [shape((total, channels), BF16)])
+    (summed,) = simple(add_kernel, where, arrived, [half_shape(total + small)])
     arrived = [summed] + [swapped(summed, "dp", 2 * j) for j in range(1, depths)]
     (joined,) = simple(
-        functools.partial(join_kernel, ways), where, arrived + back_zero + back_one + back_two,
-        [shape((depths * total + 16, channels), BF16)],
+        functools.partial(join_kernel, ways, small), where, arrived + back_zero + back_one + back_two,
+        [half_shape(depths * (total + small) + 16)],
     )
     arrived = [joined] + [swapped(joined, "section", j) for j in range(1, sections)]
-    half, norm_sums = simple(
-        gather_kernel, where, arrived,
-        [shape((sections * depths * total, channels), BF16), shape((8, channels), F32)],
-    )
-    other = swapped(half, "dp", 1)
+    norms = shape(bn_scale.shape, F32)
+    gathered, grad_scale, grad_shift = simple(
+        functools.partial(gather_kernel, depths * total), where, arrived,
+        [half_shape(blocks * total + depths * small), norms, norms],
+    )
+    other = swapped(gathered, "dp", 1)
     grad_second, grad_first, grad_down = simple(
-        functools.partial(final_kernel, parts), where, [half, other],
+        functools.partial(final_kernel, parts, blocks), where, [gathered, other],
         [shape((conv_rows, channels), F32), shape((conv_rows, channels), F32), shape((wide, channels), F32)],
     )
     return (
@@ -521,8 +604,8 @@
         grad_down.reshape(w_down.shape),
         grad_first.reshape(w_first.shape),
         grad_second.reshape(w_second.shape),
-        norm_sums[1:6:2],
-        norm_sums[0:6:2],
+        grad_scale,
+        grad_shift,
     )
 
 

time: 174 us -> 152 us (0.87)
  Pallas kernels: 67.2 us -> 50.8 us
  waiting for transfers between devices: 45.5 us -> 41 us
  local copies, waits for them, and re-layouts: 5.63 us -> 3.52 us
    pallas_call x8, Pallas kernels: 61.1 us -> 44.1 us  [call(): pl.pallas_call(kernel, grid_spec=pltpu.PrefetchScalarGridSpec(num_scalar_...]
    ppermute x16, waiting for transfers between devices: 25.4 us -> 20.2 us  [swapped(): return lax.ppermute(value, axis, [(i, i ^ step) for i in range(count)])]
    unnamed x24 -> x22, local copies, waits for them, and re-layouts: 4.45 us -> 3.52 us
  transfers between devices with their start and end apart: 40 -> 40, of which waited for: 26 -> 25; matrix products, arithmetic and copies ran while one was open for 1% -> 0% of each run, Pallas kernels for 11% -> 9%
where the time goes in v3:
time: 152 us; the launch traced here: 151 us
  starting transfers between devices  55.2 us (36%)
  Pallas kernels  50.8 us (33%)
  waiting for transfers between devices  41 us (27%)
  local copies, waits for them, and re-layouts  3.52 us (2%)
    pallas_call x8, Pallas kernels, call(): pl.pallas_call(kernel, grid_spec=pltpu.PrefetchScalarGridSpec(num_scalar_...  44.1 us
    ppermute x16, starting transfers between devices, swapped(): return lax.ppermute(value, axis, [(i, i ^ step) for i in range(count)])  23.6 us
    ppermute x18, starting transfers between devices, bucket_sums(): lax.ppermute(value, axis, [(i, i ^ step) for i in range(count)])  22.5 us
    ppermute x16, waiting for transfers between devices, swapped(): return lax.ppermute(value, axis, [(i, i ^ step) for i in range(count)])  20.2 us
    ppermute x18, waiting for transfers between devices, bucket_sums(): lax.ppermute(value, axis, [(i, i ^ step) for i in range(count)])  15.5 us
    ppermute x6, starting transfers between devices, bucket_sums(): lax.ppermute(value, axis, [(i, i ^ 1) for i in range(count)])  9.18 us
    pallas_call x6, Pallas kernels, simple(): pl.pallas_call(kernel, in_specs=[pl.BlockSpec(memory_space=pltpu.SMEM)] +...  6.62 us
    ppermute x6, waiting for transfers between devices, bucket_sums(): lax.ppermute(value, axis, [(i, i ^ 1) for i in range(count)])  5.26 us
  transfers between devices with their start and end apart: 40, of which 25 were waited for; matrix products, arithmetic and copies ran while one was open for 0% of the time, Pallas kernels for 9%

profile of v3, /device:TPU:1, one launch (start us, length us, event | category | flops | bytes accessed | tf_op | source)
XLA Modules:
  0.0 151.4 jit_solution(16950637543274370363)
XLA Ops:
  0.8 1.7 %copy-done.3 = bf16[8,2048,64]{1,2,0:T(8,128)(2,1)S(1)} copy-done((bf16[8,2048,64]{1,2,0:T(8,128)(2,1)S(1)}, bf16[8,2048,64]{1,2,0:T(8,128)(2,1)}, u32[]{:S(2)}) %copy-start.3) | copy-done | bytes 2097176
  4.2 4.9 %shard_map.144 = (f32[2,512,128]{2,1,0:T(8,128)S(1)}, f32[2,8,128]{2,1,0:T(8,128)S(1)}, bf16[2,512,512]{2,1,0:T(8,128)(2,1)S(1)}, f32[2,8,2048]{2,1,0:T(8,128)S(1)}) custom-call(s32[4]{0:T(128)S(1)} %pad_add_fusion.where_ref, bf16[8,64,2048]{2,1,0:T(8,128)(2,1)S(1)} %bitcast.17, s32[8,8,512]{2,1,0:T(8,128)S(1)} %copy-done.5, bf16[512,128]{1,0:T(8,128)(2,1)S(1)} %bitcast.18), custom_call_target="tpu_custom_call" | custom-call | tf_op jit(solution)/shard_map/pallas_call | solution.py:423
  10.4 2.5 %collective-permute-start.1 = (f32[2,8,128]{2,1,0:T(8,128)S(1)}, f32[2,8,128]{2,1,0:T(8,128)S(1)}, u32[]{:S(2)}, u32[]{:S(2)}) collective-permute-start(f32[2,8,128]{2,1,0:T(8,128)S(1)} %add.24.refs_0_.refs_16_), channel_id=1, source_target_pairs={{0,2},{1,3},{2,0},{3,1},{4,6},{5,7},{6,4},{7,5},{8,10},{9,11},{10,... | collective-permute-start | bytes 24584 | tf_op jit(solution)/shard_map/ppermute | solution.py:458
  12.9 2.3 %collective-permute-start.2 = (f32[2,8,128]{2,1,0:T(8,128)S(1)}, f32[2,8,128]{2,1,0:T(8,128)S(1)}, u32[]{:S(2)}, u32[]{:S(2)}) collective-permute-start(f32[2,8,128]{2,1,0:T(8,128)S(1)} %add.24.refs_0_.refs_16_), channel_id=1, source_target_pairs={{0,4},{1,5},{2,6},{3,7},{4,0},{5,1},{6,2},{7,3},{8,12},{9,13},{10,... | collective-permute-start | bytes 24584 | tf_op jit(solution)/shard_map/ppermute | solution.py:458
  16.3 3.2 %collective-permute-done.3.refs_3_.refs_19_ = f32[2,8,128]{2,1,0:T(8,128)S(1)} collective-permute-done((f32[2,8,128]{2,1,0:T(8,128)S(1)}, f32[2,8,128]{2,1,0:T(8,128)S(1)}, u32[]{:S(2)}, u32[]{:S(2)}) %collective-permute-start.3) | collective-permute-done | bytes 8224 | tf_op jit(solution)/shard_map/ppermute | solution.py:458
  19.5 7.1 %shard_map.145 = (bf16[2,512,128]{2,1,0:T(8,128)(2,1)S(1)}, f32[2,512,128]{2,1,0:T(8,128)S(1)}, f32[2,8,128]{2,1,0:T(8,128)S(1)}) custom-call(s32[4]{0:T(128)S(1)} %pad_add_fusion.where_ref, f32[2,512,128]{2,1,0:T(8,128)S(1)} %get-tuple-element.45.hidden_ref.refs_2_, s32[27,8,512]{2,1,0:T(8,128)S(1)} %bitcast.11, bf16[27,128,128]{2,1,0:T(8,128)(2,1)S(1)} %copy-done.2, ...), custom_call_target="tpu_custom_call" | custom-call | tf_op jit(solution)/shard_map/pallas_call | solution.py:423
  26.7 2.1 %collective-permute-start.4 = (f32[2,8,128]{2,1,0:T(8,128)S(1)}, f32[2,8,128]{2,1,0:T(8,128)S(1)}, u32[]{:S(2)}, u32[]{:S(2)}) collective-permute-start(f32[2,8,128]{2,1,0:T(8,128)S(1)} %get-tuple-element.48), channel_id=1, source_target_pairs={{0,1},{1,0},{2,3},{3,2},{4,5},{5,4},{6,7},{7,6},{8,9},{9,8},{10,11... | collective-permute-start | bytes 24584 | tf_op jit(solution)/shard_map/ppermute | solution.py:456
  29.7 3.5 %collective-permute-start.7 = (f32[2,8,128]{2,1,0:T(8,128)S(1)}, f32[2,8,128]{2,1,0:T(8,128)S(1)}, u32[]{:S(2)}, u32[]{:S(2)}) collective-permute-start(f32[2,8,128]{2,1,0:T(8,128)S(1)} %add.25.refs_0_.refs_16_.refs_8_), channel_id=1, source_target_pairs={{0,6},{1,7},{2,4},{3,5},{4,2},{5,3},{6,0},{7,1},{8,14},{9,15},{10,... | collective-permute-start | bytes 24584 | tf_op jit(solution)/shard_map/ppermute | solution.py:458
  34.3 7.2 %shard_map.146 = (bf16[2,512,128]{2,1,0:T(8,128)(2,1)S(1)}, bf16[2,512,128]{2,1,0:T(8,128)(2,1)S(1)}, f32[2,8,128]{2,1,0:T(8,128)S(1)}) custom-call(s32[4]{0:T(128)S(1)} %pad_add_fusion.where_ref, f32[2,512,128]{2,1,0:T(8,128)S(1)} %get-tuple-element.47.hidden_ref.refs_2_.refs_1_, s32[27,8,512]{2,1,0:T(8,128)S(1)} %bitcast.12, ...), custom_call_target="tpu_custom_call" | custom-call | tf_op jit(solution)/shard_map/pallas_call | solution.py:423
  41.5 1.8 %collective-permute-start.8 = (f32[2,8,128]{2,1,0:T(8,128)S(1)}, f32[2,8,128]{2,1,0:T(8,128)S(1)}, u32[]{:S(2)}, u32[]{:S(2)}) collective-permute-start(f32[2,8,128]{2,1,0:T(8,128)S(1)} %get-tuple-element.51), channel_id=1, source_target_pairs={{0,1},{1,0},{2,3},{3,2},{4,5},{5,4},{6,7},{7,6},{8,9},{9,8},{10,11... | collective-permute-start | bytes 24584 | tf_op jit(solution)/shard_map/ppermute | solution.py:456
  44.3 3.3 %collective-permute-start.11 = (f32[2,8,128]{2,1,0:T(8,128)S(1)}, f32[2,8,128]{2,1,0:T(8,128)S(1)}, u32[]{:S(2)}, u32[]{:S(2)}) collective-permute-start(f32[2,8,128]{2,1,0:T(8,128)S(1)} %add.26.refs_0_.refs_8_), channel_id=1, source_target_pairs={{0,6},{1,7},{2,4},{3,5},{4,2},{5,3},{6,0},{7,1},{8,14},{9,15},{10,... | collective-permute-start | bytes 24584 | tf_op jit(solution)/shard_map/ppermute | solution.py:458
  48.7 1.4 collective-permute-done.9.refs_1_.refs_9_
  50.1 1.8 %shard_map.147 = (bf16[2,512,128]{2,1,0:T(8,128)(2,1)}, f32[2,512,128]{2,1,0:T(8,128)S(1)}, f32[2,8,128]{2,1,0:T(8,128)S(1)}) custom-call(s32[4]{0:T(128)S(1)} %pad_add_fusion.where_ref, bf16[2,512,128]{2,1,0:T(8,128)(2,1)S(1)} %get-tuple-element.49.hidden_ref.refs_1_, bf16[2,512,128]{2,1,0:T(8,128)(2,1)S(1)} %get-tuple-element.50.act_ref.refs_3_, ...), custom_call_target="tpu_custom_call" | custom-call | tf_op jit(solution)/shard_map/pallas_call | solution.py:423
  51.9 1.8 %collective-permute-start.12 = (f32[2,8,128]{2,1,0:T(8,128)S(1)}, f32[2,8,128]{2,1,0:T(8,128)S(1)}, u32[]{:S(2)}, u32[]{:S(2)}) collective-permute-start(f32[2,8,128]{2,1,0:T(8,128)S(1)} %get-tuple-element.55), channel_id=1, source_target_pairs={{0,1},{1,0},{2,3},{3,2},{4,5},{5,4},{6,7},{7,6},{8,9},{9,8},{10,11... | collective-permute-start | bytes 24584 | tf_op jit(solution)/shard_map/ppermute | solution.py:456
  54.8 1.5 %collective-permute-start.14 = (f32[2,8,128]{2,1,0:T(8,128)S(1)}, f32[2,8,128]{2,1,0:T(8,128)S(1)}, u32[]{:S(2)}, u32[]{:S(2)}) collective-permute-start(f32[2,8,128]{2,1,0:T(8,128)S(1)} %add.27.refs_12_), channel_id=1, source_target_pairs={{0,4},{1,5},{2,6},{3,7},{4,0},{5,1},{6,2},{7,3},{8,12},{9,13},{10,... | collective-permute-start | bytes 24584 | tf_op jit(solution)/shard_map/ppermute | solution.py:458
  56.4 1.7 %collective-permute-start.15 = (f32[2,8,128]{2,1,0:T(8,128)S(1)}, f32[2,8,128]{2,1,0:T(8,128)S(1)}, u32[]{:S(2)}, u32[]{:S(2)}) collective-permute-start(f32[2,8,128]{2,1,0:T(8,128)S(1)} %add.27.refs_12_), channel_id=1, source_target_pairs={{0,6},{1,7},{2,4},{3,5},{4,2},{5,3},{6,0},{7,1},{8,14},{9,15},{10,... | collective-permute-start | bytes 24584 | tf_op jit(solution)/shard_map/ppermute | solution.py:458
  58.2 2.4 %collective-permute-done.15.refs_15_ = f32[2,8,128]{2,1,0:T(8,128)S(1)} collective-permute-done((f32[2,8,128]{2,1,0:T(8,128)S(1)}, f32[2,8,128]{2,1,0:T(8,128)S(1)}, u32[]{:S(2)}, u32[]{:S(2)}) %collective-permute-start.15) | collective-permute-done | bytes 8224 | tf_op jit(solution)/shard_map/ppermute | solution.py:458
  60.7 8.9 %shard_map.148 = (f32[2,512,128]{2,1,0:T(8,128)S(1)}, f32[2,8,128]{2,1,0:T(8,128)S(1)}, bf16[1792,128]{1,0:T(8,128)(2,1)S(1)}, bf16[1792,128]{1,0:T(8,128)(2,1)S(1)}) custom-call(s32[4]{0:T(128)S(1)} %pad_add_fusion.where_ref, f32[2,512,128]{2,1,0:T(8,128)S(1)} %get-tuple-element.53.refs_0_.refs_20_, ...), custom_call_target="tpu_custom_call" | custom-call | tf_op jit(solution)/shard_map/pallas_call | solution.py:423
  69.5 2.1 %collective-permute-start.16 = (f32[2,8,128]{2,1,0:T(8,128)S(1)}, f32[2,8,128]{2,1,0:T(8,128)S(1)}, u32[]{:S(2)}, u32[]{:S(2)}) collective-permute-start(f32[2,8,128]{2,1,0:T(8,128)S(1)} %get-tuple-element.57), channel_id=1, source_target_pairs={{0,1},{1,0},{2,3},{3,2},{4,5},{5,4},{6,7},{7,6},{8,9},{9,8},{10,11... | collective-permute-start | bytes 24584 | tf_op jit(solution)/shard_map/ppermute | solution.py:456
  72.5 2.0 %collective-permute-start.18 = (f32[2,8,128]{2,1,0:T(8,128)S(1)}, f32[2,8,128]{2,1,0:T(8,128)S(1)}, u32[]{:S(2)}, u32[]{:S(2)}) collective-permute-start(f32[2,8,128]{2,1,0:T(8,128)S(1)} %add.28.refs_12_.refs_8_), channel_id=1, source_target_pairs={{0,4},{1,5},{2,6},{3,7},{4,0},{5,1},{6,2},{7,3},{8,12},{9,13},{10,... | collective-permute-start | bytes 24584 | tf_op jit(solution)/shard_map/ppermute | solution.py:458
  74.5 1.5 %collective-permute-start.19 = (f32[2,8,128]{2,1,0:T(8,128)S(1)}, f32[2,8,128]{2,1,0:T(8,128)S(1)}, u32[]{:S(2)}, u32[]{:S(2)}) collective-permute-start(f32[2,8,128]{2,1,0:T(8,128)S(1)} %add.28.refs_12_.refs_8_), channel_id=1, source_target_pairs={{0,6},{1,7},{2,4},{3,5},{4,2},{5,3},{6,0},{7,1},{8,14},{9,15},{10,... | collective-permute-start | bytes 24584 | tf_op jit(solution)/shard_map/ppermute | solution.py:458
  77.2 1.6 %collective-permute-done.19.refs_15_.refs_11_ = f32[2,8,128]{2,1,0:T(8,128)S(1)} collective-permute-done((f32[2,8,128]{2,1,0:T(8,128)S(1)}, f32[2,8,128]{2,1,0:T(8,128)S(1)}, u32[]{:S(2)}, u32[]{:S(2)}) %collective-permute-start.19) | collective-permute-done | bytes 8224 | tf_op jit(solution)/shard_map/ppermute | solution.py:458
  78.8 8.6 %shard_map.149 = (f32[2,512,128]{2,1,0:T(8,128)S(1)}, f32[2,8,128]{2,1,0:T(8,128)S(1)}, bf16[1792,128]{1,0:T(8,128)(2,1)S(1)}, bf16[1792,128]{1,0:T(8,128)(2,1)S(1)}) custom-call(s32[4]{0:T(128)S(1)} %pad_add_fusion.where_ref, f32[2,512,128]{2,1,0:T(8,128)S(1)} %get-tuple-element.56.refs_0_, f32[2,512,128]{2,1,0:T(8,128)S(1)} %get-tuple-element.47.hidden_ref.refs_2_.refs_1_, ...), custom_call_target="tpu_custom_call" | custom-call | tf_op jit(solution)/shard_map/pallas_call | solution.py:423
  87.4 2.1 %collective-permute-start.25 = (bf16[1792,128]{1,0:T(8,128)(2,1)S(1)}, bf16[1792,128]{1,0:T(8,128)(2,1)S(1)}, u32[]{:S(2)}, u32[]{:S(2)}) collective-permute-start(bf16[1792,128]{1,0:T(8,128)(2,1)S(1)} %get-tuple-element.66), channel_id=1, source_target_pairs={{0,1},{1,0},{2,3},{3,2},{4,5},{5,4},{6,7},{7,6},{8,9},{9,8},{10,11... | collective-permute-start | bytes 1376264 | tf_op jit(solution)/shard_map/ppermute | solution.py:451
  89.6 1.4 collective-permute-done.25.refs_3_
  91.8 1.3 collective-permute-start.26
  93.1 1.2 collective-permute-start.27
  94.5 1.2 collective-permute-start.20
  96.5 1.8 %collective-permute-start.22 = (f32[2,8,128]{2,1,0:T(8,128)S(1)}, f32[2,8,128]{2,1,0:T(8,128)S(1)}, u32[]{:S(2)}, u32[]{:S(2)}) collective-permute-start(f32[2,8,128]{2,1,0:T(8,128)S(1)} %add.29.refs_4_), channel_id=1, source_target_pairs={{0,4},{1,5},{2,6},{3,7},{4,0},{5,1},{6,2},{7,3},{8,12},{9,13},{10,... | collective-permute-start | bytes 24584 | tf_op jit(solution)/shard_map/ppermute | solution.py:458
  99.3 1.5 %collective-permute-start.23 = (f32[2,8,128]{2,1,0:T(8,128)S(1)}, f32[2,8,128]{2,1,0:T(8,128)S(1)}, u32[]{:S(2)}, u32[]{:S(2)}) collective-permute-start(f32[2,8,128]{2,1,0:T(8,128)S(1)} %add.29.refs_4_), channel_id=1, source_target_pairs={{0,6},{1,7},{2,4},{3,5},{4,2},{5,3},{6,0},{7,1},{8,14},{9,15},{10,... | collective-permute-start | bytes 24584 | tf_op jit(solution)/shard_map/ppermute | solution.py:458
  100.9 2.8 %collective-permute-done.23.refs_7_ = f32[2,8,128]{2,1,0:T(8,128)S(1)} collective-permute-done((f32[2,8,128]{2,1,0:T(8,128)S(1)}, f32[2,8,128]{2,1,0:T(8,128)S(1)}, u32[]{:S(2)}, u32[]{:S(2)}) %collective-permute-start.23) | collective-permute-done | bytes 8224 | tf_op jit(solution)/shard_map/ppermute | solution.py:458
  103.6 1.5 shard_map.150
  105.2 2.4 %collective-permute-start.29 = (bf16[256,128]{1,0:T(8,128)(2,1)S(1)}, bf16[256,128]{1,0:T(8,128)(2,1)S(1)}, u32[]{:S(2)}, u32[]{:S(2)}) collective-permute-start(bf16[256,128]{1,0:T(8,128)(2,1)S(1)} %get-tuple-element.72), channel_id=1, source_target_pairs={{0,1},{1,0},{2,3},{3,2},{4,5},{5,4},{6,7},{7,6},{8,9},{9,8},{10,11... | collective-permute-start | bytes 196616 | tf_op jit(solution)/shard_map/ppermute | solution.py:451
  109.2 1.8 %collective-permute-start.31 = (bf16[288,128]{1,0:T(8,128)(2,1)S(1)}, bf16[288,128]{1,0:T(8,128)(2,1)S(1)}, u32[]{:S(2)}, u32[]{:S(2)}) collective-permute-start(bf16[288,128]{1,0:T(8,128)(2,1)S(1)} %get-tuple-element.75), channel_id=1, source_target_pairs={{0,4},{1,5},{2,6},{3,7},{4,0},{5,1},{6,2},{7,3},{8,12},{9,13},{10,... | collective-permute-start | bytes 221192 | tf_op jit(solution)/shard_map/ppermute | solution.py:451
  111.0 1.7 %collective-permute-start.32 = (bf16[288,128]{1,0:T(8,128)(2,1)S(1)}, bf16[288,128]{1,0:T(8,128)(2,1)S(1)}, u32[]{:S(2)}, u32[]{:S(2)}) collective-permute-start(bf16[288,128]{1,0:T(8,128)(2,1)S(1)} %get-tuple-element.76), channel_id=1, source_target_pairs={{0,6},{1,7},{2,4},{3,5},{4,2},{5,3},{6,0},{7,1},{8,14},{9,15},{10,... | collective-permute-start | bytes 221192 | tf_op jit(solution)/shard_map/ppermute | solution.py:451
  113.5 2.9 %collective-permute-done.32.refs_3_ = bf16[288,128]{1,0:T(8,128)(2,1)S(1)} collective-permute-done((bf16[288,128]{1,0:T(8,128)(2,1)S(1)}, bf16[288,128]{1,0:T(8,128)(2,1)S(1)}, u32[]{:S(2)}, u32[]{:S(2)}) %collective-permute-start.32) | collective-permute-done | bytes 73760 | tf_op jit(solution)/shard_map/ppermute | solution.py:451
  117.0 2.1 %collective-permute-start.33 = (bf16[288,128]{1,0:T(8,128)(2,1)S(1)}, bf16[288,128]{1,0:T(8,128)(2,1)S(1)}, u32[]{:S(2)}, u32[]{:S(2)}) collective-permute-start(bf16[288,128]{1,0:T(8,128)(2,1)S(1)} %shard_map.154.refs_0_), channel_id=1, source_target_pairs={{0,2},{1,3},{2,0},{3,1},{4,6},{5,7},{6,4},{7,5},{8,10},{9,11},{10,... | collective-permute-start | bytes 221192 | tf_op jit(solution)/shard_map/ppermute | solution.py:451
  119.8 1.4 collective-permute-start.35
  121.2 2.7 %collective-permute-done.34.refs_2_ = bf16[288,128]{1,0:T(8,128)(2,1)S(1)} collective-permute-done((bf16[288,128]{1,0:T(8,128)(2,1)S(1)}, bf16[288,128]{1,0:T(8,128)(2,1)S(1)}, u32[]{:S(2)}, u32[]{:S(2)}) %collective-permute-start.34) | collective-permute-done | bytes 73760 | tf_op jit(solution)/shard_map/ppermute | solution.py:451
  124.0 1.5 %collective-permute-done.35.refs_3_ = bf16[288,128]{1,0:T(8,128)(2,1)S(1)} collective-permute-done((bf16[288,128]{1,0:T(8,128)(2,1)S(1)}, bf16[288,128]{1,0:T(8,128)(2,1)S(1)}, u32[]{:S(2)}, u32[]{:S(2)}) %collective-permute-start.35) | collective-permute-done | bytes 73760 | tf_op jit(solution)/shard_map/ppermute | solution.py:451
  126.1 1.3 collective-permute-start.36
  127.4 1.2 collective-permute-start.37
  128.8 3.0 %collective-permute-done.36.refs_1_ = bf16[1168,128]{1,0:T(8,128)(2,1)S(1)} collective-permute-done((bf16[1168,128]{1,0:T(8,128)(2,1)S(1)}, bf16[1168,128]{1,0:T(8,128)(2,1)S(1)}, u32[]{:S(2)}, u32[]{:S(2)}) %collective-permute-start.36) | collective-permute-done | bytes 299040 | tf_op jit(solution)/shard_map/ppermute | solution.py:451
  131.8 2.7 %collective-permute-done.37.refs_2_ = bf16[1168,128]{1,0:T(8,128)(2,1)S(1)} collective-permute-done((bf16[1168,128]{1,0:T(8,128)(2,1)S(1)}, bf16[1168,128]{1,0:T(8,128)(2,1)S(1)}, u32[]{:S(2)}, u32[]{:S(2)}) %collective-permute-start.37) | collective-permute-done | bytes 299040 | tf_op jit(solution)/shard_map/ppermute | solution.py:451
  134.5 4.3 %collective-permute-done.38.refs_3_ = bf16[1168,128]{1,0:T(8,128)(2,1)S(1)} collective-permute-done((bf16[1168,128]{1,0:T(8,128)(2,1)S(1)}, bf16[1168,128]{1,0:T(8,128)(2,1)S(1)}, u32[]{:S(2)}, u32[]{:S(2)}) %collective-permute-start.38) | collective-permute-done | bytes 299040 | tf_op jit(solution)/shard_map/ppermute | solution.py:451
  139.9 4.6 %collective-permute-start.39 = (bf16[3840,128]{1,0:T(8,128)(2,1)S(1)}, bf16[3840,128]{1,0:T(8,128)(2,1)S(1)}, u32[]{:S(2)}, u32[]{:S(2)}) collective-permute-start(bf16[3840,128]{1,0:T(8,128)(2,1)S(1)} %get-tuple-element.77.own_ref), channel_id=1, source_target_pairs={{0,1},{1,0},{2,3},{3,2},{4,5},{5,4},{6,7},{7,6},{8,9},{9,8},{10,11... | collective-permute-start | bytes 2949128 | tf_op jit(solution)/shard_map/ppermute | solution.py:451
  144.5 4.1 %shard_map.151 = bf16[2,64,2048]{2,1,0:T(8,128)(2,1)} custom-call(s32[4]{0:T(128)S(1)} %pad_add_fusion.where_ref, bf16[2,512,128]{2,1,0:T(8,128)(2,1)S(1)} %get-tuple-element.61.rows_ref, f32[2,8,2048]{2,1,0:T(8,128)S(1)} %get-tuple-element.62.which_ref, s32[8,8,512]{2,1,0:T(8,128)S(1)} %copy-done.6, bf16[512,128]{1,0:T(8,128)(2,1)S(1)} %bitcast.19), custom_call_target="tpu_custom_call" | custom-call | tf_op jit(solution)/shard_map/pallas_call | solution.py:423
  148.6 2.8 %shard_map.157 = (f32[3456,128]{1,0:T(8,128)}, f32[3456,128]{1,0:T(8,128)}, f32[512,128]{1,0:T(8,128)}) custom-call(s32[4]{0:T(128)S(1)} %pad_add_fusion.where_ref, bf16[3840,128]{1,0:T(8,128)(2,1)S(1)} %get-tuple-element.77.own_ref, bf16[3840,128]{1,0:T(8,128)(2,1)S(1)} %collective-permute-done.39.other_ref), custom_call_target="tpu_custom_call" | custom-call | tf_op jit(solution)/shard_map/pallas_call | solution.py:440
  (75 shorter events, 20.2 us)
Async XLA Ops:
  0.6 18.9 %copy-start = (s32[8,27,512]{2,0,1:T(8,128)S(1)}, s32[8,27,512]{2,0,1:T(8,128)}, u32[]{:S(2)}) copy-start(s32[8,27,512]{2,0,1:T(8,128)} %param.11) | copy-start | bytes 1327108
  0.6 18.9 %copy-start.2 = (bf16[27,128,128]{2,1,0:T(8,128)(2,1)S(1)}, bf16[27,128,128]{2,1,0:T(8,128)(2,1)}, u32[]{:S(2)}) copy-start(bf16[27,128,128]{2,1,0:T(8,128)(2,1)} %refs_5_.3) | copy-start | bytes 2654212
  4.2 15.3 %copy-start.9 = (f32[3,128]{1,0:T(4,128)S(1)}, f32[3,128]{1,0:T(4,128)}, u32[]{:S(2)}) copy-start(f32[3,128]{1,0:T(4,128)} %scale_ref.7) | copy-start | bytes 4612
  4.2 15.3 %copy-start.10 = (f32[3,128]{1,0:T(4,128)S(1)}, f32[3,128]{1,0:T(4,128)}, u32[]{:S(2)}) copy-start(f32[3,128]{1,0:T(4,128)} %refs_7_.3) | copy-start | bytes 4612
  4.2 30.1 %copy-start.1 = (bf16[27,128,128]{2,1,0:T(8,128)(2,1)S(1)}, bf16[27,128,128]{2,1,0:T(8,128)(2,1)}, u32[]{:S(2)}) copy-start(bf16[27,128,128]{2,1,0:T(8,128)(2,1)} %refs_5_.2) | copy-start | bytes 2654212
  9.2 1.2 collective-permute-start
  10.4 4.8 %collective-permute-start.1 = (f32[2,8,128]{2,1,0:T(8,128)S(1)}, f32[2,8,128]{2,1,0:T(8,128)S(1)}, u32[]{:S(2)}, u32[]{:S(2)}) collective-permute-start(f32[2,8,128]{2,1,0:T(8,128)S(1)} %add.24.refs_0_.refs_16_), channel_id=1, source_target_pairs={{0,2},{1,3},{2,0},{3,1},{4,6},{5,7},{6,4},{7,5},{8,10},{9,11},{10,... | collective-permute-start | bytes 24584 | tf_op jit(solution)/shard_map/ppermute | solution.py:458
  12.9 3.4 %collective-permute-start.2 = (f32[2,8,128]{2,1,0:T(8,128)S(1)}, f32[2,8,128]{2,1,0:T(8,128)S(1)}, u32[]{:S(2)}, u32[]{:S(2)}) collective-permute-start(f32[2,8,128]{2,1,0:T(8,128)S(1)} %add.24.refs_0_.refs_16_), channel_id=1, source_target_pairs={{0,4},{1,5},{2,6},{3,7},{4,0},{5,1},{6,2},{7,3},{8,12},{9,13},{10,... | collective-permute-start | bytes 24584 | tf_op jit(solution)/shard_map/ppermute | solution.py:458
  15.2 4.3 %collective-permute-start.3 = (f32[2,8,128]{2,1,0:T(8,128)S(1)}, f32[2,8,128]{2,1,0:T(8,128)S(1)}, u32[]{:S(2)}, u32[]{:S(2)}) collective-permute-start(f32[2,8,128]{2,1,0:T(8,128)S(1)} %add.24.refs_0_.refs_16_), channel_id=1, source_target_pairs={{0,6},{1,7},{2,4},{3,5},{4,2},{5,3},{6,0},{7,1},{8,14},{9,15},{10,... | collective-permute-start | bytes 24584 | tf_op jit(solution)/shard_map/ppermute | solution.py:458
  19.5 30.6 %copy-start.4 = (bf16[8,512,128]{2,1,0:T(8,128)(2,1)S(1)}, bf16[8,512,128]{2,1,0:T(8,128)(2,1)}, u32[]{:S(2)}) copy-start(bf16[8,512,128]{2,1,0:T(8,128)(2,1)} %grad_ref.1) | copy-start | bytes 3145732
  26.7 2.9 %collective-permute-start.4 = (f32[2,8,128]{2,1,0:T(8,128)S(1)}, f32[2,8,128]{2,1,0:T(8,128)S(1)}, u32[]{:S(2)}, u32[]{:S(2)}) collective-permute-start(f32[2,8,128]{2,1,0:T(8,128)S(1)} %get-tuple-element.48), channel_id=1, source_target_pairs={{0,1},{1,0},{2,3},{3,2},{4,5},{5,4},{6,7},{7,6},{8,9},{9,8},{10,11... | collective-permute-start | bytes 24584 | tf_op jit(solution)/shard_map/ppermute | solution.py:456
  29.6 3.6 %collective-permute-start.5 = (f32[2,8,128]{2,1,0:T(8,128)S(1)}, f32[2,8,128]{2,1,0:T(8,128)S(1)}, u32[]{:S(2)}, u32[]{:S(2)}) collective-permute-start(f32[2,8,128]{2,1,0:T(8,128)S(1)} %add.25.refs_0_.refs_16_.refs_8_), channel_id=1, source_target_pairs={{0,2},{1,3},{2,0},{3,1},{4,6},{5,7},{6,4},{7,5},{8,10},{9,11},{10,... | collective-permute-start | bytes 24584 | tf_op jit(solution)/shard_map/ppermute | solution.py:458
  29.6 3.6 %collective-permute-start.6 = (f32[2,8,128]{2,1,0:T(8,128)S(1)}, f32[2,8,128]{2,1,0:T(8,128)S(1)}, u32[]{:S(2)}, u32[]{:S(2)}) collective-permute-start(f32[2,8,128]{2,1,0:T(8,128)S(1)} %add.25.refs_0_.refs_16_.refs_8_), channel_id=1, source_target_pairs={{0,4},{1,5},{2,6},{3,7},{4,0},{5,1},{6,2},{7,3},{8,12},{9,13},{10,... | collective-permute-start | bytes 24584 | tf_op jit(solution)/shard_map/ppermute | solution.py:458
  29.7 4.6 %collective-permute-start.7 = (f32[2,8,128]{2,1,0:T(8,128)S(1)}, f32[2,8,128]{2,1,0:T(8,128)S(1)}, u32[]{:S(2)}, u32[]{:S(2)}) collective-permute-start(f32[2,8,128]{2,1,0:T(8,128)S(1)} %add.25.refs_0_.refs_16_.refs_8_), channel_id=1, source_target_pairs={{0,6},{1,7},{2,4},{3,5},{4,2},{5,3},{6,0},{7,1},{8,14},{9,15},{10,... | collective-permute-start | bytes 24584 | tf_op jit(solution)/shard_map/ppermute | solution.py:458
  41.5 2.7 %collective-permute-start.8 = (f32[2,8,128]{2,1,0:T(8,128)S(1)}, f32[2,8,128]{2,1,0:T(8,128)S(1)}, u32[]{:S(2)}, u32[]{:S(2)}) collective-permute-start(f32[2,8,128]{2,1,0:T(8,128)S(1)} %get-tuple-element.51), channel_id=1, source_target_pairs={{0,1},{1,0},{2,3},{3,2},{4,5},{5,4},{6,7},{7,6},{8,9},{9,8},{10,11... | collective-permute-start | bytes 24584 | tf_op jit(solution)/shard_map/ppermute | solution.py:456
  44.1 3.7 %collective-permute-start.10 = (f32[2,8,128]{2,1,0:T(8,128)S(1)}, f32[2,8,128]{2,1,0:T(8,128)S(1)}, u32[]{:S(2)}, u32[]{:S(2)}) collective-permute-start(f32[2,8,128]{2,1,0:T(8,128)S(1)} %add.26.refs_0_.refs_8_), channel_id=1, source_target_pairs={{0,4},{1,5},{2,6},{3,7},{4,0},{5,1},{6,2},{7,3},{8,12},{9,13},{10,... | collective-permute-start | bytes 24584 | tf_op jit(solution)/shard_map/ppermute | solution.py:458
  44.3 4.4 %collective-permute-start.11 = (f32[2,8,128]{2,1,0:T(8,128)S(1)}, f32[2,8,128]{2,1,0:T(8,128)S(1)}, u32[]{:S(2)}, u32[]{:S(2)}) collective-permute-start(f32[2,8,128]{2,1,0:T(8,128)S(1)} %add.26.refs_0_.refs_8_), channel_id=1, source_target_pairs={{0,6},{1,7},{2,4},{3,5},{4,2},{5,3},{6,0},{7,1},{8,14},{9,15},{10,... | collective-permute-start | bytes 24584 | tf_op jit(solution)/shard_map/ppermute | solution.py:458
  47.6 2.5 %collective-permute-start.9 = (f32[2,8,128]{2,1,0:T(8,128)S(1)}, f32[2,8,128]{2,1,0:T(8,128)S(1)}, u32[]{:S(2)}, u32[]{:S(2)}) collective-permute-start(f32[2,8,128]{2,1,0:T(8,128)S(1)} %add.26.refs_0_.refs_8_), channel_id=1, source_target_pairs={{0,2},{1,3},{2,0},{3,1},{4,6},{5,7},{6,4},{7,5},{8,10},{9,11},{10,... | collective-permute-start | bytes 24584 | tf_op jit(solution)/shard_map/ppermute | solution.py:458
  51.9 2.6 %collective-permute-start.12 = (f32[2,8,128]{2,1,0:T(8,128)S(1)}, f32[2,8,128]{2,1,0:T(8,128)S(1)}, u32[]{:S(2)}, u32[]{:S(2)}) collective-permute-start(f32[2,8,128]{2,1,0:T(8,128)S(1)} %get-tuple-element.55), channel_id=1, source_target_pairs={{0,1},{1,0},{2,3},{3,2},{4,5},{5,4},{6,7},{7,6},{8,9},{9,8},{10,11... | collective-permute-start | bytes 24584 | tf_op jit(solution)/shard_map/ppermute | solution.py:456
  54.6 3.6 %collective-permute-start.13 = (f32[2,8,128]{2,1,0:T(8,128)S(1)}, f32[2,8,128]{2,1,0:T(8,128)S(1)}, u32[]{:S(2)}, u32[]{:S(2)}) collective-permute-start(f32[2,8,128]{2,1,0:T(8,128)S(1)} %add.27.refs_12_), channel_id=1, source_target_pairs={{0,2},{1,3},{2,0},{3,1},{4,6},{5,7},{6,4},{7,5},{8,10},{9,11},{10,... | collective-permute-start | bytes 24584 | tf_op jit(solution)/shard_map/ppermute | solution.py:458
  54.8 3.4 %collective-permute-start.14 = (f32[2,8,128]{2,1,0:T(8,128)S(1)}, f32[2,8,128]{2,1,0:T(8,128)S(1)}, u32[]{:S(2)}, u32[]{:S(2)}) collective-permute-start(f32[2,8,128]{2,1,0:T(8,128)S(1)} %add.27.refs_12_), channel_id=1, source_target_pairs={{0,4},{1,5},{2,6},{3,7},{4,0},{5,1},{6,2},{7,3},{8,12},{9,13},{10,... | collective-permute-start | bytes 24584 | tf_op jit(solution)/shard_map/ppermute | solution.py:458
  56.4 4.3 %collective-permute-start.15 = (f32[2,8,128]{2,1,0:T(8,128)S(1)}, f32[2,8,128]{2,1,0:T(8,128)S(1)}, u32[]{:S(2)}, u32[]{:S(2)}) collective-permute-start(f32[2,8,128]{2,1,0:T(8,128)S(1)} %add.27.refs_12_), channel_id=1, source_target_pairs={{0,6},{1,7},{2,4},{3,5},{4,2},{5,3},{6,0},{7,1},{8,14},{9,15},{10,... | collective-permute-start | bytes 24584 | tf_op jit(solution)/shard_map/ppermute | solution.py:458
  69.5 2.9 %collective-permute-start.16 = (f32[2,8,128]{2,1,0:T(8,128)S(1)}, f32[2,8,128]{2,1,0:T(8,128)S(1)}, u32[]{:S(2)}, u32[]{:S(2)}) collective-permute-start(f32[2,8,128]{2,1,0:T(8,128)S(1)} %get-tuple-element.57), channel_id=1, source_target_pairs={{0,1},{1,0},{2,3},{3,2},{4,5},{5,4},{6,7},{7,6},{8,9},{9,8},{10,11... | collective-permute-start | bytes 24584 | tf_op jit(solution)/shard_map/ppermute | solution.py:456
  72.5 4.7 %collective-permute-start.17 = (f32[2,8,128]{2,1,0:T(8,128)S(1)}, f32[2,8,128]{2,1,0:T(8,128)S(1)}, u32[]{:S(2)}, u32[]{:S(2)}) collective-permute-start(f32[2,8,128]{2,1,0:T(8,128)S(1)} %add.28.refs_12_.refs_8_), channel_id=1, source_target_pairs={{0,2},{1,3},{2,0},{3,1},{4,6},{5,7},{6,4},{7,5},{8,10},{9,11},{10,... | collective-permute-start | bytes 24584 | tf_op jit(solution)/shard_map/ppermute | solution.py:458
  72.5 4.7 %collective-permute-start.18 = (f32[2,8,128]{2,1,0:T(8,128)S(1)}, f32[2,8,128]{2,1,0:T(8,128)S(1)}, u32[]{:S(2)}, u32[]{:S(2)}) collective-permute-start(f32[2,8,128]{2,1,0:T(8,128)S(1)} %add.28.refs_12_.refs_8_), channel_id=1, source_target_pairs={{0,4},{1,5},{2,6},{3,7},{4,0},{5,1},{6,2},{7,3},{8,12},{9,13},{10,... | collective-permute-start | bytes 24584 | tf_op jit(solution)/shard_map/ppermute | solution.py:458
  74.5 4.3 %collective-permute-start.19 = (f32[2,8,128]{2,1,0:T(8,128)S(1)}, f32[2,8,128]{2,1,0:T(8,128)S(1)}, u32[]{:S(2)}, u32[]{:S(2)}) collective-permute-start(f32[2,8,128]{2,1,0:T(8,128)S(1)} %add.28.refs_12_.refs_8_), channel_id=1, source_target_pairs={{0,6},{1,7},{2,4},{3,5},{4,2},{5,3},{6,0},{7,1},{8,14},{9,15},{10,... | collective-permute-start | bytes 24584 | tf_op jit(solution)/shard_map/ppermute | solution.py:458
  76.0 13.6 %collective-permute-start.24 = (bf16[1792,128]{1,0:T(8,128)(2,1)S(1)}, bf16[1792,128]{1,0:T(8,128)(2,1)S(1)}, u32[]{:S(2)}, u32[]{:S(2)}) collective-permute-start(bf16[1792,128]{1,0:T(8,128)(2,1)S(1)} %get-tuple-element.64), channel_id=1, source_target_pairs={{0,1},{1,0},{2,3},{3,2},{4,5},{5,4},{6,7},{7,6},{8,9},{9,8},{10,11... | collective-permute-start | bytes 1376264 | tf_op jit(solution)/shard_map/ppermute | solution.py:451
  87.4 3.6 %collective-permute-start.25 = (bf16[1792,128]{1,0:T(8,128)(2,1)S(1)}, bf16[1792,128]{1,0:T(8,128)(2,1)S(1)}, u32[]{:S(2)}, u32[]{:S(2)}) collective-permute-start(bf16[1792,128]{1,0:T(8,128)(2,1)S(1)} %get-tuple-element.66), channel_id=1, source_target_pairs={{0,1},{1,0},{2,3},{3,2},{4,5},{5,4},{6,7},{7,6},{8,9},{9,8},{10,11... | collective-permute-start | bytes 1376264 | tf_op jit(solution)/shard_map/ppermute | solution.py:451
  91.8 16.7 %collective-permute-start.26 = (bf16[896,128]{1,0:T(8,128)(2,1)S(1)}, bf16[896,128]{1,0:T(8,128)(2,1)S(1)}, u32[]{:S(2)}, u32[]{:S(2)}) collective-permute-start(bf16[896,128]{1,0:T(8,128)(2,1)S(1)} %get-tuple-element.68), channel_id=1, source_target_pairs={{0,8},{8,0},{16,24},{24,16},{1,9},{9,1},{17,25},{25,17},{2,10},{10... | collective-permute-start | bytes 688136 | tf_op jit(solution)/shard_map/ppermute | solution.py:451
  93.1 15.4 %collective-permute-start.27 = (bf16[896,128]{1,0:T(8,128)(2,1)S(1)}, bf16[896,128]{1,0:T(8,128)(2,1)S(1)}, u32[]{:S(2)}, u32[]{:S(2)}) collective-permute-start(bf16[896,128]{1,0:T(8,128)(2,1)S(1)} %get-tuple-element.69), channel_id=1, source_target_pairs={{0,16},{8,24},{16,0},{24,8},{1,17},{9,25},{17,1},{25,9},{2,18},{10... | collective-permute-start | bytes 688136 | tf_op jit(solution)/shard_map/ppermute | solution.py:451
  94.3 14.2 %collective-permute-start.28 = (bf16[896,128]{1,0:T(8,128)(2,1)S(1)}, bf16[896,128]{1,0:T(8,128)(2,1)S(1)}, u32[]{:S(2)}, u32[]{:S(2)}) collective-permute-start(bf16[896,128]{1,0:T(8,128)(2,1)S(1)} %get-tuple-element.70), channel_id=1, source_target_pairs={{0,24},{8,16},{16,8},{24,0},{1,25},{9,17},{17,9},{25,1},{2,26},{10... | collective-permute-start | bytes 688136 | tf_op jit(solution)/shard_map/ppermute | solution.py:451
  94.5 2.0 %collective-permute-start.20 = (f32[2,8,128]{2,1,0:T(8,128)S(1)}, f32[2,8,128]{2,1,0:T(8,128)S(1)}, u32[]{:S(2)}, u32[]{:S(2)}) collective-permute-start(f32[2,8,128]{2,1,0:T(8,128)S(1)} %get-tuple-element.60), channel_id=1, source_target_pairs={{0,1},{1,0},{2,3},{3,2},{4,5},{5,4},{6,7},{7,6},{8,9},{9,8},{10,11... | collective-permute-start | bytes 24584 | tf_op jit(solution)/shard_map/ppermute | solution.py:456
  96.5 2.8 %collective-permute-start.21 = (f32[2,8,128]{2,1,0:T(8,128)S(1)}, f32[2,8,128]{2,1,0:T(8,128)S(1)}, u32[]{:S(2)}, u32[]{:S(2)}) collective-permute-start(f32[2,8,128]{2,1,0:T(8,128)S(1)} %add.29.refs_4_), channel_id=1, source_target_pairs={{0,2},{1,3},{2,0},{3,1},{4,6},{5,7},{6,4},{7,5},{8,10},{9,11},{10,... | collective-permute-start | bytes 24584 | tf_op jit(solution)/shard_map/ppermute | solution.py:458
  96.5 4.3 %collective-permute-start.22 = (f32[2,8,128]{2,1,0:T(8,128)S(1)}, f32[2,8,128]{2,1,0:T(8,128)S(1)}, u32[]{:S(2)}, u32[]{:S(2)}) collective-permute-start(f32[2,8,128]{2,1,0:T(8,128)S(1)} %add.29.refs_4_), channel_id=1, source_target_pairs={{0,4},{1,5},{2,6},{3,7},{4,0},{5,1},{6,2},{7,3},{8,12},{9,13},{10,... | collective-permute-start | bytes 24584 | tf_op jit(solution)/shard_map/ppermute | solution.py:458
  99.3 4.3 %collective-permute-start.23 = (f32[2,8,128]{2,1,0:T(8,128)S(1)}, f32[2,8,128]{2,1,0:T(8,128)S(1)}, u32[]{:S(2)}, u32[]{:S(2)}) collective-permute-start(f32[2,8,128]{2,1,0:T(8,128)S(1)} %add.29.refs_4_), channel_id=1, source_target_pairs={{0,6},{1,7},{2,4},{3,5},{4,2},{5,3},{6,0},{7,1},{8,14},{9,15},{10,... | collective-permute-start | bytes 24584 | tf_op jit(solution)/shard_map/ppermute | solution.py:458
  105.1 39.4 %copy-start.6 = (s32[8,8,512]{2,1,0:T(8,128)S(1)}, s32[8,8,512]{2,1,0:T(8,128)}, u32[]{:S(2)}) copy-start(s32[8,8,512]{2,1,0:T(8,128)} %down_ref.1) | copy-start | bytes 393220
  105.1 39.4 %copy-start.8 = (bf16[8,64,128]{2,1,0:T(8,128)(2,1)S(1)}, bf16[8,64,128]{2,1,0:T(8,128)(2,1)}, u32[]{:S(2)}) copy-start(bf16[8,64,128]{2,1,0:T(8,128)(2,1)} %param.12) | copy-start | bytes 393220
  105.2 3.3 %collective-permute-start.29 = (bf16[256,128]{1,0:T(8,128)(2,1)S(1)}, bf16[256,128]{1,0:T(8,128)(2,1)S(1)}, u32[]{:S(2)}, u32[]{:S(2)}) collective-permute-start(bf16[256,128]{1,0:T(8,128)(2,1)S(1)} %get-tuple-element.72), channel_id=1, source_target_pairs={{0,1},{1,0},{2,3},{3,2},{4,5},{5,4},{6,7},{7,6},{8,9},{9,8},{10,11... | collective-permute-start | bytes 196616 | tf_op jit(solution)/shard_map/ppermute | solution.py:451
  109.2 3.6 %collective-permute-start.30 = (bf16[288,128]{1,0:T(8,128)(2,1)S(1)}, bf16[288,128]{1,0:T(8,128)(2,1)S(1)}, u32[]{:S(2)}, u32[]{:S(2)}) collective-permute-start(bf16[288,128]{1,0:T(8,128)(2,1)S(1)} %get-tuple-element.74), channel_id=1, source_target_pairs={{0,2},{1,3},{2,0},{3,1},{4,6},{5,7},{6,4},{7,5},{8,10},{9,11},{10,... | collective-permute-start | bytes 221192 | tf_op jit(solution)/shard_map/ppermute | solution.py:451
  109.2 4.3 %collective-permute-start.31 = (bf16[288,128]{1,0:T(8,128)(2,1)S(1)}, bf16[288,128]{1,0:T(8,128)(2,1)S(1)}, u32[]{:S(2)}, u32[]{:S(2)}) collective-permute-start(bf16[288,128]{1,0:T(8,128)(2,1)S(1)} %get-tuple-element.75), channel_id=1, source_target_pairs={{0,4},{1,5},{2,6},{3,7},{4,0},{5,1},{6,2},{7,3},{8,12},{9,13},{10,... | collective-permute-start | bytes 221192 | tf_op jit(solution)/shard_map/ppermute | solution.py:451
  111.0 5.4 %collective-permute-start.32 = (bf16[288,128]{1,0:T(8,128)(2,1)S(1)}, bf16[288,128]{1,0:T(8,128)(2,1)S(1)}, u32[]{:S(2)}, u32[]{:S(2)}) collective-permute-start(bf16[288,128]{1,0:T(8,128)(2,1)S(1)} %get-tuple-element.76), channel_id=1, source_target_pairs={{0,6},{1,7},{2,4},{3,5},{4,2},{5,3},{6,0},{7,1},{8,14},{9,15},{10,... | collective-permute-start | bytes 221192 | tf_op jit(solution)/shard_map/ppermute | solution.py:451
  117.0 4.3 %collective-permute-start.33 = (bf16[288,128]{1,0:T(8,128)(2,1)S(1)}, bf16[288,128]{1,0:T(8,128)(2,1)S(1)}, u32[]{:S(2)}, u32[]{:S(2)}) collective-permute-start(bf16[288,128]{1,0:T(8,128)(2,1)S(1)} %shard_map.154.refs_0_), channel_id=1, source_target_pairs={{0,2},{1,3},{2,0},{3,1},{4,6},{5,7},{6,4},{7,5},{8,10},{9,11},{10,... | collective-permute-start | bytes 221192 | tf_op jit(solution)/shard_map/ppermute | solution.py:451
  119.1 4.9 %collective-permute-start.34 = (bf16[288,128]{1,0:T(8,128)(2,1)S(1)}, bf16[288,128]{1,0:T(8,128)(2,1)S(1)}, u32[]{:S(2)}, u32[]{:S(2)}) collective-permute-start(bf16[288,128]{1,0:T(8,128)(2,1)S(1)} %shard_map.154.refs_0_), channel_id=1, source_target_pairs={{0,4},{1,5},{2,6},{3,7},{4,0},{5,1},{6,2},{7,3},{8,12},{9,13},{10,... | collective-permute-start | bytes 221192 | tf_op jit(solution)/shard_map/ppermute | solution.py:451
  119.8 5.7 %collective-permute-start.35 = (bf16[288,128]{1,0:T(8,128)(2,1)S(1)}, bf16[288,128]{1,0:T(8,128)(2,1)S(1)}, u32[]{:S(2)}, u32[]{:S(2)}) collective-permute-start(bf16[288,128]{1,0:T(8,128)(2,1)S(1)} %shard_map.154.refs_0_), channel_id=1, source_target_pairs={{0,6},{1,7},{2,4},{3,5},{4,2},{5,3},{6,0},{7,1},{8,14},{9,15},{10,... | collective-permute-start | bytes 221192 | tf_op jit(solution)/shard_map/ppermute | solution.py:451
  126.1 5.7 %collective-permute-start.36 = (bf16[1168,128]{1,0:T(8,128)(2,1)S(1)}, bf16[1168,128]{1,0:T(8,128)(2,1)S(1)}, u32[]{:S(2)}, u32[]{:S(2)}) collective-permute-start(bf16[1168,128]{1,0:T(8,128)(2,1)S(1)} %shard_map.155.refs_0_), channel_id=1, source_target_pairs={{0,8},{8,0},{16,24},{24,16},{1,9},{9,1},{17,25},{25,17},{2,10},{10... | collective-permute-start | bytes 897032 | tf_op jit(solution)/shard_map/ppermute | solution.py:451
  127.4 7.1 %collective-permute-start.37 = (bf16[1168,128]{1,0:T(8,128)(2,1)S(1)}, bf16[1168,128]{1,0:T(8,128)(2,1)S(1)}, u32[]{:S(2)}, u32[]{:S(2)}) collective-permute-start(bf16[1168,128]{1,0:T(8,128)(2,1)S(1)} %shard_map.155.refs_0_), channel_id=1, source_target_pairs={{0,16},{8,24},{16,0},{24,8},{1,17},{9,25},{17,1},{25,9},{2,18},{10... | collective-permute-start | bytes 897032 | tf_op jit(solution)/shard_map/ppermute | solution.py:451
  128.6 10.1 %collective-permute-start.38 = (bf16[1168,128]{1,0:T(8,128)(2,1)S(1)}, bf16[1168,128]{1,0:T(8,128)(2,1)S(1)}, u32[]{:S(2)}, u32[]{:S(2)}) collective-permute-start(bf16[1168,128]{1,0:T(8,128)(2,1)S(1)} %shard_map.155.refs_0_), channel_id=1, source_target_pairs={{0,24},{8,16},{16,8},{24,0},{1,25},{9,17},{17,9},{25,1},{2,26},{10... | collective-permute-start | bytes 897032 | tf_op jit(solution)/shard_map/ppermute | solution.py:451
  139.9 8.7 %collective-permute-start.39 = (bf16[3840,128]{1,0:T(8,128)(2,1)S(1)}, bf16[3840,128]{1,0:T(8,128)(2,1)S(1)}, u32[]{:S(2)}, u32[]{:S(2)}) collective-permute-start(bf16[3840,128]{1,0:T(8,128)(2,1)S(1)} %get-tuple-element.77.own_ref), channel_id=1, source_target_pairs={{0,1},{1,0},{2,3},{3,2},{4,5},{5,4},{6,7},{7,6},{8,9},{9,8},{10,11... | collective-permute-start | bytes 2949128 | tf_op jit(solution)/shard_map/ppermute | solution.py:451
  (3 other events, 3.5 us)
